TPU v7x, 32 devices: a whole 2x2x4 slice. The times are simulated.
32 devices in a mesh: ctx: 8 (over z, core), ch: 4 (over y, x).
Axes of the slice: x: 2, y: 2, z: 4, core: 2. Of those that a mesh axis runs over, the one named last changes fastest.
Arguments:
- output_gate: bfloat16 [4096, 4096], P('ctx', 'ch'), may hold values from -6 to 6
- input_gate: bfloat16 [4096, 4096], P('ctx', 'ch'), may hold values from -6 to 6
- value_input: bfloat16 [4096, 4096], P('ctx', 'ch'), may hold values from -6 to 6
- short_filter: float32 [128, 4096], P(None, 'ch'), may hold values from -0.5 to 0.5
- long_filter: float32 [4096, 256], P('ctx', 'ch'), may hold values from -0.09375 to 0.09375
- skip_gain: float32 [4096], P('ch'), may hold values from -4 to 4
Outputs:
- mixed: bfloat16 [4096, 4096], P('ctx', 'ch')
All inputs are finite; a program needn't handle non-finite values.
Results may differ from a plain program's by a relative error of at most 0.001.
Values may be sent and summed in bfloat16 or wider, within the bound.
No kernel may reach another device: no remote copies, remote signals or barrier semaphores. Data moves between devices by JAX's collectives and lax.ppermute only.
A program may use at most 64 MiB of HBM per device.

v0:
```python
import functools
import math

import jax
import jax.numpy as jnp
import numpy as np
from jax import lax
from jax.experimental import pallas as pl
from jax.experimental.pallas import tpu as pltpu
from jax.sharding import PartitionSpec as P

HIGHEST = lax.Precision.HIGHEST
LANES = 128
TILE = 16
SPAN = 250.0
BIAS = 125.0
TINY = 1e-30
MIB = 1 << 20


def passed_along(block, axis, distance):
    devices = range(lax.axis_size(axis))
    route = [(i - distance, i) for i in devices if i - distance in devices]
    return lax.ppermute(block, axis, route)


def depthwise(extended, filter_taps):
    kernel = filter_taps[::-1][:, None, :]
    result = lax.conv_general_dilated(
        extended[None],
        kernel,
        (1,),
        "VALID",
        dimension_numbers=("NWC", "WIO", "NWC"),
        feature_group_count=extended.shape[1],
        precision=HIGHEST,
    )
    return result[0]


def rotate(real_part, imag_part, cosine, sine):
    return (real_part * cosine - imag_part * sine, real_part * sine + imag_part * cosine)


def table_apply(pattern, cosine, sine, real_part, imag_part):
    out_real = jnp.einsum(pattern, cosine, real_part, precision=HIGHEST) - jnp.einsum(
        pattern, sine, imag_part, precision=HIGHEST
    )
    out_imag = jnp.einsum(pattern, cosine, imag_part, precision=HIGHEST) + jnp.einsum(
        pattern, sine, real_part, precision=HIGHEST
    )
    return (out_real, out_imag)


def dft_table(length, sign):
    index_vals = jnp.arange(length, dtype=jnp.int32)
    exponent = index_vals[:, None] * index_vals[None, :] % length
    angle = sign * 2.0 * math.pi * exponent.astype(jnp.float32) / length
    return (jnp.cos(angle), jnp.sin(angle))


def channel_local(signal, filt):
    length, cols = signal.shape
    fft_length = 2 * length
    size_a = math.gcd(length, 1 << fft_length.bit_length() // 2)
    size_b = fft_length // size_a
    half_b = size_b // 2
    pair_cols = cols // 2
    paired = signal.reshape(half_b, size_a, pair_cols, 2)
    sig_real = paired[..., 0]
    sig_imag = paired[..., 1]
    filt_real = filt.reshape(half_b, size_a, pair_cols, 2)[..., 0]
    b_cos, b_sin = dft_table(size_b, -1.0)
    in_cos = b_cos[:, :half_b]
    in_sin = b_sin[:, :half_b]
    data_real, data_imag = table_apply("kb,bap->kap", in_cos, in_sin, sig_real, sig_imag)
    spec_real = jnp.einsum("kb,bap->kap", in_cos, filt_real, precision=HIGHEST)
    spec_imag = jnp.einsum("kb,bap->kap", in_sin, filt_real, precision=HIGHEST)
    fine_index = jnp.arange(size_b, dtype=jnp.int32)
    coarse_index = jnp.arange(size_a, dtype=jnp.int32)
    exponent = fine_index[:, None] * coarse_index[None, :] % fft_length
    tw_angle = -2.0 * math.pi * exponent.astype(jnp.float32) / fft_length
    tw_cos = jnp.cos(tw_angle)[:, :, None]
    tw_sin = jnp.sin(tw_angle)[:, :, None]
    data_real, data_imag = rotate(data_real, data_imag, tw_cos, tw_sin)
    spec_real, spec_imag = rotate(spec_real, spec_imag, tw_cos, tw_sin)
    a_cos, a_sin = dft_table(size_a, -1.0)
    data_real, data_imag = table_apply("ka,bap->bkp", a_cos, a_sin, data_real, data_imag)
    spec_real, spec_imag = table_apply("ka,bap->bkp", a_cos, a_sin, spec_real, spec_imag)
    prod_real = data_real * spec_real - data_imag * spec_imag
    prod_imag = data_real * spec_imag + data_imag * spec_real
    back_real, back_imag = table_apply("ak,bkp->bap", a_cos, -a_sin, prod_real, prod_imag)
    back_real, back_imag = rotate(back_real, back_imag, tw_cos, -tw_sin)
    final_real, final_imag = table_apply(
        "bk,kap->bap", b_cos[:half_b], -b_sin[:half_b], back_real, back_imag
    )
    joined = jnp.stack([final_real, final_imag], axis=-1).reshape(length, cols)
    return joined / fft_length


def plain(output_gate, input_gate, value_input, short_filter, long_filter, skip_gain):
    row_count, chan_count = value_input.shape
    group_total = long_filter.shape[1]
    tap_count = short_filter.shape[0]
    earlier = passed_along(value_input[row_count - tap_count + 1 :], "ctx", 1)
    extended = jnp.concatenate([earlier, value_input], axis=0).astype(jnp.float32)
    gated = input_gate.astype(jnp.float32) * depthwise(extended, short_filter)
    widened = jnp.repeat(long_filter, chan_count // group_total, axis=1)
    moved = (
        lax.all_to_all(gated, "ctx", split_axis=1, concat_axis=0, tiled=True),
        lax.all_to_all(widened, "ctx", split_axis=1, concat_axis=0, tiled=True),
    )
    convolved = channel_local(moved[0], moved[1])
    long_out = lax.all_to_all(convolved, "ctx", split_axis=0, concat_axis=1, tiled=True)
    mixed = output_gate.astype(jnp.float32) * (long_out + skip_gain[None, :] * gated)
    return mixed.astype(jnp.bfloat16)


def split(values):
    high = values.astype(jnp.bfloat16)
    return high, (values - high.astype(jnp.float32)).astype(jnp.bfloat16)


def split_table(table):
    high = table.astype(np.float32).astype(jnp.bfloat16)
    low = (table - high.astype(np.float64)).astype(np.float32).astype(jnp.bfloat16)
    return np.stack([high, low])


@functools.lru_cache
def tables(half):
    bins = np.arange(half)[:, None] + 0.5
    angle = 2.0 * np.pi * bins * np.arange(2 * half)[None, :] / (2 * half)
    forward = np.concatenate([np.cos(angle), -np.sin(angle)], 0)
    return forward, forward.T / half


def widening(groups, lanes):
    one = np.kron(np.eye(groups), np.ones((1, lanes // groups)))
    return np.kron(np.eye(2), one).astype(jnp.bfloat16)


def dot(a, b):
    return jnp.dot(a, b, preferred_element_type=jnp.float32)


def dot3(table, values):
    high, low = split(values)
    cols = values.shape[1]
    both = dot(table[0], jnp.concatenate([high, low], 1))
    return both[:, :cols] + both[:, cols:] + dot(table[1], high)


def scale_of(top):
    return jnp.maximum(top * 1.01, TINY).astype(jnp.bfloat16).astype(jnp.float32)


def to_code(values, scale):
    power = jnp.exp2(jnp.abs(values) * (SPAN / scale) - BIAS)
    return jnp.where(values < 0.0, -power, power).astype(jnp.bfloat16)


def from_code(code, scale):
    power = code.astype(jnp.float32)
    size = (jnp.log(jnp.abs(power)) * (1.0 / math.log(2.0)) + BIAS) * (scale * (1.0 / SPAN))
    return jnp.where(power < 0.0, -size, size)


def short_rows(ext, taps_spec, fwd, inv):
    count = taps_spec.shape[0] // 2
    rows, cols = ext.shape
    starts = range(0, rows - count, count)
    wide = jnp.concatenate([ext[s : s + 2 * count] for s in starts], 1)
    spec = dot(fwd[0], wide) + dot(fwd[1], wide)
    t_re = jnp.concatenate([taps_spec[:count]] * len(starts), 1)
    t_im = jnp.concatenate([taps_spec[count:]] * len(starts), 1)
    s_re, s_im = spec[:count], spec[count:]
    prod = jnp.concatenate([s_re * t_re - s_im * t_im, s_re * t_im + s_im * t_re], 0)
    back = dot3(inv, prod)
    return jnp.concatenate([back[:, w * cols : (w + 1) * cols] for w in range(len(starts))], 0)


IN_VMEM = pl.BlockSpec(memory_space=pltpu.VMEM)
IN_SMEM = pl.BlockSpec(memory_space=pltpu.SMEM)
IN_ANY = pl.BlockSpec(memory_space=pl.ANY)


def kernel_params(mib):
    return pltpu.CompilerParams(vmem_limit_bytes=mib * MIB)


def cost(scale):
    return pl.CostEstimate(flops=scale * 1_000_000, bytes_accessed=scale * 1000, transcendentals=0)


def lanes_of(slab):
    return pl.ds(pl.multiple_of(slab * LANES, LANES), LANES)


def main_body(value, gate, taps, fwd, inv, gated, spec_out):
    count = taps.shape[0]
    wide = 2 * LANES
    for c in range(0, value.shape[1], wide):
        cols = slice(c, c + wide)
        taps_spec = dot3(fwd[:, :, :count], taps[:, cols])
        spec_out[:, cols] = taps_spec
        short = short_rows(value[:, cols], taps_spec, fwd, inv)
        gated[:, cols] = gate[count:, cols].astype(jnp.float32) * short


def main_call(value, gate, taps, fwd, inv):
    rows, chans = value.shape
    count = taps.shape[0]
    return pl.pallas_call(
        main_body,
        in_specs=[IN_VMEM] * 5,
        out_specs=[IN_VMEM] * 2,
        out_shape=[
            jax.ShapeDtypeStruct((rows - count, chans), jnp.float32),
            jax.ShapeDtypeStruct((2 * count, chans), jnp.float32),
        ],
        compiler_params=kernel_params(12),
        cost_estimate=cost(4),
        name="short_main",
    )(value, gate, taps, fwd, inv)


def head_body(part, count, me, halo, value, gate, gated, taps_spec, long_taps, fwd, inv, *outs):
    taps = halo.shape[0]
    rows = taps + gated.shape[0]
    groups = 8
    tops, codes = outs[: len(part)], outs[len(part) :]
    for d, top, code in zip(part, tops, codes):
        slab = lax.rem(me[0] + d, count)
        cols = lanes_of(slab)
        ext = jnp.concatenate([halo[:, cols], value[:taps, cols]], 0)
        short = short_rows(ext, taps_spec[:, cols], fwd, inv)
        first = gate[:taps, cols].astype(jnp.float32) * short
        top[...] = first
        later = gated[:, cols]
        peak = jnp.maximum(
            jnp.max(jnp.abs(first), axis=0, keepdims=True),
            jnp.max(jnp.abs(later), axis=0, keepdims=True),
        )
        scale = scale_of(peak)
        held = long_taps[slab]
        size = jnp.abs(held)
        most = size[:groups]
        for c in range(groups, held.shape[0], groups):
            most = jnp.maximum(most, size[c : c + groups])
        filter_scale = scale_of(jnp.max(most, axis=1, keepdims=True))
        filter_scale = jnp.broadcast_to(filter_scale, (groups, LANES))
        many = held.shape[0] // groups
        code[:taps] = to_code(first, scale)
        code[taps:rows] = to_code(later, scale)
        both = jnp.concatenate([jnp.broadcast_to(scale, (8, LANES)), filter_scale], 0)
        code[rows : rows + TILE] = both.astype(jnp.bfloat16)
        code[rows + TILE :] = to_code(held, jnp.concatenate([filter_scale] * many, 0))


def head_call(part, count, me, halo, value, gate, gated, taps_spec, long_taps, fwd, inv):
    taps = halo.shape[0]
    rows = taps + gated.shape[0]
    held = long_taps.shape[1]
    code = jax.ShapeDtypeStruct((rows + TILE + held, LANES), jnp.bfloat16)
    top = jax.ShapeDtypeStruct((taps, LANES), jnp.float32)
    return pl.pallas_call(
        functools.partial(head_body, part, count),
        in_specs=[IN_SMEM] + [IN_VMEM] * 8,
        out_specs=[IN_VMEM] * (2 * len(part)),
        out_shape=[top] * len(part) + [code] * len(part),
        compiler_params=kernel_params(12),
        cost_estimate=cost(len(part)),
        name="short_head",
    )(me, halo, value, gate, gated, taps_spec, long_taps, fwd, inv)


def forward_body(code, fwd, widen, spec_out, filter_out):
    rows = fwd.shape[2]
    groups = 8
    x_high, x_low = split(from_code(code[:rows], code[rows : rows + 1].astype(jnp.float32)))
    scale = code[rows : rows + TILE].astype(jnp.float32)[groups:]
    held = code[rows + TILE :]
    many = held.shape[0] // groups
    h_high, h_low = split(from_code(held, jnp.concatenate([scale] * many, 0)))
    h_high, h_low = h_high.astype(jnp.float32), h_low.astype(jnp.float32)
    parts = []
    for c in range(0, held.shape[0], groups):
        pair = jnp.concatenate([h_high[c : c + groups], h_low[c : c + groups]], 0)
        parts.append(dot(pair.T.astype(jnp.bfloat16), widen[...]).astype(jnp.bfloat16))
    taps = jnp.concatenate(parts, 0)
    x_wide = dot(fwd[0], jnp.concatenate([x_high, x_low], 1))
    h_wide = dot(fwd[0], taps)
    low = dot(fwd[1], jnp.concatenate([x_high, taps[:, :LANES]], 1))
    spec_out[...] = x_wide[:, :LANES] + x_wide[:, LANES:] + low[:, :LANES]
    filter_out[...] = h_wide[:, :LANES] + h_wide[:, LANES:] + low[:, LANES:]


def forward_call(code, fwd, widen):
    bins = fwd.shape[1]
    spec = jax.ShapeDtypeStruct((bins, LANES), jnp.float32)
    return pl.pallas_call(
        forward_body,
        in_specs=[IN_VMEM] * 3,
        out_specs=[IN_VMEM] * 2,
        out_shape=[spec, spec],
        compiler_params=kernel_params(12),
        cost_estimate=cost(1),
        name="forward",
    )(code, fwd, widen)


def by_lag_body(me_ref, *refs):
    spectra, out = refs[:-1], refs[-1]
    count = len(spectra)
    half = out.shape[1] // 2
    me = me_ref[0]
    odd = lax.broadcasted_iota(jnp.int32, (8, LANES), 0) % 2 == 1
    sign = jnp.where(odd, 1.0, -1.0)
    lags = [lax.rem(me - d + count, count) for d in range(count)]
    signs = [sign * (lag > 0).astype(jnp.float32) for lag in lags]

    def chunk(c, _):
        re = pl.ds(pl.multiple_of(c * 8, 8), 8)
        im = pl.ds(pl.multiple_of(half + c * 8, 8), 8)
        for d in range(count):
            before = spectra[(d + 1) % count]
            out[lags[d], re] = spectra[d][re] + signs[d] * before[im]
            out[lags[d], im] = spectra[d][im] - signs[d] * before[re]
        out[count, re] = jnp.zeros((8, LANES), jnp.float32)
        out[count, im] = jnp.zeros((8, LANES), jnp.float32)
        return 0

    lax.fori_loop(0, half // 8, chunk, 0, unroll=2)


def by_lag_call(me, spectra):
    count = len(spectra)
    bins = spectra[0].shape[0]
    return pl.pallas_call(
        by_lag_body,
        in_specs=[IN_SMEM] + [IN_VMEM] * count,
        out_specs=IN_VMEM,
        out_shape=jax.ShapeDtypeStruct((count + 1, bins, LANES), jnp.float32),
        compiler_params=kernel_params(12),
        cost_estimate=cost(1),
        name="by_lag",
    )(me, *spectra)


def back_body(part, count, me_ref, filt, inv, *refs):
    specs, codes, total = refs[:count], refs[-1 - len(part) : -1], refs[-1]
    half = filt.shape[1] // 2
    rows = inv.shape[1]
    me = me_ref[0]

    for e, code in zip(part, codes):
        target = lax.rem(me + e, count)
        lags = []
        for d in range(count):
            lag = target - lax.rem(me - d + count, count)
            lags.append(jnp.where(lag >= 0, lag, count))

        def chunk(c, _):
            re = pl.ds(pl.multiple_of(c * 8, 8), 8)
            im = pl.ds(pl.multiple_of(half + c * 8, 8), 8)
            acc_re = jnp.zeros((8, LANES), jnp.float32)
            acc_im = acc_re
            for d in range(count):
                x_re, x_im = specs[d][re], specs[d][im]
                g_re, g_im = filt[lags[d], re], filt[lags[d], im]
                acc_re += x_re * g_re - x_im * g_im
                acc_im += x_re * g_im + x_im * g_re
            total[re] = acc_re
            total[im] = acc_im
            return 0

        lax.fori_loop(0, half // 8, chunk, 0, unroll=2)
        values = dot3(inv, total[...])
        scale = scale_of(jnp.max(jnp.abs(values), axis=0, keepdims=True))
        code[:rows] = to_code(values, scale)
        code[rows:] = jnp.broadcast_to(scale, (TILE, LANES)).astype(jnp.bfloat16)


def back_call(part, me, filt, inv, specs, after):
    count = len(specs)
    bins = specs[0].shape[0]
    code = jax.ShapeDtypeStruct((bins // 2 + TILE, LANES), jnp.bfloat16)
    return pl.pallas_call(
        functools.partial(back_body, part, count),
        in_specs=[IN_SMEM] + [IN_VMEM] * (2 + count) + [IN_ANY] * len(after),
        out_specs=[IN_VMEM] * len(part),
        out_shape=[code] * len(part),
        scratch_shapes=[pltpu.VMEM((bins, LANES), jnp.float32)],
        compiler_params=kernel_params(12),
        cost_estimate=cost(len(part)),
        name="back",
    )(me, filt, inv, *specs, *after)


def final_body(part, count, me, *refs):
    many = len(part)
    codes, tops, (gated, gate, skip) = refs[:many], refs[many : 2 * many], refs[2 * many : 2 * many + 3]
    out, held, sems = refs[-3:]
    taps = tops[0].shape[0]
    rows = gate.shape[0]
    copies = []
    for at, d in enumerate(part):
        cols = lanes_of(lax.rem(me[0] + d, count))
        code, top = codes[at], tops[at]
        scale = code[rows : rows + 1].astype(jnp.float32)
        for r, part_gated in ((slice(0, taps), top[...]), (slice(taps, rows), gated[:, cols])):
            total = from_code(code[r], scale) + skip[:, cols] * part_gated
            held[at, r] = (gate[r, cols].astype(jnp.float32) * total).astype(jnp.bfloat16)
        copies.append(pltpu.make_async_copy(held.at[at], out.at[:, cols], sems.at[at]))
        copies[-1].start()
    for copy in copies:
        copy.wait()


def final_call(part, count, me, codes, tops, gated, gate, skip, so_far):
    rows = gate.shape[0]
    many = len(part)
    args = [me, *codes, *tops, gated, gate, skip]
    specs = [IN_SMEM] + [IN_VMEM] * (2 * many + 3)
    alias = {}
    if so_far is not None:
        alias = {len(args): 0}
        args.append(so_far)
        specs.append(IN_ANY)
    return pl.pallas_call(
        functools.partial(final_body, part, count),
        in_specs=specs,
        out_specs=IN_ANY,
        out_shape=jax.ShapeDtypeStruct(gate.shape, jnp.bfloat16),
        scratch_shapes=[
            pltpu.VMEM((many, rows, LANES), jnp.bfloat16),
            pltpu.SemaphoreType.DMA((many,)),
        ],
        input_output_aliases=alias,
        compiler_params=kernel_params(12),
        cost_estimate=cost(many),
        name="final",
    )(*args)


def rotation_order(count):
    return sorted(range(1, count), key=lambda d: (-min(d, count - d), d))


def in_slabs(output_gate, input_gate, value_input, short_filter, long_filter, skip_gain):
    count = lax.axis_size("ctx")
    me = lax.axis_index("ctx").reshape(1)
    rows = value_input.shape[0]
    taps = short_filter.shape[0]
    groups = long_filter.shape[1] // count
    order = rotation_order(count) + [0]

    def rotated(block, distance):
        return lax.ppermute(block, "ctx", [(i, (i + distance) % count) for i in range(count)])

    def table(values):
        return jnp.asarray(split_table(values))

    halo = passed_along(value_input[rows - taps :], "ctx", 1)
    long_taps = long_filter.T.reshape(count, groups, rows // LANES, LANES)
    long_taps = jnp.swapaxes(long_taps, 1, 2).reshape(count, -1, LANES)

    forward, inverse = tables(taps)
    short_fwd, short_inv = table(forward), table(inverse[taps:])
    forward, inverse = tables(rows)
    fwd, inv = table(forward[:, :rows]), table(inverse[:rows])
    widen = jnp.asarray(widening(groups, LANES))

    gated, taps_spec = main_call(value_input, input_gate, short_filter, short_fwd, short_inv)
    came, tops = {}, {}
    for part in (order[:1], order[1:3], order[3:]):
        outs = head_call(
            part, count, me, halo, value_input, input_gate, gated, taps_spec, long_taps,
            short_fwd, short_inv,
        )
        for d, top, code in zip(part, outs, outs[len(part) :]):
            tops[d] = top
            came[d] = rotated(code, d) if d else code

    specs, spectra = [None] * count, [None] * count
    for d in order[-1:] + order[:-1]:
        specs[d], spectra[d] = forward_call(came[d], fwd, widen)
    filt = by_lag_call(me, spectra)

    answers, after = {}, []
    for part in (order[:1], order[1:3], order[3:]):
        codes = back_call(part, me, filt, inv, specs, after)
        for e, code in zip(part, codes):
            answers[e] = rotated(code, e) if e else code
        after = codes[:1]

    mixed = None
    for part in (order[-1:] + order[:3], order[3:6], order[6:-1]):
        owners = [(count - e) % count for e in part]
        mixed = final_call(
            owners, count, me, [answers[e] for e in part], [tops[d] for d in owners], gated,
            output_gate, skip_gain[None], mixed,
        )
    return mixed


def local(output_gate, input_gate, value_input, short_filter, long_filter, skip_gain):
    count = lax.axis_size("ctx")
    rows, chans = value_input.shape
    taps = short_filter.shape[0]
    groups = long_filter.shape[1]
    fits = chans == LANES * count and groups == 8 * count and taps == LANES
    fits = fits and rows % taps == 0 and rows > taps
    run = in_slabs if fits else plain
    return run(output_gate, input_gate, value_input, short_filter, long_filter, skip_gain)


def solution(mesh):
    placed = (
        P("ctx", "ch"),
        P("ctx", "ch"),
        P("ctx", "ch"),
        P(None, "ch"),
        P("ctx", "ch"),
        P("ch"),
    )
    return jax.shard_map(
        local, mesh=mesh, in_specs=placed, out_specs=P("ctx", "ch"), check_vma=False
    )
```

profile of v0, /device:TPU:0, one launch (start us, length us, event | category | flops | bytes accessed | tf_op | source)
XLA Modules:
  0.0 80.1 jit_solution(12386665923162182807)
XLA Ops:
  0.0 1.0 %slice.3 = bf16[128,1024]{1,0:T(8,128)(2,1)S(1)} slice(bf16[512,1024]{1,0:T(8,128)(2,1)} %value.7), slice={[384:512], [0:1024]} | slice | bytes 524288 | tf_op jit(solution)/shard_map/slice | solution.py:465
  1.0 2.4 %collective-permute-start = (bf16[128,1024]{1,0:T(8,128)(2,1)S(1)}, bf16[128,1024]{1,0:T(8,128)(2,1)S(1)}, u32[]{:S(2)}, u32[]{:S(2)}) collective-permute-start(bf16[128,1024]{1,0:T(8,128)(2,1)S(1)} %slice.3), channel_id=1, source_target_pairs={{0,4},{4,8},{8,12},{12,16},{16,20},{20,24},{24,28},{1,5},{5,9},{9,... | collective-permute-start | bytes 786440 | tf_op jit(solution)/shard_map/ppermute | solution.py:24
  3.4 0.0 copy-start.1
  3.4 1.2 %copy-done.1 = bf16[512,1024]{1,0:T(8,128)(2,1)S(1)} copy-done((bf16[512,1024]{1,0:T(8,128)(2,1)S(1)}, bf16[512,1024]{1,0:T(8,128)(2,1)}, u32[]{:S(2)}) %copy-start.1) | copy-done | bytes 1048600
  4.6 1.2 %copy-done.3 = bf16[512,1024]{1,0:T(8,128)(2,1)S(1)} copy-done((bf16[512,1024]{1,0:T(8,128)(2,1)S(1)}, bf16[512,1024]{1,0:T(8,128)(2,1)}, u32[]{:S(2)}) %copy-start.3) | copy-done | bytes 1048600
  5.8 0.9 %copy-done.5 = bf16[2,256,256]{2,1,0:T(8,128)(2,1)S(1)} copy-done((bf16[2,256,256]{2,1,0:T(8,128)(2,1)S(1)}, bf16[2,256,256]{2,1,0:T(8,128)(2,1)}, u32[]{:S(2)}) %copy-start.5) | copy-done | bytes 262168
  6.8 0.9 %copy-done.6 = bf16[2,128,256]{2,1,0:T(8,128)(2,1)S(1)} copy-done((bf16[2,128,256]{2,1,0:T(8,128)(2,1)S(1)}, bf16[2,128,256]{2,1,0:T(8,128)(2,1)}, u32[]{:S(2)}) %copy-start.6) | copy-done | bytes 131096
  7.7 1.0 %copy-done.9 = f32[128,1024]{1,0:T(8,128)S(1)} copy-done((f32[128,1024]{1,0:T(8,128)S(1)}, f32[128,1024]{1,0:T(8,128)}, u32[]{:S(2)}) %copy-start.9) | copy-done | bytes 524312
  8.7 2.7 %short_main.1 = (f32[384,1024]{1,0:T(8,128)S(1)}, f32[256,1024]{1,0:T(8,128)S(1)}) custom-call(bf16[512,1024]{1,0:T(8,128)(2,1)S(1)} %copy-done.1, bf16[512,1024]{1,0:T(8,128)(2,1)S(1)} %copy-done.3, f32[128,1024]{1,0:T(8,128)S(1)} %copy-done.9, bf16[2,256,256]{2,1,0:T(8,128)(2,1)S(1)} %copy-done.5, bf16[2,128,256]{2,1,0:T(8,128)(2,1)S(1)} %copy-done.6), custom_call_target="tpu_custom_call" | custom-call | flops 4000000 | bytes 4000 | tf_op jit(solution)/shard_map/short_main/pallas_call | solution.py:214
  11.5 0.0 collective-permute-done.halo
  11.5 0.0 copy-done.7
  11.5 1.8 %short_head.3 = (f32[128,128]{1,0:T(8,128)S(1)}, f32[128,128]{1,0:T(8,128)S(1)}, f32[128,128]{1,0:T(8,128)S(1)}, f32[128,128]{1,0:T(8,128)S(1)}, f32[128,128]{1,...) custom-call(s32[1]{0:T(128)} %bitcast.me.me_ref, ...), custom_call_target="tpu_custom_call" | custom-call | flops 5000000 | bytes 5000 | tf_op jit(solution)/shard_map/short_head/pallas_call | solution.py:267
  13.3 4.6 %collective-permute-start.6 = (bf16[560,128]{1,0:T(8,128)(2,1)S(1)}, bf16[560,128]{1,0:T(8,128)(2,1)S(1)}, u32[]{:S(2)}, u32[]{:S(2)}) collective-permute-start(bf16[560,128]{1,0:T(8,128)(2,1)S(1)} %get-tuple-element.60), channel_id=1, source_target_pairs={{0,24},{4,28},{8,0},{12,4},{16,8},{20,12},{24,16},{28,20},{1,25},{... | collective-permute-start | bytes 430088 | tf_op jit(solution)/shard_map/ppermute | solution.py:460
  17.9 1.5 %collective-permute-start.7 = (bf16[560,128]{1,0:T(8,128)(2,1)S(1)}, bf16[560,128]{1,0:T(8,128)(2,1)S(1)}, u32[]{:S(2)}, u32[]{:S(2)}) collective-permute-start(bf16[560,128]{1,0:T(8,128)(2,1)S(1)} %get-tuple-element.62), channel_id=1, source_target_pairs={{0,28},{4,0},{8,4},{12,8},{16,12},{20,16},{24,20},{28,24},{1,29},{... | collective-permute-start | bytes 430088 | tf_op jit(solution)/shard_map/ppermute | solution.py:460
  19.4 0.0 collective-permute-start.1
  19.4 0.0 collective-permute-start.2
  19.4 0.8 %short_head.4 = (f32[128,128]{1,0:T(8,128)S(1)}, f32[128,128]{1,0:T(8,128)S(1)}, bf16[560,128]{1,0:T(8,128)(2,1)S(1)}, bf16[560,128]{1,0:T(8,128)(2,1)S(1)}) custom-call(s32[1]{0:T(128)} %bitcast.me.me_ref, bf16[128,1024]{1,0:T(8,128)(2,1)S(1)} %collective-permute-done.halo, bf16[512,1024]{1,0:T(8,128)(2,1)S(1)} %copy-done.1, ...), custom_call_target="tpu_custom_call" | custom-call | flops 2000000 | bytes 2000 | tf_op jit(solution)/shard_map/short_head/pallas_call | solution.py:267
  20.2 0.0 copy-start
  20.2 0.0 copy-start.8
  20.2 3.9 %collective-permute-start.5 = (bf16[560,128]{1,0:T(8,128)(2,1)S(1)}, bf16[560,128]{1,0:T(8,128)(2,1)S(1)}, u32[]{:S(2)}, u32[]{:S(2)}) collective-permute-start(bf16[560,128]{1,0:T(8,128)(2,1)S(1)} %get-tuple-element.58), channel_id=1, source_target_pairs={{0,20},{4,24},{8,28},{12,0},{16,4},{20,8},{24,12},{28,16},{1,21},{... | collective-permute-start | bytes 430088 | tf_op jit(solution)/shard_map/ppermute | solution.py:460
  24.1 0.5 short_head.5
  24.6 0.0 collective-permute-done.6.code
  24.6 0.2 collective-permute-start.3
  24.9 0.3 collective-permute-done.7.code
  25.1 0.0 collective-permute-start.4
  25.2 0.0 copy-done
  25.2 0.0 copy-done.8
  25.2 1.2 %forward.8 = (f32[1024,128]{1,0:T(8,128)S(1)}, f32[1024,128]{1,0:T(8,128)S(1)}) custom-call(bf16[560,128]{1,0:T(8,128)(2,1)S(1)} %get-tuple-element.48.code, bf16[2,1024,512]{2,1,0:T(8,128)(2,1)S(1)} %copy-done, bf16[16,256]{1,0:T(8,128)(2,1)S(1)} %copy-done.8), custom_call_target="tpu_custom_call" | custom-call | flops 1000000 | bytes 1000 | tf_op jit(solution)/shard_map/forward/pallas_call | solution.py:302
  26.3 1.2 %forward.15 = (f32[1024,128]{1,0:T(8,128)S(1)}, f32[1024,128]{1,0:T(8,128)S(1)}) custom-call(bf16[560,128]{1,0:T(8,128)(2,1)S(1)} %collective-permute-done.7.code, bf16[2,1024,512]{2,1,0:T(8,128)(2,1)S(1)} %copy-done, bf16[16,256]{1,0:T(8,128)(2,1)S(1)} %copy-done.8), custom_call_target="tpu_custom_call" | custom-call | flops 1000000 | bytes 1000 | tf_op jit(solution)/shard_map/forward/pallas_call | solution.py:302
  27.5 1.2 %forward.14 = (f32[1024,128]{1,0:T(8,128)S(1)}, f32[1024,128]{1,0:T(8,128)S(1)}) custom-call(bf16[560,128]{1,0:T(8,128)(2,1)S(1)} %collective-permute-done.6.code, bf16[2,1024,512]{2,1,0:T(8,128)(2,1)S(1)} %copy-done, bf16[16,256]{1,0:T(8,128)(2,1)S(1)} %copy-done.8), custom_call_target="tpu_custom_call" | custom-call | flops 1000000 | bytes 1000 | tf_op jit(solution)/shard_map/forward/pallas_call | solution.py:302
  28.6 0.0 collective-permute-done.2.code
  28.7 1.2 %forward.10 = (f32[1024,128]{1,0:T(8,128)S(1)}, f32[1024,128]{1,0:T(8,128)S(1)}) custom-call(bf16[560,128]{1,0:T(8,128)(2,1)S(1)} %collective-permute-done.2.code, bf16[2,1024,512]{2,1,0:T(8,128)(2,1)S(1)} %copy-done, bf16[16,256]{1,0:T(8,128)(2,1)S(1)} %copy-done.8), custom_call_target="tpu_custom_call" | custom-call | flops 1000000 | bytes 1000 | tf_op jit(solution)/shard_map/forward/pallas_call | solution.py:302
  29.8 0.0 collective-permute-done.1.code
  29.8 1.2 %forward.9 = (f32[1024,128]{1,0:T(8,128)S(1)}, f32[1024,128]{1,0:T(8,128)S(1)}) custom-call(bf16[560,128]{1,0:T(8,128)(2,1)S(1)} %collective-permute-done.1.code, bf16[2,1024,512]{2,1,0:T(8,128)(2,1)S(1)} %copy-done, bf16[16,256]{1,0:T(8,128)(2,1)S(1)} %copy-done.8), custom_call_target="tpu_custom_call" | custom-call | flops 1000000 | bytes 1000 | tf_op jit(solution)/shard_map/forward/pallas_call | solution.py:302
  31.0 0.3 collective-permute-done.5.code
  31.3 1.1 %forward.13 = (f32[1024,128]{1,0:T(8,128)S(1)}, f32[1024,128]{1,0:T(8,128)S(1)}) custom-call(bf16[560,128]{1,0:T(8,128)(2,1)S(1)} %collective-permute-done.5.code, bf16[2,1024,512]{2,1,0:T(8,128)(2,1)S(1)} %copy-done, bf16[16,256]{1,0:T(8,128)(2,1)S(1)} %copy-done.8), custom_call_target="tpu_custom_call" | custom-call | flops 1000000 | bytes 1000 | tf_op jit(solution)/shard_map/forward/pallas_call | solution.py:302
  32.4 10.2 %collective-permute-done.3.code = bf16[560,128]{1,0:T(8,128)(2,1)S(1)} collective-permute-done((bf16[560,128]{1,0:T(8,128)(2,1)S(1)}, bf16[560,128]{1,0:T(8,128)(2,1)S(1)}, u32[]{:S(2)}, u32[]{:S(2)}) %collective-permute-start.3) | collective-permute-done | bytes 143392 | tf_op jit(solution)/shard_map/ppermute | solution.py:460
  42.6 1.2 %forward.11 = (f32[1024,128]{1,0:T(8,128)S(1)}, f32[1024,128]{1,0:T(8,128)S(1)}) custom-call(bf16[560,128]{1,0:T(8,128)(2,1)S(1)} %collective-permute-done.3.code, bf16[2,1024,512]{2,1,0:T(8,128)(2,1)S(1)} %copy-done, bf16[16,256]{1,0:T(8,128)(2,1)S(1)} %copy-done.8), custom_call_target="tpu_custom_call" | custom-call | flops 1000000 | bytes 1000 | tf_op jit(solution)/shard_map/forward/pallas_call | solution.py:302
  43.8 0.0 collective-permute-done.4.code
  43.8 1.2 %forward.12 = (f32[1024,128]{1,0:T(8,128)S(1)}, f32[1024,128]{1,0:T(8,128)S(1)}) custom-call(bf16[560,128]{1,0:T(8,128)(2,1)S(1)} %collective-permute-done.4.code, bf16[2,1024,512]{2,1,0:T(8,128)(2,1)S(1)} %copy-done, bf16[16,256]{1,0:T(8,128)(2,1)S(1)} %copy-done.8), custom_call_target="tpu_custom_call" | custom-call | flops 1000000 | bytes 1000 | tf_op jit(solution)/shard_map/forward/pallas_call | solution.py:302
  45.0 0.0 copy-start.2
  45.0 0.8 by_lag.1.filt
  45.8 0.8 %copy-done.2 = bf16[2,512,1024]{2,1,0:T(8,128)(2,1)S(1)} copy-done((bf16[2,512,1024]{2,1,0:T(8,128)(2,1)S(1)}, bf16[2,512,1024]{2,1,0:T(8,128)(2,1)}, u32[]{:S(2)}) %copy-start.2) | copy-done | bytes 2097176
  46.6 1.8 %back.3.refs_8_ = bf16[528,128]{1,0:T(8,128)(2,1)S(1)} custom-call(s32[1]{0:T(128)} %bitcast.me.me_ref, f32[9,1024,128]{2,1,0:T(8,128)S(1)} %by_lag.1.filt, bf16[2,512,1024]{2,1,0:T(8,128)(2,1)S(1)} %copy-done.2, f32[1024,128]{1,0:T(8,128)S(1)} %get-tuple-element.64.refs_0_, f32[1024,128]{1,0:T(8,128)S(1)} %get-tuple-element.65.refs_1_, ...), custom_call_target="tpu_custom_call" | custom-call | flops 1000000 | bytes 1000 | tf_op jit(solution)/shard_map/back/pallas_call | solution.py:389
  48.4 0.1 collective-permute-start.12
  48.5 3.8 %back.4 = (bf16[528,128]{1,0:T(8,128)(2,1)S(1)}, bf16[528,128]{1,0:T(8,128)(2,1)S(1)}) custom-call(s32[1]{0:T(128)} %bitcast.me.me_ref, f32[9,1024,128]{2,1,0:T(8,128)S(1)} %by_lag.1.filt, bf16[2,512,1024]{2,1,0:T(8,128)(2,1)S(1)} %copy-done.2, f32[1024,128]{1,0:T(8,128)S(1)} %get-tuple-element.64.refs_0_, f32[1024,128]{1,0:T(8,128)S(1)} %get-tuple-element.65.refs_1_, ...), custom_call_target="tpu_custom_call" | custom-call | flops 2000000 | bytes 2000 | tf_op jit(solution)/shard_map/back/pallas_call | solution.py:389
  52.3 2.4 %collective-permute-start.14 = (bf16[528,128]{1,0:T(8,128)(2,1)S(1)}, bf16[528,128]{1,0:T(8,128)(2,1)S(1)}, u32[]{:S(2)}, u32[]{:S(2)}) collective-permute-start(bf16[528,128]{1,0:T(8,128)(2,1)S(1)} %get-tuple-element.82), channel_id=1, source_target_pairs={{0,20},{4,24},{8,28},{12,0},{16,4},{20,8},{24,12},{28,16},{1,21},{... | collective-permute-start | bytes 405512 | tf_op jit(solution)/shard_map/ppermute | solution.py:460
  54.7 0.0 collective-permute-start.13
  54.7 9.4 %back.5 = (bf16[528,128]{1,0:T(8,128)(2,1)S(1)}, bf16[528,128]{1,0:T(8,128)(2,1)S(1)}, bf16[528,128]{1,0:T(8,128)(2,1)S(1)}, bf16[528,128]{1,0:T(8,128)(2,1)S(1)}, bf16[528,128]{1,0:T(8,128)(2,1)S(1)}) custom-call(s32[1]{0:T(128)} %bitcast.me.me_ref, f32[9,1024,128]{2,1,0:T(8,128)S(1)} %by_lag.1.filt, bf16[2,512,1024]{2,1,0:T(8,128)(2,1)S(1)} %copy-done.2, ...), custom_call_target="tpu_custom_call" | custom-call | flops 5000000 | bytes 5000 | tf_op jit(solution)/shard_map/back/pallas_call | solution.py:389
  64.1 2.2 %collective-permute-start.9 = (bf16[528,128]{1,0:T(8,128)(2,1)S(1)}, bf16[528,128]{1,0:T(8,128)(2,1)S(1)}, u32[]{:S(2)}, u32[]{:S(2)}) collective-permute-start(bf16[528,128]{1,0:T(8,128)(2,1)S(1)} %get-tuple-element.75), channel_id=1, source_target_pairs={{0,8},{4,12},{8,16},{12,20},{16,24},{20,28},{24,0},{28,4},{1,9},{5... | collective-permute-start | bytes 405512 | tf_op jit(solution)/shard_map/ppermute | solution.py:460
  66.3 1.7 %collective-permute-start.10 = (bf16[528,128]{1,0:T(8,128)(2,1)S(1)}, bf16[528,128]{1,0:T(8,128)(2,1)S(1)}, u32[]{:S(2)}, u32[]{:S(2)}) collective-permute-start(bf16[528,128]{1,0:T(8,128)(2,1)S(1)} %get-tuple-element.76), channel_id=1, source_target_pairs={{0,24},{4,28},{8,0},{12,4},{16,8},{20,12},{24,16},{28,20},{1,25},{... | collective-permute-start | bytes 405512 | tf_op jit(solution)/shard_map/ppermute | solution.py:460
  68.0 0.0 collective-permute-done.12.refs_1_
  68.0 0.3 collective-permute-start.11
  68.3 0.0 collective-permute-done.14.refs_3_
  68.3 3.2 %collective-permute-start.8 = (bf16[528,128]{1,0:T(8,128)(2,1)S(1)}, bf16[528,128]{1,0:T(8,128)(2,1)S(1)}, u32[]{:S(2)}, u32[]{:S(2)}) collective-permute-start(bf16[528,128]{1,0:T(8,128)(2,1)S(1)} %get-tuple-element.73), channel_id=1, source_target_pairs={{0,28},{4,0},{8,4},{12,8},{16,12},{20,16},{24,20},{28,24},{1,29},{... | collective-permute-start | bytes 405512 | tf_op jit(solution)/shard_map/ppermute | solution.py:460
  71.5 0.0 collective-permute-done.13.refs_2_
  71.5 0.0 copy-done.10
  71.5 1.2 %final.3.refs_9_ = bf16[512,1024]{1,0:T(8,128)(2,1)} custom-call(s32[1]{0:T(128)} %bitcast.me.me_ref, bf16[528,128]{1,0:T(8,128)(2,1)S(1)} %get-tuple-element.81.refs_0_, bf16[528,128]{1,0:T(8,128)(2,1)S(1)} %collective-permute-done.12.refs_1_, bf16[528,128]{1,0:T(8,128)(2,1)S(1)} %collective-permute-done.13.refs_2_, ...), custom_call_target="tpu_custom_call" | custom-call | flops 4000000 | bytes 4000 | tf_op jit(solution)/shard_map/final/pallas_call | solution.py:431
  72.8 0.0 collective-permute-done.9.refs_0_
  72.8 2.1 %collective-permute-done.10.refs_1_ = bf16[528,128]{1,0:T(8,128)(2,1)S(1)} collective-permute-done((bf16[528,128]{1,0:T(8,128)(2,1)S(1)}, bf16[528,128]{1,0:T(8,128)(2,1)S(1)}, u32[]{:S(2)}, u32[]{:S(2)}) %collective-permute-start.10) | collective-permute-done | bytes 135200 | tf_op jit(solution)/shard_map/ppermute | solution.py:460
  74.9 3.2 %collective-permute-done.11.refs_2_ = bf16[528,128]{1,0:T(8,128)(2,1)S(1)} collective-permute-done((bf16[528,128]{1,0:T(8,128)(2,1)S(1)}, bf16[528,128]{1,0:T(8,128)(2,1)S(1)}, u32[]{:S(2)}, u32[]{:S(2)}) %collective-permute-start.11) | collective-permute-done | bytes 135200 | tf_op jit(solution)/shard_map/ppermute | solution.py:460
  78.0 1.1 %final.4.refs_5_ = bf16[512,1024]{1,0:T(8,128)(2,1)} custom-call(s32[1]{0:T(128)} %bitcast.me.me_ref, bf16[528,128]{1,0:T(8,128)(2,1)S(1)} %collective-permute-done.9.refs_0_, bf16[528,128]{1,0:T(8,128)(2,1)S(1)} %collective-permute-done.10.refs_1_, bf16[528,128]{1,0:T(8,128)(2,1)S(1)} %collective-permute-done.11.refs_2_, ...), custom_call_target="tpu_custom_call", output_to_operand_aliasing={{}: (10, {})} | custom-call | flops 3000000 | bytes 3000 | tf_op jit(solution)/shard_map/final/pallas_call | solution.py:431
  79.1 0.0 collective-permute-done.8.refs_0_
  79.1 0.8 %final.5 = bf16[512,1024]{1,0:T(8,128)(2,1)} custom-call(s32[1]{0:T(128)} %bitcast.me.me_ref, bf16[528,128]{1,0:T(8,128)(2,1)S(1)} %collective-permute-done.8.refs_0_, f32[128,128]{1,0:T(8,128)S(1)} %get-tuple-element.74.refs_1_, f32[384,1024]{1,0:T(8,128)S(1)} %get-tuple-element.46.gated.refs_8_.refs_6_.refs_2_, ...), custom_call_target="tpu_custom_call", output_to_operand_aliasing={{}: (6, {})} | custom-call | flops 1000000 | bytes 1000 | tf_op jit(solution)/shard_map/final/pallas_call | solution.py:431
  (8 shorter events, 0.0 us)
Async XLA Ops:
  0.0 11.5 %copy-start.7 = (f32[512,64]{0,1:T(8,128)S(1)}, f32[512,64]{0,1:T(8,128)}, u32[]{:S(2)}) copy-start(f32[512,64]{0,1:T(8,128)} %param.15) | copy-start | bytes 393220
  1.0 10.5 %collective-permute-start = (bf16[128,1024]{1,0:T(8,128)(2,1)S(1)}, bf16[128,1024]{1,0:T(8,128)(2,1)S(1)}, u32[]{:S(2)}, u32[]{:S(2)}) collective-permute-start(bf16[128,1024]{1,0:T(8,128)(2,1)S(1)} %slice.3), channel_id=1, source_target_pairs={{0,4},{4,8},{8,12},{12,16},{16,20},{20,24},{24,28},{1,5},{5,9},{9,... | collective-permute-start | bytes 786440 | tf_op jit(solution)/shard_map/ppermute | solution.py:24
  3.4 1.2 %copy-start.1 = (bf16[512,1024]{1,0:T(8,128)(2,1)S(1)}, bf16[512,1024]{1,0:T(8,128)(2,1)}, u32[]{:S(2)}) copy-start(bf16[512,1024]{1,0:T(8,128)(2,1)} %value.7) | copy-start | bytes 3145732
  4.6 1.2 %copy-start.3 = (bf16[512,1024]{1,0:T(8,128)(2,1)S(1)}, bf16[512,1024]{1,0:T(8,128)(2,1)}, u32[]{:S(2)}) copy-start(bf16[512,1024]{1,0:T(8,128)(2,1)} %gate.7) | copy-start | bytes 3145732
  5.8 0.9 %copy-start.5 = (bf16[2,256,256]{2,1,0:T(8,128)(2,1)S(1)}, bf16[2,256,256]{2,1,0:T(8,128)(2,1)}, u32[]{:S(2)}) copy-start(bf16[2,256,256]{2,1,0:T(8,128)(2,1)} %constant.16.clone.fwd) | copy-start | bytes 786436
  6.8 0.9 %copy-start.6 = (bf16[2,128,256]{2,1,0:T(8,128)(2,1)S(1)}, bf16[2,128,256]{2,1,0:T(8,128)(2,1)}, u32[]{:S(2)}) copy-start(bf16[2,128,256]{2,1,0:T(8,128)(2,1)} %constant.17.clone.inv) | copy-start | bytes 393220
  7.7 1.0 %copy-start.9 = (f32[128,1024]{1,0:T(8,128)S(1)}, f32[128,1024]{1,0:T(8,128)}, u32[]{:S(2)}) copy-start(f32[128,1024]{1,0:T(8,128)} %taps.1) | copy-start | bytes 1572868
  13.3 11.3 %collective-permute-start.6 = (bf16[560,128]{1,0:T(8,128)(2,1)S(1)}, bf16[560,128]{1,0:T(8,128)(2,1)S(1)}, u32[]{:S(2)}, u32[]{:S(2)}) collective-permute-start(bf16[560,128]{1,0:T(8,128)(2,1)S(1)} %get-tuple-element.60), channel_id=1, source_target_pairs={{0,24},{4,28},{8,0},{12,4},{16,8},{20,12},{24,16},{28,20},{1,25},{... | collective-permute-start | bytes 430088 | tf_op jit(solution)/shard_map/ppermute | solution.py:460
  17.9 7.2 %collective-permute-start.7 = (bf16[560,128]{1,0:T(8,128)(2,1)S(1)}, bf16[560,128]{1,0:T(8,128)(2,1)S(1)}, u32[]{:S(2)}, u32[]{:S(2)}) collective-permute-start(bf16[560,128]{1,0:T(8,128)(2,1)S(1)} %get-tuple-element.62), channel_id=1, source_target_pairs={{0,28},{4,0},{8,4},{12,8},{16,12},{20,16},{24,20},{28,24},{1,29},{... | collective-permute-start | bytes 430088 | tf_op jit(solution)/shard_map/ppermute | solution.py:460
  19.4 10.4 %collective-permute-start.1 = (bf16[560,128]{1,0:T(8,128)(2,1)S(1)}, bf16[560,128]{1,0:T(8,128)(2,1)S(1)}, u32[]{:S(2)}, u32[]{:S(2)}) collective-permute-start(bf16[560,128]{1,0:T(8,128)(2,1)S(1)} %get-tuple-element.50), channel_id=1, source_target_pairs={{0,4},{4,8},{8,12},{12,16},{16,20},{20,24},{24,28},{28,0},{1,5},{5... | collective-permute-start | bytes 430088 | tf_op jit(solution)/shard_map/ppermute | solution.py:460
  19.4 9.2 %collective-permute-start.2 = (bf16[560,128]{1,0:T(8,128)(2,1)S(1)}, bf16[560,128]{1,0:T(8,128)(2,1)S(1)}, u32[]{:S(2)}, u32[]{:S(2)}) collective-permute-start(bf16[560,128]{1,0:T(8,128)(2,1)S(1)} %get-tuple-element.52), channel_id=1, source_target_pairs={{0,8},{4,12},{8,16},{12,20},{16,24},{20,28},{24,0},{28,4},{1,9},{5... | collective-permute-start | bytes 430088 | tf_op jit(solution)/shard_map/ppermute | solution.py:460
  20.2 4.9 %copy-start = (bf16[2,1024,512]{2,1,0:T(8,128)(2,1)S(1)}, bf16[2,1024,512]{2,1,0:T(8,128)(2,1)}, u32[]{:S(2)}) copy-start(bf16[2,1024,512]{2,1,0:T(8,128)(2,1)} %constant.18.clone.fwd) | copy-start | bytes 6291460
  20.2 4.9 %copy-start.8 = (bf16[16,256]{1,0:T(8,128)(2,1)S(1)}, bf16[16,256]{1,0:T(8,128)(2,1)}, u32[]{:S(2)}) copy-start(bf16[16,256]{1,0:T(8,128)(2,1)} %constant.20.clone.widen) | copy-start | bytes 24580
  20.2 11.0 %collective-permute-start.5 = (bf16[560,128]{1,0:T(8,128)(2,1)S(1)}, bf16[560,128]{1,0:T(8,128)(2,1)S(1)}, u32[]{:S(2)}, u32[]{:S(2)}) collective-permute-start(bf16[560,128]{1,0:T(8,128)(2,1)S(1)} %get-tuple-element.58), channel_id=1, source_target_pairs={{0,20},{4,24},{8,28},{12,0},{16,4},{20,8},{24,12},{28,16},{1,21},{... | collective-permute-start | bytes 430088 | tf_op jit(solution)/shard_map/ppermute | solution.py:460
  24.6 18.0 %collective-permute-start.3 = (bf16[560,128]{1,0:T(8,128)(2,1)S(1)}, bf16[560,128]{1,0:T(8,128)(2,1)S(1)}, u32[]{:S(2)}, u32[]{:S(2)}) collective-permute-start(bf16[560,128]{1,0:T(8,128)(2,1)S(1)} %get-tuple-element.54), channel_id=1, source_target_pairs={{0,12},{4,16},{8,20},{12,24},{16,28},{20,0},{24,4},{28,8},{1,13},{... | collective-permute-start | bytes 430088 | tf_op jit(solution)/shard_map/ppermute | solution.py:460
  25.1 18.7 %collective-permute-start.4 = (bf16[560,128]{1,0:T(8,128)(2,1)S(1)}, bf16[560,128]{1,0:T(8,128)(2,1)S(1)}, u32[]{:S(2)}, u32[]{:S(2)}) collective-permute-start(bf16[560,128]{1,0:T(8,128)(2,1)S(1)} %get-tuple-element.56), channel_id=1, source_target_pairs={{0,16},{4,20},{8,24},{12,28},{16,0},{20,4},{24,8},{28,12},{1,17},{... | collective-permute-start | bytes 430088 | tf_op jit(solution)/shard_map/ppermute | solution.py:460
  45.0 1.6 %copy-start.2 = (bf16[2,512,1024]{2,1,0:T(8,128)(2,1)S(1)}, bf16[2,512,1024]{2,1,0:T(8,128)(2,1)}, u32[]{:S(2)}) copy-start(bf16[2,512,1024]{2,1,0:T(8,128)(2,1)} %constant.19.clone.inv) | copy-start | bytes 6291460
  48.4 19.6 %collective-permute-start.12 = (bf16[528,128]{1,0:T(8,128)(2,1)S(1)}, bf16[528,128]{1,0:T(8,128)(2,1)S(1)}, u32[]{:S(2)}, u32[]{:S(2)}) collective-permute-start(bf16[528,128]{1,0:T(8,128)(2,1)S(1)} %back.3.refs_8_), channel_id=1, source_target_pairs={{0,16},{4,20},{8,24},{12,28},{16,0},{20,4},{24,8},{28,12},{1,17},{... | collective-permute-start | bytes 405512 | tf_op jit(solution)/shard_map/ppermute | solution.py:460
  52.3 16.0 %collective-permute-start.14 = (bf16[528,128]{1,0:T(8,128)(2,1)S(1)}, bf16[528,128]{1,0:T(8,128)(2,1)S(1)}, u32[]{:S(2)}, u32[]{:S(2)}) collective-permute-start(bf16[528,128]{1,0:T(8,128)(2,1)S(1)} %get-tuple-element.82), channel_id=1, source_target_pairs={{0,20},{4,24},{8,28},{12,0},{16,4},{20,8},{24,12},{28,16},{1,21},{... | collective-permute-start | bytes 405512 | tf_op jit(solution)/shard_map/ppermute | solution.py:460
  54.7 16.8 %copy-start.4 = (bf16[512,1024]{1,0:T(8,128)(2,1)S(1)}, bf16[512,1024]{1,0:T(8,128)(2,1)}, u32[]{:S(2)}) copy-start(bf16[512,1024]{1,0:T(8,128)(2,1)} %refs_3_.1) | copy-start | bytes 3145732
  54.7 16.8 %copy-start.10 = (f32[1024]{0:T(1024)S(1)}, f32[1024]{0:T(1024)}, u32[]{:S(2)}) copy-start(f32[1024]{0:T(1024)} %param.16) | copy-start | bytes 12292
  54.7 16.8 %collective-permute-start.13 = (bf16[528,128]{1,0:T(8,128)(2,1)S(1)}, bf16[528,128]{1,0:T(8,128)(2,1)S(1)}, u32[]{:S(2)}, u32[]{:S(2)}) collective-permute-start(bf16[528,128]{1,0:T(8,128)(2,1)S(1)} %get-tuple-element.72.refs_8_), channel_id=1, source_target_pairs={{0,12},{4,16},{8,20},{12,24},{16,28},{20,0},{24,4},{28,8},{1,13},{... | collective-permute-start | bytes 405512 | tf_op jit(solution)/shard_map/ppermute | solution.py:460
  64.1 8.7 %collective-permute-start.9 = (bf16[528,128]{1,0:T(8,128)(2,1)S(1)}, bf16[528,128]{1,0:T(8,128)(2,1)S(1)}, u32[]{:S(2)}, u32[]{:S(2)}) collective-permute-start(bf16[528,128]{1,0:T(8,128)(2,1)S(1)} %get-tuple-element.75), channel_id=1, source_target_pairs={{0,8},{4,12},{8,16},{12,20},{16,24},{20,28},{24,0},{28,4},{1,9},{5... | collective-permute-start | bytes 405512 | tf_op jit(solution)/shard_map/ppermute | solution.py:460
  66.3 8.6 %collective-permute-start.10 = (bf16[528,128]{1,0:T(8,128)(2,1)S(1)}, bf16[528,128]{1,0:T(8,128)(2,1)S(1)}, u32[]{:S(2)}, u32[]{:S(2)}) collective-permute-start(bf16[528,128]{1,0:T(8,128)(2,1)S(1)} %get-tuple-element.76), channel_id=1, source_target_pairs={{0,24},{4,28},{8,0},{12,4},{16,8},{20,12},{24,16},{28,20},{1,25},{... | collective-permute-start | bytes 405512 | tf_op jit(solution)/shard_map/ppermute | solution.py:460
  68.0 10.1 %collective-permute-start.11 = (bf16[528,128]{1,0:T(8,128)(2,1)S(1)}, bf16[528,128]{1,0:T(8,128)(2,1)S(1)}, u32[]{:S(2)}, u32[]{:S(2)}) collective-permute-start(bf16[528,128]{1,0:T(8,128)(2,1)S(1)} %get-tuple-element.77), channel_id=1, source_target_pairs={{0,4},{4,8},{8,12},{12,16},{16,20},{20,24},{24,28},{28,0},{1,5},{5... | collective-permute-start | bytes 405512 | tf_op jit(solution)/shard_map/ppermute | solution.py:460
  68.3 10.8 %collective-permute-start.8 = (bf16[528,128]{1,0:T(8,128)(2,1)S(1)}, bf16[528,128]{1,0:T(8,128)(2,1)S(1)}, u32[]{:S(2)}, u32[]{:S(2)}) collective-permute-start(bf16[528,128]{1,0:T(8,128)(2,1)S(1)} %get-tuple-element.73), channel_id=1, source_target_pairs={{0,28},{4,0},{8,4},{12,8},{16,12},{20,16},{24,20},{28,24},{1,29},{... | collective-permute-start | bytes 405512 | tf_op jit(solution)/shard_map/ppermute | solution.py:460
where the time goes:
time: 80.5 us; the launch traced here: 80.1 us
  Pallas kernels  33.8 us (42%)
  starting transfers between devices  22.5 us (28%)
  waiting for transfers between devices  16.1 us (20%)
  local copies, waits for them, and re-layouts  7.19 us (9%)
    ppermute x14, starting transfers between devices, rotated(): lax.ppermute(block, 'ctx', [(i, (i + distance) % count) for i in range(co...  20.2 us
    ppermute x14, waiting for transfers between devices, rotated(): lax.ppermute(block, 'ctx', [(i, (i + distance) % count) for i in range(co...  16.1 us
    pallas_call x3, Pallas kernels, back_call(): pl.pallas_call(functools.partial(back_body, part, count), in_specs=[IN_SM...  15 us
    pallas_call x8, Pallas kernels, forward_call(): pl.pallas_call(forward_body, in_specs=[IN_VMEM] * 3, out_specs=[IN_VMEM]...  9.23 us
    unnamed x22, local copies, waits for them, and re-layouts  6.19 us
    pallas_call x3, Pallas kernels, final_call(): pl.pallas_call(functools.partial(final_body, part, count), in_specs=specs...  3.08 us
    pallas_call x3, Pallas kernels, head_call(): pl.pallas_call(functools.partial(head_body, part, count), in_specs=[IN_SM...  3.05 us
    pallas_call x1, Pallas kernels, main_call(): pl.pallas_call(main_body, in_specs=[IN_VMEM] * 5, out_specs=[IN_VMEM] * 2...  2.74 us
  transfers between devices with their start and end apart: 15, of which 5 were waited for; matrix products, arithmetic and copies ran while one was open for 0% of the time, Pallas kernels for 34%

commit v1 on v0

--- a/solution.py
+++ b/solution.py
@@ -135,6 +135,12 @@
     return forward, forward.T / half
 
 
+def turning(rows, lanes):
+    angle = 2.0 * np.pi * (np.arange(rows // 2) + 0.5) / (2 * rows)
+    both = np.concatenate([np.cos(angle), -np.sin(angle)]).astype(np.float32)
+    return np.repeat(both[:, None], lanes, 1)
+
+
 def widening(groups, lanes):
     one = np.kron(np.eye(groups), np.ones((1, lanes // groups)))
     return np.kron(np.eye(2), one).astype(jnp.bfloat16)
@@ -183,6 +189,7 @@
 IN_VMEM = pl.BlockSpec(memory_space=pltpu.VMEM)
 IN_SMEM = pl.BlockSpec(memory_space=pltpu.SMEM)
 IN_ANY = pl.BlockSpec(memory_space=pl.ANY)
+IN_HBM = pl.BlockSpec(memory_space=pltpu.HBM)
 
 
 def kernel_params(mib):
@@ -197,45 +204,98 @@
     return pl.ds(pl.multiple_of(slab * LANES, LANES), LANES)
 
 
-def main_body(value, gate, taps, fwd, inv, gated, spec_out):
+def tail_body(value, out, sem):
+    count = out.shape[0]
+    copy = pltpu.make_async_copy(value.at[value.shape[0] - count :], out, sem)
+    copy.start()
+    copy.wait()
+
+
+def tail_call(value, count):
+    return pl.pallas_call(
+        tail_body,
+        in_specs=[IN_HBM],
+        out_specs=IN_VMEM,
+        out_shape=jax.ShapeDtypeStruct((count, value.shape[1]), value.dtype),
+        scratch_shapes=[pltpu.SemaphoreType.DMA],
+        compiler_params=kernel_params(4),
+        cost_estimate=pl.CostEstimate(flops=10_000_000_000, bytes_accessed=1000, transcendentals=0),
+        name="tail",
+    )(value)
+
+
+def main_body(value, gate, taps, fwd, inv, gated, spec_out, *scratch):
+    tops, held, fwd_held, inv_held = scratch[:2], scratch[2:5], scratch[5], scratch[6]
+    sems = scratch[7]
     count = taps.shape[0]
     wide = 2 * LANES
-    for c in range(0, value.shape[1], wide):
-        cols = slice(c, c + wide)
-        taps_spec = dot3(fwd[:, :, :count], taps[:, cols])
+    chunks = [slice(c, c + wide) for c in range(0, value.shape[1], wide)]
+    tables_in = [
+        pltpu.make_async_copy(fwd, fwd_held, sems.at[0, 0]),
+        pltpu.make_async_copy(inv, inv_held, sems.at[0, 1]),
+    ]
+    pieces = [
+        [
+            pltpu.make_async_copy(src.at[:, cols], dst.at[:, cols], sems.at[1 + at, k])
+            for k, (src, dst) in enumerate(zip((taps, value, gate), held))
+        ]
+        for at, cols in enumerate(chunks)
+    ]
+    for copy in sum(pieces[:1], tables_in) + sum(pieces[1:], []):
+        copy.start()
+    for copy in tables_in:
+        copy.wait()
+    for at, cols in enumerate(chunks):
+        for copy in pieces[at]:
+            copy.wait()
+        taps_spec = dot3(fwd_held[:, :, :count], held[0][:, cols])
         spec_out[:, cols] = taps_spec
-        short = short_rows(value[:, cols], taps_spec, fwd, inv)
-        gated[:, cols] = gate[count:, cols].astype(jnp.float32) * short
+        short = short_rows(held[1][:, cols], taps_spec, fwd_held, inv_held)
+        gated[:, cols] = held[2][count:, cols].astype(jnp.float32) * short
+        for top, whole in zip(tops, held[1:]):
+            top[:, cols] = whole[:count, cols]
 
 
 def main_call(value, gate, taps, fwd, inv):
     rows, chans = value.shape
     count = taps.shape[0]
+    top = jax.ShapeDtypeStruct((count, chans), jnp.bfloat16)
     return pl.pallas_call(
         main_body,
-        in_specs=[IN_VMEM] * 5,
-        out_specs=[IN_VMEM] * 2,
+        in_specs=[IN_HBM] * 5,
+        out_specs=[IN_VMEM] * 4,
         out_shape=[
             jax.ShapeDtypeStruct((rows - count, chans), jnp.float32),
             jax.ShapeDtypeStruct((2 * count, chans), jnp.float32),
+            top,
+            top,
         ],
-        compiler_params=kernel_params(12),
+        scratch_shapes=[
+            pltpu.VMEM(taps.shape, taps.dtype),
+            pltpu.VMEM(value.shape, value.dtype),
+            pltpu.VMEM(gate.shape, gate.dtype),
+            pltpu.VMEM(fwd.shape, fwd.dtype),
+            pltpu.VMEM(inv.shape, inv.dtype),
+            pltpu.SemaphoreType.DMA((1 + chans // (2 * LANES), 3)),
+        ],
+        compiler_params=kernel_params(16),
         cost_estimate=cost(4),
         name="short_main",
     )(value, gate, taps, fwd, inv)
 
 
-def head_body(part, count, me, halo, value, gate, gated, taps_spec, long_taps, fwd, inv, *outs):
+def head_body(part, count, me, halo, value, gate, gated, taps_spec, long_taps, fwd, inv, *rest):
     taps = halo.shape[0]
     rows = taps + gated.shape[0]
     groups = 8
+    outs = rest[-2 * len(part) :]
     tops, codes = outs[: len(part)], outs[len(part) :]
     for d, top, code in zip(part, tops, codes):
         slab = lax.rem(me[0] + d, count)
         cols = lanes_of(slab)
-        ext = jnp.concatenate([halo[:, cols], value[:taps, cols]], 0)
+        ext = jnp.concatenate([halo[:, cols], value[:, cols]], 0)
         short = short_rows(ext, taps_spec[:, cols], fwd, inv)
-        first = gate[:taps, cols].astype(jnp.float32) * short
+        first = gate[:, cols].astype(jnp.float32) * short
         top[...] = first
         later = gated[:, cols]
         peak = jnp.maximum(
@@ -258,7 +318,7 @@
         code[rows + TILE :] = to_code(held, jnp.concatenate([filter_scale] * many, 0))
 
 
-def head_call(part, count, me, halo, value, gate, gated, taps_spec, long_taps, fwd, inv):
+def head_call(part, count, me, halo, value, gate, gated, taps_spec, long_taps, fwd, inv, after):
     taps = halo.shape[0]
     rows = taps + gated.shape[0]
     held = long_taps.shape[1]
@@ -266,48 +326,70 @@
     top = jax.ShapeDtypeStruct((taps, LANES), jnp.float32)
     return pl.pallas_call(
         functools.partial(head_body, part, count),
-        in_specs=[IN_SMEM] + [IN_VMEM] * 8,
+        in_specs=[IN_SMEM] + [IN_VMEM] * 8 + [IN_ANY] * len(after),
         out_specs=[IN_VMEM] * (2 * len(part)),
         out_shape=[top] * len(part) + [code] * len(part),
         compiler_params=kernel_params(12),
         cost_estimate=cost(len(part)),
         name="short_head",
-    )(me, halo, value, gate, gated, taps_spec, long_taps, fwd, inv)
-
-
-def forward_body(code, fwd, widen, spec_out, filter_out):
-    rows = fwd.shape[2]
+    )(me, halo, value, gate, gated, taps_spec, long_taps, fwd, inv, *after)
+
+
+def forward_body(code, fwd, turn, widen, *rest):
+    spec_out, filter_out, held_x, held_h = rest[-4:]
+    rows = held_x.shape[0]
+    half = rows // 2
     groups = 8
-    x_high, x_low = split(from_code(code[:rows], code[rows : rows + 1].astype(jnp.float32)))
+    held_x[...] = from_code(code[:rows], code[rows : rows + 1].astype(jnp.float32))
     scale = code[rows : rows + TILE].astype(jnp.float32)[groups:]
-    held = code[rows + TILE :]
-    many = held.shape[0] // groups
-    h_high, h_low = split(from_code(held, jnp.concatenate([scale] * many, 0)))
+    taps = code[rows + TILE :]
+    many = taps.shape[0] // groups
+    h_high, h_low = split(from_code(taps, jnp.concatenate([scale] * many, 0)))
     h_high, h_low = h_high.astype(jnp.float32), h_low.astype(jnp.float32)
-    parts = []
-    for c in range(0, held.shape[0], groups):
-        pair = jnp.concatenate([h_high[c : c + groups], h_low[c : c + groups]], 0)
-        parts.append(dot(pair.T.astype(jnp.bfloat16), widen[...]).astype(jnp.bfloat16))
-    taps = jnp.concatenate(parts, 0)
-    x_wide = dot(fwd[0], jnp.concatenate([x_high, x_low], 1))
-    h_wide = dot(fwd[0], taps)
-    low = dot(fwd[1], jnp.concatenate([x_high, taps[:, :LANES]], 1))
-    spec_out[...] = x_wide[:, :LANES] + x_wide[:, LANES:] + low[:, :LANES]
-    filter_out[...] = h_wide[:, :LANES] + h_wide[:, LANES:] + low[:, LANES:]
-
-
-def forward_call(code, fwd, widen):
-    bins = fwd.shape[1]
-    spec = jax.ShapeDtypeStruct((bins, LANES), jnp.float32)
+    for c in range(many):
+        at = slice(c * groups, (c + 1) * groups)
+        pair = jnp.concatenate([h_high[at], h_low[at]], 0).T.astype(jnp.bfloat16)
+        wide = dot(pair, widen[...])
+        for k in range(2):
+            held_h[k, c * LANES : (c + 1) * LANES] = wide[:, k * LANES : (k + 1) * LANES]
+    highs, lows = [], []
+    for odd in range(2):
+        step = pl.ds(odd, half, stride=2)
+        high, low = split(held_x[step])
+        highs += [high, held_h[0, step].astype(jnp.bfloat16)]
+        lows += [low, held_h[1, step].astype(jnp.bfloat16)]
+    width = 4 * LANES
+    both = dot(fwd[0], jnp.concatenate(highs + lows, 1))
+    both = both[:, :width] + both[:, width:] + dot(fwd[1], jnp.concatenate(highs, 1))
+    w_re, w_im = turn[:half], turn[half:]
+    for at, out in enumerate((spec_out, filter_out)):
+        even = both[:, at * LANES : (at + 1) * LANES]
+        odd = both[:, (2 + at) * LANES : (3 + at) * LANES]
+        o_re, o_im = odd[:half], odd[half:]
+        t_re = o_re * w_re - o_im * w_im
+        t_im = o_re * w_im + o_im * w_re
+        out[:half] = even[:half] + t_re
+        out[half:rows] = even[:half] - t_re
+        out[rows : rows + half] = even[half:] + t_im
+        out[rows + half :] = even[half:] - t_im
+
+
+def forward_call(code, fwd, turn, widen, early, after):
+    rows = 2 * fwd.shape[2]
+    spec = jax.ShapeDtypeStruct((2 * rows, LANES), jnp.float32)
     return pl.pallas_call(
         forward_body,
-        in_specs=[IN_VMEM] * 3,
+        in_specs=[IN_VMEM] * (4 + len(early)) + [IN_ANY] * len(after),
         out_specs=[IN_VMEM] * 2,
         out_shape=[spec, spec],
+        scratch_shapes=[
+            pltpu.VMEM((rows, LANES), jnp.float32),
+            pltpu.VMEM((2, rows, LANES), jnp.float32),
+        ],
         compiler_params=kernel_params(12),
         cost_estimate=cost(1),
         name="forward",
-    )(code, fwd, widen)
+    )(code, fwd, turn, widen, *early, *after)
 
 
 def by_lag_body(me_ref, *refs):
@@ -348,10 +430,10 @@
     )(me, *spectra)
 
 
-def back_body(part, count, me_ref, filt, inv, *refs):
-    specs, codes, total = refs[:count], refs[-1 - len(part) : -1], refs[-1]
-    half = filt.shape[1] // 2
-    rows = inv.shape[1]
+def back_body(part, count, me_ref, filt, inv, turn, *refs):
+    specs, codes, total, held = refs[:count], refs[-2 - len(part) : -2], refs[-2], refs[-1]
+    rows = held.shape[0]
+    half = rows // 2
     me = me_ref[0]
 
     for e, code in zip(part, codes):
@@ -362,40 +444,57 @@
             lags.append(jnp.where(lag >= 0, lag, count))
 
         def chunk(c, _):
-            re = pl.ds(pl.multiple_of(c * 8, 8), 8)
-            im = pl.ds(pl.multiple_of(half + c * 8, 8), 8)
-            acc_re = jnp.zeros((8, LANES), jnp.float32)
-            acc_im = acc_re
-            for d in range(count):
-                x_re, x_im = specs[d][re], specs[d][im]
-                g_re, g_im = filt[lags[d], re], filt[lags[d], im]
-                acc_re += x_re * g_re - x_im * g_im
-                acc_im += x_re * g_im + x_im * g_re
-            total[re] = acc_re
-            total[im] = acc_im
+            def piece(start):
+                return pl.ds(pl.multiple_of(start + c * 8, 8), 8)
+
+            sums = []
+            for start in (0, half):
+                re, im = piece(start), piece(rows + start)
+                acc_re = jnp.zeros((8, LANES), jnp.float32)
+                acc_im = acc_re
+                for d in range(count):
+                    x_re, x_im = specs[d][re], specs[d][im]
+                    g_re, g_im = filt[lags[d], re], filt[lags[d], im]
+                    acc_re += x_re * g_re - x_im * g_im
+                    acc_im += x_re * g_im + x_im * g_re
+                sums += [acc_re, acc_im]
+            a_re, a_im, b_re, b_im = sums
+            re, im = piece(0), piece(half)
+            w_re, w_im = turn[re], turn[im]
+            d_re, d_im = a_re - b_re, a_im - b_im
+            total[re, :LANES] = a_re + b_re
+            total[im, :LANES] = a_im + b_im
+            total[re, LANES:] = d_re * w_re + d_im * w_im
+            total[im, LANES:] = d_im * w_re - d_re * w_im
             return 0
 
         lax.fori_loop(0, half // 8, chunk, 0, unroll=2)
         values = dot3(inv, total[...])
-        scale = scale_of(jnp.max(jnp.abs(values), axis=0, keepdims=True))
-        code[:rows] = to_code(values, scale)
+        held[pl.ds(0, half, stride=2)] = values[:, :LANES]
+        held[pl.ds(1, half, stride=2)] = values[:, LANES:]
+        peak = jnp.max(jnp.abs(values), axis=0, keepdims=True)
+        scale = scale_of(jnp.maximum(peak[:, :LANES], peak[:, LANES:]))
+        code[:rows] = to_code(held[...], scale)
         code[rows:] = jnp.broadcast_to(scale, (TILE, LANES)).astype(jnp.bfloat16)
 
 
-def back_call(part, me, filt, inv, specs, after):
+def back_call(part, me, filt, inv, turn, specs, after):
     count = len(specs)
     bins = specs[0].shape[0]
     code = jax.ShapeDtypeStruct((bins // 2 + TILE, LANES), jnp.bfloat16)
     return pl.pallas_call(
         functools.partial(back_body, part, count),
-        in_specs=[IN_SMEM] + [IN_VMEM] * (2 + count) + [IN_ANY] * len(after),
+        in_specs=[IN_SMEM] + [IN_VMEM] * (3 + count) + [IN_ANY] * len(after),
         out_specs=[IN_VMEM] * len(part),
         out_shape=[code] * len(part),
-        scratch_shapes=[pltpu.VMEM((bins, LANES), jnp.float32)],
+        scratch_shapes=[
+            pltpu.VMEM((bins // 2, 2 * LANES), jnp.float32),
+            pltpu.VMEM((bins // 2, LANES), jnp.float32),
+        ],
         compiler_params=kernel_params(12),
         cost_estimate=cost(len(part)),
         name="back",
-    )(me, filt, inv, *specs, *after)
+    )(me, filt, inv, turn, *specs, *after)
 
 
 def final_body(part, count, me, *refs):
@@ -418,16 +517,16 @@
         copy.wait()
 
 
-def final_call(part, count, me, codes, tops, gated, gate, skip, so_far):
+def final_call(part, count, me, codes, tops, gated, gate, skip, so_far, after):
     rows = gate.shape[0]
     many = len(part)
     args = [me, *codes, *tops, gated, gate, skip]
     specs = [IN_SMEM] + [IN_VMEM] * (2 * many + 3)
     alias = {}
-    if so_far is not None:
+    if so_far:
         alias = {len(args): 0}
-        args.append(so_far)
-        specs.append(IN_ANY)
+    args += so_far + after
+    specs += [IN_ANY] * len(so_far + after)
     return pl.pallas_call(
         functools.partial(final_body, part, count),
         in_specs=specs,
@@ -462,47 +561,79 @@
     def table(values):
         return jnp.asarray(split_table(values))
 
-    halo = passed_along(value_input[rows - taps :], "ctx", 1)
+    halo = passed_along(tail_call(value_input, taps), "ctx", 1)
     long_taps = long_filter.T.reshape(count, groups, rows // LANES, LANES)
     long_taps = jnp.swapaxes(long_taps, 1, 2).reshape(count, -1, LANES)
 
     forward, inverse = tables(taps)
     short_fwd, short_inv = table(forward), table(inverse[taps:])
-    forward, inverse = tables(rows)
-    fwd, inv = table(forward[:, :rows]), table(inverse[:rows])
+    half = rows // 2
+    forward, inverse = tables(half)
+    fwd, inv = table(forward[:, :half]), table(inverse[:half] / 2)
+    turn = jnp.asarray(turning(rows, LANES))
     widen = jnp.asarray(widening(groups, LANES))
 
-    gated, taps_spec = main_call(value_input, input_gate, short_filter, short_fwd, short_inv)
-    came, tops = {}, {}
-    for part in (order[:1], order[1:3], order[3:]):
+    gated, taps_spec, value_top, gate_top = main_call(
+        value_input, input_gate, short_filter, short_fwd, short_inv
+    )
+    came, tops, codes, specs, spectra = {}, {}, {}, {}, {}
+    after = []
+
+    def heads(*part):
         outs = head_call(
-            part, count, me, halo, value_input, input_gate, gated, taps_spec, long_taps,
-            short_fwd, short_inv,
+            part, count, me, halo, value_top, gate_top, gated, taps_spec, long_taps,
+            short_fwd, short_inv, after,
         )
+        after[:] = outs[:1]
         for d, top, code in zip(part, outs, outs[len(part) :]):
             tops[d] = top
             came[d] = rotated(code, d) if d else code
 
-    specs, spectra = [None] * count, [None] * count
-    for d in order[-1:] + order[:-1]:
-        specs[d], spectra[d] = forward_call(came[d], fwd, widen)
-    filt = by_lag_call(me, spectra)
+    def forwards(d, early=()):
+        specs[d], spectra[d] = forward_call(came[d], fwd, turn, widen, early, after)
+        after[:] = [specs[d]]
+
+    heads(order[0])
+    heads(*order[1:3])
+    heads(*order[3:5], 0)
+    forwards(0, [inv])
+    forwards(order[0])
+    heads(order[5])
+    forwards(order[1])
+    heads(order[6])
+    for d in order[2:7]:
+        forwards(d)
+    specs = [specs[d] for d in range(count)]
+    filt = by_lag_call(me, [spectra[d] for d in range(count)])
 
     answers, after = {}, []
-    for part in (order[:1], order[1:3], order[3:]):
-        codes = back_call(part, me, filt, inv, specs, after)
-        for e, code in zip(part, codes):
-            answers[e] = rotated(code, e) if e else code
-        after = codes[:1]
-
-    mixed = None
-    for part in (order[-1:] + order[:3], order[3:6], order[6:-1]):
+    mixed = []
+
+    def backs(e):
+        (code,) = back_call([e], me, filt, inv, turn, specs, after)
+        answers[e] = rotated(code, e) if e else code
+        after[:] = [code]
+
+    def finals(*part):
         owners = [(count - e) % count for e in part]
-        mixed = final_call(
-            owners, count, me, [answers[e] for e in part], [tops[d] for d in owners], gated,
-            output_gate, skip_gain[None], mixed,
-        )
-    return mixed
+        mixed[:] = [
+            final_call(
+                owners, count, me, [answers[e] for e in part], [tops[d] for d in owners],
+                gated, output_gate, skip_gain[None], mixed, after,
+            )
+        ]
+        after[:] = mixed
+
+    for e in order[:5]:
+        backs(e)
+    backs(0)
+    finals(0, order[0])
+    backs(order[5])
+    finals(order[1])
+    backs(order[6])
+    for e in order[2:7]:
+        finals(e)
+    return mixed[0]
 
 
 def local(output_gate, input_gate, value_input, short_filter, long_filter, skip_gain):

time: 80.5 us -> 74.1 us (0.920)
  starting transfers between devices: 22.5 us -> 33.2 us
  waiting for transfers between devices: 16.1 us -> 5.9 us
  local copies, waits for them, and re-layouts: 7.19 us -> 2.53 us
  Pallas kernels: 33.8 us -> 31.6 us
    ppermute x14, starting transfers between devices: 20.2 us -> 30.7 us  [rotated(): lax.ppermute(block, 'ctx', [(i, (i + distance) % count) for i in range(co...]
    ppermute x14, waiting for transfers between devices: 16.1 us -> 5.89 us  [rotated(): lax.ppermute(block, 'ctx', [(i, (i + distance) % count) for i in range(co...]
    unnamed x22 -> x30, local copies, waits for them, and re-layouts: 6.19 us -> 2.53 us
    pallas_call x3 -> x8, Pallas kernels: 15 us -> 12.9 us  [back_call(): pl.pallas_call(functools.partial(back_body, part, count), in_specs=[IN_SM...]
    slice x1 -> x0, local copies, waits for them, and re-layouts: 1 us -> none  [in_slabs(): halo = passed_along(value_input[rows - taps:], 'ctx', 1)]
    pallas_call x3 -> x7, Pallas kernels: 3.08 us -> 2.41 us  [final_call(): pl.pallas_call(functools.partial(final_body, part, count), in_specs=specs...]
    pallas_call x3 -> x5, Pallas kernels: 3.05 us -> 3.39 us  [head_call(): pl.pallas_call(functools.partial(head_body, part, count), in_specs=[IN_SM...]
    pallas_call x9 -> x10, Pallas kernels: 12 us -> 12.1 us  [the longest x8 7.22 us: forward_call(): pl.pallas_call(forward_body, in_specs=[IN_VMEM] * (4 + len(early)) + [IN_...]
  transfers between devices with their start and end apart: 15 -> 15, of which waited for: 5 -> 3; matrix products, arithmetic and copies ran while one was open for 0% -> 2% of each run, Pallas kernels for 34% -> 36%
where the time goes in v1:
time: 74.1 us; the launch traced here: 73.9 us
  starting transfers between devices  33.2 us (45%)
  Pallas kernels  31.6 us (43%)
  waiting for transfers between devices  5.9 us (8%)
  local copies, waits for them, and re-layouts  2.53 us (3%)
    ppermute x14, starting transfers between devices, rotated(): lax.ppermute(block, 'ctx', [(i, (i + distance) % count) for i in range(co...  30.7 us
    pallas_call x8, Pallas kernels, back_call(): pl.pallas_call(functools.partial(back_body, part, count), in_specs=[IN_SM...  12.9 us
    pallas_call x8, Pallas kernels, forward_call(): pl.pallas_call(forward_body, in_specs=[IN_VMEM] * (4 + len(early)) + [IN_...  7.22 us
    ppermute x14, waiting for transfers between devices, rotated(): lax.ppermute(block, 'ctx', [(i, (i + distance) % count) for i in range(co...  5.89 us
    pallas_call x1, Pallas kernels, main_call(): pl.pallas_call(main_body, in_specs=[IN_HBM] * 5, out_specs=[IN_VMEM] * 4,...  4.16 us
    pallas_call x5, Pallas kernels, head_call(): pl.pallas_call(functools.partial(head_body, part, count), in_specs=[IN_SM...  3.39 us
    unnamed x30, local copies, waits for them, and re-layouts  2.53 us
    ppermute x1, starting transfers between devices, passed_along(): return lax.ppermute(block, axis, route)  2.51 us
  transfers between devices with their start and end apart: 15, of which 3 were waited for; matrix products, arithmetic and copies ran while one was open for 2% of the time, Pallas kernels for 36%

profile of v1, /device:TPU:0, one launch (start us, length us, event | category | flops | bytes accessed | tf_op | source)
XLA Modules:
  0.0 73.9 jit_solution(58459311023398621)
XLA Ops:
  0.0 1.3 %copy-done.7 = bf16[512,1024]{1,0:T(8,128)(2,1)S(1)} copy-done((bf16[512,1024]{1,0:T(8,128)(2,1)S(1)}, bf16[512,1024]{1,0:T(8,128)(2,1)}, u32[]{:S(2)}) %copy-start.7) | copy-done | bytes 1048600
  1.3 0.7 tail.1
  2.0 2.5 %collective-permute-start = (bf16[128,1024]{1,0:T(8,128)(2,1)}, bf16[128,1024]{1,0:T(8,128)(2,1)S(1)}, u32[]{:S(2)}, u32[]{:S(2)}) collective-permute-start(bf16[128,1024]{1,0:T(8,128)(2,1)} %tail.1), channel_id=1, source_target_pairs={{0,4},{4,8},{8,12},{12,16},{16,20},{20,24},{24,28},{1,5},{5,9},{9,... | collective-permute-start | bytes 786440 | tf_op jit(solution)/shard_map/ppermute | solution.py:24
  4.6 4.2 %short_main.1 = (f32[384,1024]{1,0:T(8,128)S(1)}, f32[256,1024]{1,0:T(8,128)S(1)}, bf16[128,1024]{1,0:T(8,128)(2,1)S(1)}, bf16[128,1024]{1,0:T(8,128)(2,1)S(1)}) custom-call(bf16[512,1024]{1,0:T(8,128)(2,1)S(1)} %copy-done.8, bf16[512,1024]{1,0:T(8,128)(2,1)S(1)} %copy-done.9, f32[128,1024]{1,0:T(8,128)S(1)} %copy-done.11, ...), custom_call_target="tpu_custom_call" | custom-call | flops 4000000 | bytes 4000 | tf_op jit(solution)/shard_map/short_main/pallas_call | solution.py:263
  8.8 0.5 short_head.5
  9.3 0.0 copy-start
  9.3 0.0 copy-start.2
  9.3 0.0 copy-start.3
  9.3 0.0 copy-start.10
  9.3 5.4 %collective-permute-start.1 = (bf16[560,128]{1,0:T(8,128)(2,1)S(1)}, bf16[560,128]{1,0:T(8,128)(2,1)S(1)}, u32[]{:S(2)}, u32[]{:S(2)}) collective-permute-start(bf16[560,128]{1,0:T(8,128)(2,1)S(1)} %get-tuple-element.50), channel_id=1, source_target_pairs={{0,16},{4,20},{8,24},{12,28},{16,0},{20,4},{24,8},{28,12},{1,17},{... | collective-permute-start | bytes 430088 | tf_op jit(solution)/shard_map/ppermute | solution.py:559
  14.7 0.8 %short_head.6 = (f32[128,128]{1,0:T(8,128)S(1)}, f32[128,128]{1,0:T(8,128)S(1)}, bf16[560,128]{1,0:T(8,128)(2,1)S(1)}, bf16[560,128]{1,0:T(8,128)(2,1)S(1)}) custom-call(s32[1]{0:T(128)} %bitcast.me.me_ref, bf16[128,1024]{1,0:T(8,128)(2,1)S(1)} %collective-permute-done.halo, bf16[128,1024]{1,0:T(8,128)(2,1)S(1)} %get-tuple-element.41.value, ...), custom_call_target="tpu_custom_call" | custom-call | flops 2000000 | bytes 2000 | tf_op jit(solution)/shard_map/short_head/pallas_call | solution.py:327
  15.5 0.1 collective-permute-start.6
  15.6 2.6 %collective-permute-start.5 = (bf16[560,128]{1,0:T(8,128)(2,1)S(1)}, bf16[560,128]{1,0:T(8,128)(2,1)S(1)}, u32[]{:S(2)}, u32[]{:S(2)}) collective-permute-start(bf16[560,128]{1,0:T(8,128)(2,1)S(1)} %get-tuple-element.56), channel_id=1, source_target_pairs={{0,20},{4,24},{8,28},{12,0},{16,4},{20,8},{24,12},{28,16},{1,21},{... | collective-permute-start | bytes 430088 | tf_op jit(solution)/shard_map/ppermute | solution.py:559
  18.2 1.1 %short_head.7 = (f32[128,128]{1,0:T(8,128)S(1)}, f32[128,128]{1,0:T(8,128)S(1)}, f32[128,128]{1,0:T(8,128)S(1)}, bf16[560,128]{1,0:T(8,128)(2,1)S(1)}, bf16[560,...) custom-call(s32[1]{0:T(128)} %bitcast.me.me_ref, bf16[128,1024]{1,0:T(8,128)(2,1)S(1)} %collective-permute-done.halo, ...), custom_call_target="tpu_custom_call" | custom-call | flops 3000000 | bytes 3000 | tf_op jit(solution)/shard_map/short_head/pallas_call | solution.py:327
  19.3 1.4 %collective-permute-start.3 = (bf16[560,128]{1,0:T(8,128)(2,1)S(1)}, bf16[560,128]{1,0:T(8,128)(2,1)S(1)}, u32[]{:S(2)}, u32[]{:S(2)}) collective-permute-start(bf16[560,128]{1,0:T(8,128)(2,1)S(1)} %get-tuple-element.54), channel_id=1, source_target_pairs={{0,24},{4,28},{8,0},{12,4},{16,8},{20,12},{24,16},{28,20},{1,25},{... | collective-permute-start | bytes 430088 | tf_op jit(solution)/shard_map/ppermute | solution.py:559
  20.8 0.7 collective-permute-start.4
  21.4 0.9 %forward.8 = (f32[1024,128]{1,0:T(8,128)S(1)}, f32[1024,128]{1,0:T(8,128)S(1)}) custom-call(bf16[560,128]{1,0:T(8,128)(2,1)S(1)} %get-tuple-element.47.code, bf16[2,512,256]{2,1,0:T(8,128)(2,1)S(1)} %copy-done.3, f32[512,128]{1,0:T(8,128)S(1)} %copy-done, bf16[16,256]{1,0:T(8,128)(2,1)S(1)} %copy-done.10, bf16[2,256,512]{2,1,0:T(8,128)(2,1)S(1)} %copy-done.2, ...), custom_call_target="tpu_custom_call" | custom-call | flops 1000000 | bytes 1000 | tf_op jit(solution)/shard_map/forward/pallas_call | solution.py:380
  22.3 4.7 %collective-permute-done.1.code = bf16[560,128]{1,0:T(8,128)(2,1)S(1)} collective-permute-done((bf16[560,128]{1,0:T(8,128)(2,1)S(1)}, bf16[560,128]{1,0:T(8,128)(2,1)S(1)}, u32[]{:S(2)}, u32[]{:S(2)}) %collective-permute-start.1) | collective-permute-done | bytes 143392 | tf_op jit(solution)/shard_map/ppermute | solution.py:559
  27.1 0.9 %forward.9 = (f32[1024,128]{1,0:T(8,128)S(1)}, f32[1024,128]{1,0:T(8,128)S(1)}) custom-call(bf16[560,128]{1,0:T(8,128)(2,1)S(1)} %collective-permute-done.1.code, bf16[2,512,256]{2,1,0:T(8,128)(2,1)S(1)} %copy-done.3, f32[512,128]{1,0:T(8,128)S(1)} %copy-done, bf16[16,256]{1,0:T(8,128)(2,1)S(1)} %copy-done.10, f32[1024,128]{1,0:T(8,128)S(1)} %get-tuple-element.51.rest_0_.refs_0_), custom_call_target="tpu_custom_call" | custom-call | flops 1000000 | bytes 1000 | tf_op jit(solution)/shard_map/forward/pallas_call | solution.py:380
  28.0 0.5 short_head.8
  28.5 0.1 collective-permute-start.2
  28.5 0.3 collective-permute-done.6.code
  28.9 0.9 %forward.10 = (f32[1024,128]{1,0:T(8,128)S(1)}, f32[1024,128]{1,0:T(8,128)S(1)}) custom-call(bf16[560,128]{1,0:T(8,128)(2,1)S(1)} %collective-permute-done.6.code, bf16[2,512,256]{2,1,0:T(8,128)(2,1)S(1)} %copy-done.3, f32[512,128]{1,0:T(8,128)S(1)} %copy-done, bf16[16,256]{1,0:T(8,128)(2,1)S(1)} %copy-done.10, f32[128,128]{1,0:T(8,128)S(1)} %get-tuple-element.58.rest_0_.refs_1_), custom_call_target="tpu_custom_call" | custom-call | flops 1000000 | bytes 1000 | tf_op jit(solution)/shard_map/forward/pallas_call | solution.py:380
  29.8 0.5 short_head.9
  30.3 3.3 %collective-permute-start.7 = (bf16[560,128]{1,0:T(8,128)(2,1)S(1)}, bf16[560,128]{1,0:T(8,128)(2,1)S(1)}, u32[]{:S(2)}, u32[]{:S(2)}) collective-permute-start(bf16[560,128]{1,0:T(8,128)(2,1)S(1)} %get-tuple-element.70), channel_id=1, source_target_pairs={{0,28},{4,0},{8,4},{12,8},{16,12},{20,16},{24,20},{28,24},{1,29},{... | collective-permute-start | bytes 430088 | tf_op jit(solution)/shard_map/ppermute | solution.py:559
  33.5 0.0 collective-permute-done.5.code
  33.5 0.9 %forward.11 = (f32[1024,128]{1,0:T(8,128)S(1)}, f32[1024,128]{1,0:T(8,128)S(1)}) custom-call(bf16[560,128]{1,0:T(8,128)(2,1)S(1)} %collective-permute-done.5.code, bf16[2,512,256]{2,1,0:T(8,128)(2,1)S(1)} %copy-done.3, f32[512,128]{1,0:T(8,128)S(1)} %copy-done, bf16[16,256]{1,0:T(8,128)(2,1)S(1)} %copy-done.10, f32[128,128]{1,0:T(8,128)S(1)} %get-tuple-element.60.rest_0_.refs_1_), custom_call_target="tpu_custom_call" | custom-call | flops 1000000 | bytes 1000 | tf_op jit(solution)/shard_map/forward/pallas_call | solution.py:380
  34.4 0.0 collective-permute-done.4.code
  34.5 0.9 %forward.12 = (f32[1024,128]{1,0:T(8,128)S(1)}, f32[1024,128]{1,0:T(8,128)S(1)}) custom-call(bf16[560,128]{1,0:T(8,128)(2,1)S(1)} %collective-permute-done.4.code, bf16[2,512,256]{2,1,0:T(8,128)(2,1)S(1)} %copy-done.3, f32[512,128]{1,0:T(8,128)S(1)} %copy-done, bf16[16,256]{1,0:T(8,128)(2,1)S(1)} %copy-done.10, f32[1024,128]{1,0:T(8,128)S(1)} %get-tuple-element.61.rest_0_.refs_5_), custom_call_target="tpu_custom_call" | custom-call | flops 1000000 | bytes 1000 | tf_op jit(solution)/shard_map/forward/pallas_call | solution.py:380
  35.4 0.0 collective-permute-done.3.code
  35.4 0.9 %forward.13 = (f32[1024,128]{1,0:T(8,128)S(1)}, f32[1024,128]{1,0:T(8,128)S(1)}) custom-call(bf16[560,128]{1,0:T(8,128)(2,1)S(1)} %collective-permute-done.3.code, bf16[2,512,256]{2,1,0:T(8,128)(2,1)S(1)} %copy-done.3, f32[512,128]{1,0:T(8,128)S(1)} %copy-done, bf16[16,256]{1,0:T(8,128)(2,1)S(1)} %copy-done.10, f32[1024,128]{1,0:T(8,128)S(1)} %get-tuple-element.62.rest_0_.refs_2_), custom_call_target="tpu_custom_call" | custom-call | flops 1000000 | bytes 1000 | tf_op jit(solution)/shard_map/forward/pallas_call | solution.py:380
  36.3 0.9 %forward.14 = (f32[1024,128]{1,0:T(8,128)S(1)}, f32[1024,128]{1,0:T(8,128)S(1)}) custom-call(bf16[560,128]{1,0:T(8,128)(2,1)S(1)} %collective-permute-done.2.code, bf16[2,512,256]{2,1,0:T(8,128)(2,1)S(1)} %copy-done.3, f32[512,128]{1,0:T(8,128)S(1)} %copy-done, bf16[16,256]{1,0:T(8,128)(2,1)S(1)} %copy-done.10, f32[1024,128]{1,0:T(8,128)S(1)} %get-tuple-element.63.rest_0_.refs_6_), custom_call_target="tpu_custom_call" | custom-call | flops 1000000 | bytes 1000 | tf_op jit(solution)/shard_map/forward/pallas_call | solution.py:380
  37.2 0.0 collective-permute-done.7.code
  37.2 0.9 %forward.15 = (f32[1024,128]{1,0:T(8,128)S(1)}, f32[1024,128]{1,0:T(8,128)S(1)}) custom-call(bf16[560,128]{1,0:T(8,128)(2,1)S(1)} %collective-permute-done.7.code, bf16[2,512,256]{2,1,0:T(8,128)(2,1)S(1)} %copy-done.3, f32[512,128]{1,0:T(8,128)S(1)} %copy-done, bf16[16,256]{1,0:T(8,128)(2,1)S(1)} %copy-done.10, f32[1024,128]{1,0:T(8,128)S(1)} %get-tuple-element.71.rest_0_.refs_1_), custom_call_target="tpu_custom_call" | custom-call | flops 1000000 | bytes 1000 | tf_op jit(solution)/shard_map/forward/pallas_call | solution.py:380
  38.1 0.8 %by_lag.1.filt = f32[9,1024,128]{2,1,0:T(8,128)S(1)} custom-call(s32[1]{0:T(128)} %bitcast.me.me_ref, f32[1024,128]{1,0:T(8,128)S(1)} %get-tuple-element.49.refs_0_, f32[1024,128]{1,0:T(8,128)S(1)} %get-tuple-element.64.refs_1_, f32[1024,128]{1,0:T(8,128)S(1)} %get-tuple-element.65.refs_2_, f32[1024,128]{1,0:T(8,128)S(1)} %get-tuple-element.66.refs_3_, ...), custom_call_target="tpu_custom_call" | custom-call | flops 1000000 | bytes 1000 | tf_op jit(solution)/shard_map/by_lag/pallas_call | solution.py:422
  38.9 1.7 %back.8.refs_8_ = bf16[528,128]{1,0:T(8,128)(2,1)S(1)} custom-call(s32[1]{0:T(128)} %bitcast.me.me_ref, f32[9,1024,128]{2,1,0:T(8,128)S(1)} %by_lag.1.filt, bf16[2,256,512]{2,1,0:T(8,128)(2,1)S(1)} %copy-done.2, f32[512,128]{1,0:T(8,128)S(1)} %copy-done, f32[1024,128]{1,0:T(8,128)S(1)} %get-tuple-element.51.rest_0_.refs_0_, ...), custom_call_target="tpu_custom_call" | custom-call | flops 1000000 | bytes 1000 | tf_op jit(solution)/shard_map/back/pallas_call | solution.py:485
  40.6 6.9 %collective-permute-start.9 = (bf16[528,128]{1,0:T(8,128)(2,1)S(1)}, bf16[528,128]{1,0:T(8,128)(2,1)S(1)}, u32[]{:S(2)}, u32[]{:S(2)}) collective-permute-start(bf16[528,128]{1,0:T(8,128)(2,1)S(1)} %back.8.refs_8_), channel_id=1, source_target_pairs={{0,16},{4,20},{8,24},{12,28},{16,0},{20,4},{24,8},{28,12},{1,17},{... | collective-permute-start | bytes 405512 | tf_op jit(solution)/shard_map/ppermute | solution.py:559
  47.4 1.6 %back.9.refs_8_ = bf16[528,128]{1,0:T(8,128)(2,1)S(1)} custom-call(s32[1]{0:T(128)} %bitcast.me.me_ref, f32[9,1024,128]{2,1,0:T(8,128)S(1)} %by_lag.1.filt, bf16[2,256,512]{2,1,0:T(8,128)(2,1)S(1)} %copy-done.2, f32[512,128]{1,0:T(8,128)S(1)} %copy-done, f32[1024,128]{1,0:T(8,128)S(1)} %get-tuple-element.51.rest_0_.refs_0_, ...), custom_call_target="tpu_custom_call" | custom-call | flops 1000000 | bytes 1000 | tf_op jit(solution)/shard_map/back/pallas_call | solution.py:485
  49.0 0.2 collective-permute-start.8
  49.3 1.6 %back.10.refs_8_ = bf16[528,128]{1,0:T(8,128)(2,1)S(1)} custom-call(s32[1]{0:T(128)} %bitcast.me.me_ref, f32[9,1024,128]{2,1,0:T(8,128)S(1)} %by_lag.1.filt, bf16[2,256,512]{2,1,0:T(8,128)(2,1)S(1)} %copy-done.2, f32[512,128]{1,0:T(8,128)S(1)} %copy-done, f32[1024,128]{1,0:T(8,128)S(1)} %get-tuple-element.51.rest_0_.refs_0_, ...), custom_call_target="tpu_custom_call" | custom-call | flops 1000000 | bytes 1000 | tf_op jit(solution)/shard_map/back/pallas_call | solution.py:485
  50.9 2.6 %collective-permute-start.14 = (bf16[528,128]{1,0:T(8,128)(2,1)S(1)}, bf16[528,128]{1,0:T(8,128)(2,1)S(1)}, u32[]{:S(2)}, u32[]{:S(2)}) collective-permute-start(bf16[528,128]{1,0:T(8,128)(2,1)S(1)} %back.10.refs_8_), channel_id=1, source_target_pairs={{0,20},{4,24},{8,28},{12,0},{16,4},{20,8},{24,12},{28,16},{1,21},{... | collective-permute-start | bytes 405512 | tf_op jit(solution)/shard_map/ppermute | solution.py:559
  53.5 1.6 %back.11.refs_8_ = bf16[528,128]{1,0:T(8,128)(2,1)S(1)} custom-call(s32[1]{0:T(128)} %bitcast.me.me_ref, f32[9,1024,128]{2,1,0:T(8,128)S(1)} %by_lag.1.filt, bf16[2,256,512]{2,1,0:T(8,128)(2,1)S(1)} %copy-done.2, f32[512,128]{1,0:T(8,128)S(1)} %copy-done, f32[1024,128]{1,0:T(8,128)S(1)} %get-tuple-element.51.rest_0_.refs_0_, ...), custom_call_target="tpu_custom_call" | custom-call | flops 1000000 | bytes 1000 | tf_op jit(solution)/shard_map/back/pallas_call | solution.py:485
  55.2 0.1 collective-permute-start.13
  55.2 1.6 %back.12.refs_8_ = bf16[528,128]{1,0:T(8,128)(2,1)S(1)} custom-call(s32[1]{0:T(128)} %bitcast.me.me_ref, f32[9,1024,128]{2,1,0:T(8,128)S(1)} %by_lag.1.filt, bf16[2,256,512]{2,1,0:T(8,128)(2,1)S(1)} %copy-done.2, f32[512,128]{1,0:T(8,128)S(1)} %copy-done, f32[1024,128]{1,0:T(8,128)S(1)} %get-tuple-element.51.rest_0_.refs_0_, ...), custom_call_target="tpu_custom_call" | custom-call | flops 1000000 | bytes 1000 | tf_op jit(solution)/shard_map/back/pallas_call | solution.py:485
  56.9 0.0 copy-start.1
  56.9 0.0 copy-start.12
  56.9 3.8 %collective-permute-start.12 = (bf16[528,128]{1,0:T(8,128)(2,1)S(1)}, bf16[528,128]{1,0:T(8,128)(2,1)S(1)}, u32[]{:S(2)}, u32[]{:S(2)}) collective-permute-start(bf16[528,128]{1,0:T(8,128)(2,1)S(1)} %back.12.refs_8_), channel_id=1, source_target_pairs={{0,24},{4,28},{8,0},{12,4},{16,8},{20,12},{24,16},{28,20},{1,25},{... | collective-permute-start | bytes 405512 | tf_op jit(solution)/shard_map/ppermute | solution.py:559
  60.7 1.6 %back.13.refs_0_.refs_7_ = bf16[528,128]{1,0:T(8,128)(2,1)S(1)} custom-call(s32[1]{0:T(128)} %bitcast.me.me_ref, f32[9,1024,128]{2,1,0:T(8,128)S(1)} %by_lag.1.filt, bf16[2,256,512]{2,1,0:T(8,128)(2,1)S(1)} %copy-done.2, f32[512,128]{1,0:T(8,128)S(1)} %copy-done, f32[1024,128]{1,0:T(8,128)S(1)} %get-tuple-element.51.rest_0_.refs_0_, ...), custom_call_target="tpu_custom_call" | custom-call | flops 1000000 | bytes 1000 | tf_op jit(solution)/shard_map/back/pallas_call | solution.py:485
  62.4 0.5 final.7.refs_8_.refs_5_
  62.8 1.6 %back.14.refs_6_ = bf16[528,128]{1,0:T(8,128)(2,1)S(1)} custom-call(s32[1]{0:T(128)} %bitcast.me.me_ref, f32[9,1024,128]{2,1,0:T(8,128)S(1)} %by_lag.1.filt, bf16[2,256,512]{2,1,0:T(8,128)(2,1)S(1)} %copy-done.2, f32[512,128]{1,0:T(8,128)S(1)} %copy-done, f32[1024,128]{1,0:T(8,128)S(1)} %get-tuple-element.51.rest_0_.refs_0_, ...), custom_call_target="tpu_custom_call" | custom-call | flops 1000000 | bytes 1000 | tf_op jit(solution)/shard_map/back/pallas_call | solution.py:485
  64.4 0.1 collective-permute-start.11
  64.5 0.2 final.8.refs_8_.refs_5_
  64.8 1.6 %back.15.refs_6_ = bf16[528,128]{1,0:T(8,128)(2,1)S(1)} custom-call(s32[1]{0:T(128)} %bitcast.me.me_ref, f32[9,1024,128]{2,1,0:T(8,128)S(1)} %by_lag.1.filt, bf16[2,256,512]{2,1,0:T(8,128)(2,1)S(1)} %copy-done.2, f32[512,128]{1,0:T(8,128)S(1)} %copy-done, f32[1024,128]{1,0:T(8,128)S(1)} %get-tuple-element.51.rest_0_.refs_0_, ...), custom_call_target="tpu_custom_call" | custom-call | flops 1000000 | bytes 1000 | tf_op jit(solution)/shard_map/back/pallas_call | solution.py:485
  66.4 3.6 %collective-permute-start.10 = (bf16[528,128]{1,0:T(8,128)(2,1)S(1)}, bf16[528,128]{1,0:T(8,128)(2,1)S(1)}, u32[]{:S(2)}, u32[]{:S(2)}) collective-permute-start(bf16[528,128]{1,0:T(8,128)(2,1)S(1)} %back.15.refs_6_), channel_id=1, source_target_pairs={{0,28},{4,0},{8,4},{12,8},{16,12},{20,16},{24,20},{28,24},{1,29},{... | collective-permute-start | bytes 405512 | tf_op jit(solution)/shard_map/ppermute | solution.py:559
  70.0 0.2 final.9.refs_6_
  70.2 0.1 copy.21.refs_5_
  70.3 0.2 final.10.refs_6_
  70.5 0.1 copy.22.refs_5_
  70.6 0.2 final.11.refs_6_
  70.9 0.1 copy.23.refs_5_
  70.9 0.8 %collective-permute-done.11.refs_0_ = bf16[528,128]{1,0:T(8,128)(2,1)S(1)} collective-permute-done((bf16[528,128]{1,0:T(8,128)(2,1)S(1)}, bf16[528,128]{1,0:T(8,128)(2,1)S(1)}, u32[]{:S(2)}, u32[]{:S(2)}) %collective-permute-start.11) | collective-permute-done | bytes 135200 | tf_op jit(solution)/shard_map/ppermute | solution.py:559
  71.8 0.2 final.12.refs_6_
  72.0 1.0 %copy.24.refs_5_ = bf16[512,1024]{1,0:T(8,128)(2,1)} copy(bf16[512,1024]{1,0:T(8,128)(2,1)S(1)} %final.12.refs_6_) | data formatting | bytes 2097152
  73.0 0.8 %final.13 = bf16[512,1024]{1,0:T(8,128)(2,1)} custom-call(s32[1]{0:T(128)} %bitcast.me.me_ref, bf16[528,128]{1,0:T(8,128)(2,1)S(1)} %collective-permute-done.10.refs_0_, f32[128,128]{1,0:T(8,128)S(1)} %get-tuple-element.58.rest_0_.refs_1_, f32[384,1024]{1,0:T(8,128)S(1)} %get-tuple-element.43.gated.refs_4_.refs_2_, ...), custom_call_target="tpu_custom_call", output_to_operand_aliasing={{}: (6, {})} | custom-call | flops 1000000 | bytes 1000 | tf_op jit(solution)/shard_map/final/pallas_call | solution.py:530
  (27 shorter events, 0.1 us)
Async XLA Ops:
  0.0 4.6 %copy-start.4 = (bf16[2,256,256]{2,1,0:T(8,128)(2,1)S(1)}, bf16[2,256,256]{2,1,0:T(8,128)(2,1)}, u32[]{:S(2)}) copy-start(bf16[2,256,256]{2,1,0:T(8,128)(2,1)} %constant.18.clone.fwd) | copy-start | bytes 786436
  0.0 4.6 %copy-start.5 = (bf16[2,128,256]{2,1,0:T(8,128)(2,1)S(1)}, bf16[2,128,256]{2,1,0:T(8,128)(2,1)}, u32[]{:S(2)}) copy-start(bf16[2,128,256]{2,1,0:T(8,128)(2,1)} %constant.19.clone.inv) | copy-start | bytes 393220
  0.0 8.8 %copy-start.6 = (f32[512,64]{0,1:T(8,128)S(1)}, f32[512,64]{0,1:T(8,128)}, u32[]{:S(2)}) copy-start(f32[512,64]{0,1:T(8,128)} %param.16) | copy-start | bytes 393220
  0.0 1.3 %copy-start.7 = (bf16[512,1024]{1,0:T(8,128)(2,1)S(1)}, bf16[512,1024]{1,0:T(8,128)(2,1)}, u32[]{:S(2)}) copy-start(bf16[512,1024]{1,0:T(8,128)(2,1)} %value.3) | copy-start | bytes 3145732
  1.3 3.3 %copy-start.8 = (bf16[512,1024]{1,0:T(8,128)(2,1)S(1)}, bf16[512,1024]{1,0:T(8,128)(2,1)}, u32[]{:S(2)}) copy-start(bf16[512,1024]{1,0:T(8,128)(2,1)} %value.3) | copy-start | bytes 3145732
  1.3 3.3 %copy-start.9 = (bf16[512,1024]{1,0:T(8,128)(2,1)S(1)}, bf16[512,1024]{1,0:T(8,128)(2,1)}, u32[]{:S(2)}) copy-start(bf16[512,1024]{1,0:T(8,128)(2,1)} %gate.1) | copy-start | bytes 3145732
  1.3 3.3 %copy-start.11 = (f32[128,1024]{1,0:T(8,128)S(1)}, f32[128,1024]{1,0:T(8,128)}, u32[]{:S(2)}) copy-start(f32[128,1024]{1,0:T(8,128)} %taps.1) | copy-start | bytes 1572868
  2.0 6.7 %collective-permute-start = (bf16[128,1024]{1,0:T(8,128)(2,1)}, bf16[128,1024]{1,0:T(8,128)(2,1)S(1)}, u32[]{:S(2)}, u32[]{:S(2)}) collective-permute-start(bf16[128,1024]{1,0:T(8,128)(2,1)} %tail.1), channel_id=1, source_target_pairs={{0,4},{4,8},{8,12},{12,16},{16,20},{20,24},{24,28},{1,5},{5,9},{9,... | collective-permute-start | bytes 786440 | tf_op jit(solution)/shard_map/ppermute | solution.py:24
  9.3 12.1 %copy-start = (f32[512,128]{1,0:T(8,128)S(1)}, f32[512,128]{1,0:T(8,128)}, u32[]{:S(2)}) copy-start(f32[512,128]{1,0:T(8,128)} %constant.22.clone.turn) | copy-start | bytes 786436
  9.3 12.1 %copy-start.2 = (bf16[2,256,512]{2,1,0:T(8,128)(2,1)S(1)}, bf16[2,256,512]{2,1,0:T(8,128)(2,1)}, u32[]{:S(2)}) copy-start(bf16[2,256,512]{2,1,0:T(8,128)(2,1)} %constant.21.clone.rest_0_.inv) | copy-start | bytes 1572868
  9.3 12.1 %copy-start.3 = (bf16[2,512,256]{2,1,0:T(8,128)(2,1)S(1)}, bf16[2,512,256]{2,1,0:T(8,128)(2,1)}, u32[]{:S(2)}) copy-start(bf16[2,512,256]{2,1,0:T(8,128)(2,1)} %constant.20.clone.fwd) | copy-start | bytes 1572868
  9.3 12.1 %copy-start.10 = (bf16[16,256]{1,0:T(8,128)(2,1)S(1)}, bf16[16,256]{1,0:T(8,128)(2,1)}, u32[]{:S(2)}) copy-start(bf16[16,256]{1,0:T(8,128)(2,1)} %constant.23.clone.widen) | copy-start | bytes 24580
  9.3 17.7 %collective-permute-start.1 = (bf16[560,128]{1,0:T(8,128)(2,1)S(1)}, bf16[560,128]{1,0:T(8,128)(2,1)S(1)}, u32[]{:S(2)}, u32[]{:S(2)}) collective-permute-start(bf16[560,128]{1,0:T(8,128)(2,1)S(1)} %get-tuple-element.50), channel_id=1, source_target_pairs={{0,16},{4,20},{8,24},{12,28},{16,0},{20,4},{24,8},{28,12},{1,17},{... | collective-permute-start | bytes 430088 | tf_op jit(solution)/shard_map/ppermute | solution.py:559
  15.5 13.3 %collective-permute-start.6 = (bf16[560,128]{1,0:T(8,128)(2,1)S(1)}, bf16[560,128]{1,0:T(8,128)(2,1)S(1)}, u32[]{:S(2)}, u32[]{:S(2)}) collective-permute-start(bf16[560,128]{1,0:T(8,128)(2,1)S(1)} %get-tuple-element.57), channel_id=1, source_target_pairs={{0,12},{4,16},{8,20},{12,24},{16,28},{20,0},{24,4},{28,8},{1,13},{... | collective-permute-start | bytes 430088 | tf_op jit(solution)/shard_map/ppermute | solution.py:559
  15.6 18.0 %collective-permute-start.5 = (bf16[560,128]{1,0:T(8,128)(2,1)S(1)}, bf16[560,128]{1,0:T(8,128)(2,1)S(1)}, u32[]{:S(2)}, u32[]{:S(2)}) collective-permute-start(bf16[560,128]{1,0:T(8,128)(2,1)S(1)} %get-tuple-element.56), channel_id=1, source_target_pairs={{0,20},{4,24},{8,28},{12,0},{16,4},{20,8},{24,12},{28,16},{1,21},{... | collective-permute-start | bytes 430088 | tf_op jit(solution)/shard_map/ppermute | solution.py:559
  19.3 16.0 %collective-permute-start.3 = (bf16[560,128]{1,0:T(8,128)(2,1)S(1)}, bf16[560,128]{1,0:T(8,128)(2,1)S(1)}, u32[]{:S(2)}, u32[]{:S(2)}) collective-permute-start(bf16[560,128]{1,0:T(8,128)(2,1)S(1)} %get-tuple-element.54), channel_id=1, source_target_pairs={{0,24},{4,28},{8,0},{12,4},{16,8},{20,12},{24,16},{28,20},{1,25},{... | collective-permute-start | bytes 430088 | tf_op jit(solution)/shard_map/ppermute | solution.py:559
  20.8 13.7 %collective-permute-start.4 = (bf16[560,128]{1,0:T(8,128)(2,1)S(1)}, bf16[560,128]{1,0:T(8,128)(2,1)S(1)}, u32[]{:S(2)}, u32[]{:S(2)}) collective-permute-start(bf16[560,128]{1,0:T(8,128)(2,1)S(1)} %get-tuple-element.55), channel_id=1, source_target_pairs={{0,8},{4,12},{8,16},{12,20},{16,24},{20,28},{24,0},{28,4},{1,9},{5... | collective-permute-start | bytes 430088 | tf_op jit(solution)/shard_map/ppermute | solution.py:559
  28.5 7.8 %collective-permute-start.2 = (bf16[560,128]{1,0:T(8,128)(2,1)S(1)}, bf16[560,128]{1,0:T(8,128)(2,1)S(1)}, u32[]{:S(2)}, u32[]{:S(2)}) collective-permute-start(bf16[560,128]{1,0:T(8,128)(2,1)S(1)} %get-tuple-element.53), channel_id=1, source_target_pairs={{0,4},{4,8},{8,12},{12,16},{16,20},{20,24},{24,28},{28,0},{1,5},{5... | collective-permute-start | bytes 430088 | tf_op jit(solution)/shard_map/ppermute | solution.py:559
  30.3 6.9 %collective-permute-start.7 = (bf16[560,128]{1,0:T(8,128)(2,1)S(1)}, bf16[560,128]{1,0:T(8,128)(2,1)S(1)}, u32[]{:S(2)}, u32[]{:S(2)}) collective-permute-start(bf16[560,128]{1,0:T(8,128)(2,1)S(1)} %get-tuple-element.70), channel_id=1, source_target_pairs={{0,28},{4,0},{8,4},{12,8},{16,12},{20,16},{24,20},{28,24},{1,29},{... | collective-permute-start | bytes 430088 | tf_op jit(solution)/shard_map/ppermute | solution.py:559
  40.6 21.7 %collective-permute-start.9 = (bf16[528,128]{1,0:T(8,128)(2,1)S(1)}, bf16[528,128]{1,0:T(8,128)(2,1)S(1)}, u32[]{:S(2)}, u32[]{:S(2)}) collective-permute-start(bf16[528,128]{1,0:T(8,128)(2,1)S(1)} %back.8.refs_8_), channel_id=1, source_target_pairs={{0,16},{4,20},{8,24},{12,28},{16,0},{20,4},{24,8},{28,12},{1,17},{... | collective-permute-start | bytes 405512 | tf_op jit(solution)/shard_map/ppermute | solution.py:559
  49.0 15.5 %collective-permute-start.8 = (bf16[528,128]{1,0:T(8,128)(2,1)S(1)}, bf16[528,128]{1,0:T(8,128)(2,1)S(1)}, u32[]{:S(2)}, u32[]{:S(2)}) collective-permute-start(bf16[528,128]{1,0:T(8,128)(2,1)S(1)} %back.9.refs_8_), channel_id=1, source_target_pairs={{0,12},{4,16},{8,20},{12,24},{16,28},{20,0},{24,4},{28,8},{1,13},{... | collective-permute-start | bytes 405512 | tf_op jit(solution)/shard_map/ppermute | solution.py:559
  50.9 19.1 %collective-permute-start.14 = (bf16[528,128]{1,0:T(8,128)(2,1)S(1)}, bf16[528,128]{1,0:T(8,128)(2,1)S(1)}, u32[]{:S(2)}, u32[]{:S(2)}) collective-permute-start(bf16[528,128]{1,0:T(8,128)(2,1)S(1)} %back.10.refs_8_), channel_id=1, source_target_pairs={{0,20},{4,24},{8,28},{12,0},{16,4},{20,8},{24,12},{28,16},{1,21},{... | collective-permute-start | bytes 405512 | tf_op jit(solution)/shard_map/ppermute | solution.py:559
  55.2 15.1 %collective-permute-start.13 = (bf16[528,128]{1,0:T(8,128)(2,1)S(1)}, bf16[528,128]{1,0:T(8,128)(2,1)S(1)}, u32[]{:S(2)}, u32[]{:S(2)}) collective-permute-start(bf16[528,128]{1,0:T(8,128)(2,1)S(1)} %back.11.refs_8_), channel_id=1, source_target_pairs={{0,8},{4,12},{8,16},{12,20},{16,24},{20,28},{24,0},{28,4},{1,9},{5... | collective-permute-start | bytes 405512 | tf_op jit(solution)/shard_map/ppermute | solution.py:559
  56.9 5.5 %copy-start.1 = (bf16[512,1024]{1,0:T(8,128)(2,1)S(1)}, bf16[512,1024]{1,0:T(8,128)(2,1)}, u32[]{:S(2)}) copy-start(bf16[512,1024]{1,0:T(8,128)(2,1)} %refs_3_.11) | copy-start | bytes 3145732
  56.9 5.5 %copy-start.12 = (f32[1024]{0:T(1024)S(1)}, f32[1024]{0:T(1024)}, u32[]{:S(2)}) copy-start(f32[1024]{0:T(1024)} %param.17) | copy-start | bytes 12292
  56.9 13.7 %collective-permute-start.12 = (bf16[528,128]{1,0:T(8,128)(2,1)S(1)}, bf16[528,128]{1,0:T(8,128)(2,1)S(1)}, u32[]{:S(2)}, u32[]{:S(2)}) collective-permute-start(bf16[528,128]{1,0:T(8,128)(2,1)S(1)} %back.12.refs_8_), channel_id=1, source_target_pairs={{0,24},{4,28},{8,0},{12,4},{16,8},{20,12},{24,16},{28,20},{1,25},{... | collective-permute-start | bytes 405512 | tf_op jit(solution)/shard_map/ppermute | solution.py:559
  64.4 7.3 %collective-permute-start.11 = (bf16[528,128]{1,0:T(8,128)(2,1)S(1)}, bf16[528,128]{1,0:T(8,128)(2,1)S(1)}, u32[]{:S(2)}, u32[]{:S(2)}) collective-permute-start(bf16[528,128]{1,0:T(8,128)(2,1)S(1)} %back.14.refs_6_), channel_id=1, source_target_pairs={{0,4},{4,8},{8,12},{12,16},{16,20},{20,24},{24,28},{28,0},{1,5},{5... | collective-permute-start | bytes 405512 | tf_op jit(solution)/shard_map/ppermute | solution.py:559
  66.4 6.6 %collective-permute-start.10 = (bf16[528,128]{1,0:T(8,128)(2,1)S(1)}, bf16[528,128]{1,0:T(8,128)(2,1)S(1)}, u32[]{:S(2)}, u32[]{:S(2)}) collective-permute-start(bf16[528,128]{1,0:T(8,128)(2,1)S(1)} %back.15.refs_6_), channel_id=1, source_target_pairs={{0,28},{4,0},{8,4},{12,8},{16,12},{20,16},{24,20},{28,24},{1,29},{... | collective-permute-start | bytes 405512 | tf_op jit(solution)/shard_map/ppermute | solution.py:559

commit v2 on v1

--- a/solution.py
+++ b/solution.py
@@ -197,152 +197,160 @@
 
 
 def cost(scale):
-    return pl.CostEstimate(flops=scale * 1_000_000, bytes_accessed=scale * 1000, transcendentals=0)
+    return pl.CostEstimate(flops=0, bytes_accessed=0, transcendentals=0)
 
 
 def lanes_of(slab):
     return pl.ds(pl.multiple_of(slab * LANES, LANES), LANES)
 
 
-def tail_body(value, out, sem):
-    count = out.shape[0]
-    copy = pltpu.make_async_copy(value.at[value.shape[0] - count :], out, sem)
-    copy.start()
-    copy.wait()
-
-
-def tail_call(value, count):
+def pace_body(me, out):
+    out[0] = me[0]
+
+
+def pace_call(me):
     return pl.pallas_call(
-        tail_body,
-        in_specs=[IN_HBM],
-        out_specs=IN_VMEM,
-        out_shape=jax.ShapeDtypeStruct((count, value.shape[1]), value.dtype),
-        scratch_shapes=[pltpu.SemaphoreType.DMA],
+        pace_body,
+        in_specs=[IN_SMEM],
+        out_specs=IN_SMEM,
+        out_shape=jax.ShapeDtypeStruct((1,), jnp.int32),
         compiler_params=kernel_params(4),
-        cost_estimate=pl.CostEstimate(flops=10_000_000_000, bytes_accessed=1000, transcendentals=0),
-        name="tail",
-    )(value)
-
-
-def main_body(value, gate, taps, fwd, inv, gated, spec_out, *scratch):
-    tops, held, fwd_held, inv_held = scratch[:2], scratch[2:5], scratch[5], scratch[6]
-    sems = scratch[7]
+        cost_estimate=pl.CostEstimate(flops=10_000_000_000, bytes_accessed=8, transcendentals=0),
+        name="pace",
+    )(me)
+
+
+def main_body(me, value, gate, taps, fwd, inv, gated, spec_out):
     count = taps.shape[0]
     wide = 2 * LANES
-    chunks = [slice(c, c + wide) for c in range(0, value.shape[1], wide)]
-    tables_in = [
-        pltpu.make_async_copy(fwd, fwd_held, sems.at[0, 0]),
-        pltpu.make_async_copy(inv, inv_held, sems.at[0, 1]),
-    ]
-    pieces = [
-        [
-            pltpu.make_async_copy(src.at[:, cols], dst.at[:, cols], sems.at[1 + at, k])
-            for k, (src, dst) in enumerate(zip((taps, value, gate), held))
-        ]
-        for at, cols in enumerate(chunks)
-    ]
-    for copy in sum(pieces[:1], tables_in) + sum(pieces[1:], []):
-        copy.start()
-    for copy in tables_in:
-        copy.wait()
-    for at, cols in enumerate(chunks):
-        for copy in pieces[at]:
-            copy.wait()
-        taps_spec = dot3(fwd_held[:, :, :count], held[0][:, cols])
+    for c in range(0, value.shape[1], wide):
+        cols = slice(c, c + wide)
+        taps_spec = dot3(fwd[:, :, :count], taps[:, cols])
         spec_out[:, cols] = taps_spec
-        short = short_rows(held[1][:, cols], taps_spec, fwd_held, inv_held)
-        gated[:, cols] = held[2][count:, cols].astype(jnp.float32) * short
-        for top, whole in zip(tops, held[1:]):
-            top[:, cols] = whole[:count, cols]
-
-
-def main_call(value, gate, taps, fwd, inv):
+        short = short_rows(value[:, cols], taps_spec, fwd, inv)
+        gated[:, cols] = gate[count:, cols].astype(jnp.float32) * short
+
+
+def main_call(me, value, gate, taps, fwd, inv, after):
     rows, chans = value.shape
     count = taps.shape[0]
-    top = jax.ShapeDtypeStruct((count, chans), jnp.bfloat16)
     return pl.pallas_call(
-        main_body,
-        in_specs=[IN_HBM] * 5,
-        out_specs=[IN_VMEM] * 4,
+        drop_after(main_body, 6, len(after)),
+        in_specs=[IN_SMEM] + [IN_VMEM] * 5 + [IN_ANY] * len(after),
+        out_specs=[IN_VMEM] * 2,
         out_shape=[
             jax.ShapeDtypeStruct((rows - count, chans), jnp.float32),
             jax.ShapeDtypeStruct((2 * count, chans), jnp.float32),
-            top,
-            top,
         ],
-        scratch_shapes=[
-            pltpu.VMEM(taps.shape, taps.dtype),
-            pltpu.VMEM(value.shape, value.dtype),
-            pltpu.VMEM(gate.shape, gate.dtype),
-            pltpu.VMEM(fwd.shape, fwd.dtype),
-            pltpu.VMEM(inv.shape, inv.dtype),
-            pltpu.SemaphoreType.DMA((1 + chans // (2 * LANES), 3)),
-        ],
-        compiler_params=kernel_params(16),
+        compiler_params=kernel_params(12),
         cost_estimate=cost(4),
         name="short_main",
-    )(value, gate, taps, fwd, inv)
-
-
-def head_body(part, count, me, halo, value, gate, gated, taps_spec, long_taps, fwd, inv, *rest):
+    )(me, value, gate, taps, fwd, inv, *after)
+
+
+def drop_after(body, keep, unused):
+    return lambda *refs: body(*refs[:keep], *refs[keep + unused :])
+
+
+def write_code(code, values, filter_rows):
+    groups = 8
+    rows = sum(v.shape[0] for v in values)
+    peak = functools.reduce(
+        jnp.maximum, [jnp.max(jnp.abs(v), axis=0, keepdims=True) for v in values]
+    )
+    scale = scale_of(peak)
+    start = 0
+    for v in values:
+        code[start : start + v.shape[0]] = to_code(v, scale)
+        start += v.shape[0]
+    scale = jnp.broadcast_to(scale, (groups, LANES))
+    if filter_rows is None:
+        both = jnp.concatenate([scale, scale], 0)
+    else:
+        size = jnp.abs(filter_rows)
+        many = filter_rows.shape[0] // groups
+        most = size[:groups]
+        for c in range(1, many):
+            most = jnp.maximum(most, size[c * groups : (c + 1) * groups])
+        filter_scale = scale_of(jnp.max(most, axis=1, keepdims=True))
+        filter_scale = jnp.broadcast_to(filter_scale, (groups, LANES))
+        both = jnp.concatenate([scale, filter_scale], 0)
+        code[rows + TILE :] = to_code(filter_rows, jnp.concatenate([filter_scale] * many, 0))
+    code[rows : rows + TILE] = both.astype(jnp.bfloat16)
+
+
+def ahead_body(part, me, value, gate, taps, long_taps, fwd, inv, *codes):
+    count = taps.shape[0]
+    for d, code in zip(part, codes):
+        slab = me[0] ^ d
+        cols = lanes_of(slab)
+        taps_spec = dot3(fwd[:, :, :count], taps[:, cols])
+        short = short_rows(value[:, cols], taps_spec, fwd, inv)
+        write_code(code, [gate[count:, cols].astype(jnp.float32) * short], long_taps[slab])
+
+
+def ahead_call(part, me, value, gate, taps, long_taps, fwd, inv, after):
+    rows = value.shape[0] - taps.shape[0] + TILE + long_taps.shape[1]
+    code = jax.ShapeDtypeStruct((rows, LANES), jnp.bfloat16)
+    return pl.pallas_call(
+        drop_after(functools.partial(ahead_body, part), 7, len(after)),
+        in_specs=[IN_SMEM] + [IN_VMEM] * 6 + [IN_ANY] * len(after),
+        out_specs=[IN_VMEM] * len(part),
+        out_shape=[code] * len(part),
+        compiler_params=kernel_params(12),
+        cost_estimate=cost(1),
+        name="short_ahead",
+    )(me, value, gate, taps, long_taps, fwd, inv, *after)
+
+
+def head_body(part, ahead, me, halo, value, gate, gated, taps_spec, long_taps, fwd, inv, *outs):
     taps = halo.shape[0]
-    rows = taps + gated.shape[0]
-    groups = 8
-    outs = rest[-2 * len(part) :]
     tops, codes = outs[: len(part)], outs[len(part) :]
     for d, top, code in zip(part, tops, codes):
-        slab = lax.rem(me[0] + d, count)
+        slab = me[0] ^ d
         cols = lanes_of(slab)
-        ext = jnp.concatenate([halo[:, cols], value[:, cols]], 0)
+        ext = jnp.concatenate([halo[:, cols], value[:taps, cols]], 0)
         short = short_rows(ext, taps_spec[:, cols], fwd, inv)
-        first = gate[:, cols].astype(jnp.float32) * short
+        first = gate[:taps, cols].astype(jnp.float32) * short
         top[...] = first
-        later = gated[:, cols]
-        peak = jnp.maximum(
-            jnp.max(jnp.abs(first), axis=0, keepdims=True),
-            jnp.max(jnp.abs(later), axis=0, keepdims=True),
-        )
-        scale = scale_of(peak)
-        held = long_taps[slab]
-        size = jnp.abs(held)
-        most = size[:groups]
-        for c in range(groups, held.shape[0], groups):
-            most = jnp.maximum(most, size[c : c + groups])
-        filter_scale = scale_of(jnp.max(most, axis=1, keepdims=True))
-        filter_scale = jnp.broadcast_to(filter_scale, (groups, LANES))
-        many = held.shape[0] // groups
-        code[:taps] = to_code(first, scale)
-        code[taps:rows] = to_code(later, scale)
-        both = jnp.concatenate([jnp.broadcast_to(scale, (8, LANES)), filter_scale], 0)
-        code[rows : rows + TILE] = both.astype(jnp.bfloat16)
-        code[rows + TILE :] = to_code(held, jnp.concatenate([filter_scale] * many, 0))
-
-
-def head_call(part, count, me, halo, value, gate, gated, taps_spec, long_taps, fwd, inv, after):
+        if d in ahead:
+            write_code(code, [first], None)
+        else:
+            write_code(code, [first, gated[:, cols]], long_taps[slab])
+
+
+def head_call(part, ahead, me, halo, value, gate, gated, taps_spec, long_taps, fwd, inv, after):
     taps = halo.shape[0]
-    rows = taps + gated.shape[0]
-    held = long_taps.shape[1]
-    code = jax.ShapeDtypeStruct((rows + TILE + held, LANES), jnp.bfloat16)
+    whole = taps + gated.shape[0] + TILE + long_taps.shape[1]
+    codes = [
+        jax.ShapeDtypeStruct((taps + TILE if d in ahead else whole, LANES), jnp.bfloat16)
+        for d in part
+    ]
     top = jax.ShapeDtypeStruct((taps, LANES), jnp.float32)
     return pl.pallas_call(
-        functools.partial(head_body, part, count),
+        drop_after(functools.partial(head_body, part, ahead), 9, len(after)),
         in_specs=[IN_SMEM] + [IN_VMEM] * 8 + [IN_ANY] * len(after),
         out_specs=[IN_VMEM] * (2 * len(part)),
-        out_shape=[top] * len(part) + [code] * len(part),
+        out_shape=[top] * len(part) + codes,
         compiler_params=kernel_params(12),
         cost_estimate=cost(len(part)),
         name="short_head",
     )(me, halo, value, gate, gated, taps_spec, long_taps, fwd, inv, *after)
 
 
-def forward_body(code, fwd, turn, widen, *rest):
+def forward_body(d, clear, pieces, me, fwd, turn, widen, *rest):
     spec_out, filter_out, held_x, held_h = rest[-4:]
     rows = held_x.shape[0]
     half = rows // 2
     groups = 8
-    held_x[...] = from_code(code[:rows], code[rows : rows + 1].astype(jnp.float32))
-    scale = code[rows : rows + TILE].astype(jnp.float32)[groups:]
-    taps = code[rows + TILE :]
+    end = rows
+    for code, length in zip(rest, pieces):
+        scales = code[length : length + TILE].astype(jnp.float32)
+        held_x[end - length : end] = from_code(code[:length], scales[:1])
+        end -= length
+    code, length = rest[0], pieces[0]
+    scale = code[length : length + TILE].astype(jnp.float32)[groups:]
+    taps = code[length + TILE :]
     many = taps.shape[0] // groups
     h_high, h_low = split(from_code(taps, jnp.concatenate([scale] * many, 0)))
     h_high, h_low = h_high.astype(jnp.float32), h_low.astype(jnp.float32)
@@ -362,72 +370,50 @@
     both = dot(fwd[0], jnp.concatenate(highs + lows, 1))
     both = both[:, :width] + both[:, width:] + dot(fwd[1], jnp.concatenate(highs, 1))
     w_re, w_im = turn[:half], turn[half:]
-    for at, out in enumerate((spec_out, filter_out)):
+    outs = []
+    for at in range(2):
         even = both[:, at * LANES : (at + 1) * LANES]
         odd = both[:, (2 + at) * LANES : (3 + at) * LANES]
         o_re, o_im = odd[:half], odd[half:]
         t_re = o_re * w_re - o_im * w_im
         t_im = o_re * w_im + o_im * w_re
-        out[:half] = even[:half] + t_re
-        out[half:rows] = even[:half] - t_re
-        out[rows : rows + half] = even[half:] + t_im
-        out[rows + half :] = even[half:] - t_im
-
-
-def forward_call(code, fwd, turn, widen, early, after):
+        outs.append((even[:half] + t_re, even[:half] - t_re, even[half:] + t_im, even[half:] - t_im))
+    for c, piece in enumerate(outs[0]):
+        spec_out[c * half : (c + 1) * half] = piece
+    if clear:
+        filter_out[...] = jnp.zeros_like(filter_out)
+    own = me[0] ^ d
+    later = jnp.where(own + 1 < filter_out.shape[0] - 2, own + 1, own + 2)
+    odd = lax.broadcasted_iota(jnp.int32, (half, LANES), 0) % 2 == 1
+    for c, piece in enumerate(outs[1]):
+        filter_out[own, c * half : (c + 1) * half] += piece
+        moved = jnp.where(odd, -piece, piece) if c < 2 else jnp.where(odd, piece, -piece)
+        at = slice(((c + 2) % 4) * half, ((c + 2) % 4 + 1) * half)
+        filter_out[later, at] += moved
+
+
+def forward_call(d, count, me, codes, fwd, turn, widen, early, so_far, after):
     rows = 2 * fwd.shape[2]
-    spec = jax.ShapeDtypeStruct((2 * rows, LANES), jnp.float32)
+    held = so_far + early
+    last = codes[-1].shape[0] - TILE
+    pieces = [rows - last, last] if len(codes) > 1 else [rows]
     return pl.pallas_call(
-        forward_body,
-        in_specs=[IN_VMEM] * (4 + len(early)) + [IN_ANY] * len(after),
+        functools.partial(forward_body, d, not so_far, pieces),
+        in_specs=[IN_SMEM] + [IN_VMEM] * (3 + len(codes) + len(held)) + [IN_ANY] * len(after),
         out_specs=[IN_VMEM] * 2,
-        out_shape=[spec, spec],
+        out_shape=[
+            jax.ShapeDtypeStruct((2 * rows, LANES), jnp.float32),
+            jax.ShapeDtypeStruct((count + 2, 2 * rows, LANES), jnp.float32),
+        ],
         scratch_shapes=[
             pltpu.VMEM((rows, LANES), jnp.float32),
             pltpu.VMEM((2, rows, LANES), jnp.float32),
         ],
+        input_output_aliases={4 + len(codes): 1} if so_far else {},
         compiler_params=kernel_params(12),
         cost_estimate=cost(1),
         name="forward",
-    )(code, fwd, turn, widen, *early, *after)
-
-
-def by_lag_body(me_ref, *refs):
-    spectra, out = refs[:-1], refs[-1]
-    count = len(spectra)
-    half = out.shape[1] // 2
-    me = me_ref[0]
-    odd = lax.broadcasted_iota(jnp.int32, (8, LANES), 0) % 2 == 1
-    sign = jnp.where(odd, 1.0, -1.0)
-    lags = [lax.rem(me - d + count, count) for d in range(count)]
-    signs = [sign * (lag > 0).astype(jnp.float32) for lag in lags]
-
-    def chunk(c, _):
-        re = pl.ds(pl.multiple_of(c * 8, 8), 8)
-        im = pl.ds(pl.multiple_of(half + c * 8, 8), 8)
-        for d in range(count):
-            before = spectra[(d + 1) % count]
-            out[lags[d], re] = spectra[d][re] + signs[d] * before[im]
-            out[lags[d], im] = spectra[d][im] - signs[d] * before[re]
-        out[count, re] = jnp.zeros((8, LANES), jnp.float32)
-        out[count, im] = jnp.zeros((8, LANES), jnp.float32)
-        return 0
-
-    lax.fori_loop(0, half // 8, chunk, 0, unroll=2)
-
-
-def by_lag_call(me, spectra):
-    count = len(spectra)
-    bins = spectra[0].shape[0]
-    return pl.pallas_call(
-        by_lag_body,
-        in_specs=[IN_SMEM] + [IN_VMEM] * count,
-        out_specs=IN_VMEM,
-        out_shape=jax.ShapeDtypeStruct((count + 1, bins, LANES), jnp.float32),
-        compiler_params=kernel_params(12),
-        cost_estimate=cost(1),
-        name="by_lag",
-    )(me, *spectra)
+    )(me, fwd, turn, widen, *codes, *held, *after)
 
 
 def back_body(part, count, me_ref, filt, inv, turn, *refs):
@@ -437,10 +423,9 @@
     me = me_ref[0]
 
     for e, code in zip(part, codes):
-        target = lax.rem(me + e, count)
         lags = []
         for d in range(count):
-            lag = target - lax.rem(me - d + count, count)
+            lag = (me ^ e) - (me ^ d)
             lags.append(jnp.where(lag >= 0, lag, count))
 
         def chunk(c, _):
@@ -468,7 +453,7 @@
             total[im, LANES:] = d_im * w_re - d_re * w_im
             return 0
 
-        lax.fori_loop(0, half // 8, chunk, 0, unroll=2)
+        lax.fori_loop(0, half // 8, chunk, 0, unroll=4)
         values = dot3(inv, total[...])
         held[pl.ds(0, half, stride=2)] = values[:, :LANES]
         held[pl.ds(1, half, stride=2)] = values[:, LANES:]
@@ -505,7 +490,7 @@
     rows = gate.shape[0]
     copies = []
     for at, d in enumerate(part):
-        cols = lanes_of(lax.rem(me[0] + d, count))
+        cols = lanes_of(me[0] ^ d)
         code, top = codes[at], tops[at]
         scale = code[rows : rows + 1].astype(jnp.float32)
         for r, part_gated in ((slice(0, taps), top[...]), (slice(taps, rows), gated[:, cols])):
@@ -543,25 +528,20 @@
     )(*args)
 
 
-def rotation_order(count):
-    return sorted(range(1, count), key=lambda d: (-min(d, count - d), d))
-
-
 def in_slabs(output_gate, input_gate, value_input, short_filter, long_filter, skip_gain):
     count = lax.axis_size("ctx")
     me = lax.axis_index("ctx").reshape(1)
     rows = value_input.shape[0]
     taps = short_filter.shape[0]
     groups = long_filter.shape[1] // count
-    order = rotation_order(count) + [0]
-
-    def rotated(block, distance):
-        return lax.ppermute(block, "ctx", [(i, (i + distance) % count) for i in range(count)])
+
+    def exchanged(block, d):
+        return lax.ppermute(block, "ctx", [(i, i ^ d) for i in range(count)]) if d else block
 
     def table(values):
         return jnp.asarray(split_table(values))
 
-    halo = passed_along(tail_call(value_input, taps), "ctx", 1)
+    halo = passed_along(value_input[rows - taps :], "ctx", 1)
     long_taps = long_filter.T.reshape(count, groups, rows // LANES, LANES)
     long_taps = jnp.swapaxes(long_taps, 1, 2).reshape(count, -1, LANES)
 
@@ -573,66 +553,92 @@
     turn = jnp.asarray(turning(rows, LANES))
     widen = jnp.asarray(widening(groups, LANES))
 
-    gated, taps_spec, value_top, gate_top = main_call(
-        value_input, input_gate, short_filter, short_fwd, short_inv
-    )
-    came, tops, codes, specs, spectra = {}, {}, {}, {}, {}
-    after = []
+    came, tops, specs, answers = {}, {}, {}, {}
+    after, filt, mixed = [], [], []
+
+    paced = pace_call(me)
+    main_out = []
+
+    def mains():
+        main_out[:] = main_call(
+            paced, value_input, input_gate, short_filter, short_fwd, short_inv, after
+        )
+        after[:] = main_out[:1]
+
+    def aheads(*part):
+        codes = ahead_call(
+            part, paced, value_input, input_gate, short_filter, long_taps, short_fwd, short_inv,
+            after,
+        )
+        after[:] = codes[:1]
+        for d, code in zip(part, codes):
+            came[d] = [exchanged(code, d)]
 
     def heads(*part):
         outs = head_call(
-            part, count, me, halo, value_top, gate_top, gated, taps_spec, long_taps,
+            part, tuple(came), me, halo, value_input, input_gate, *main_out, long_taps,
             short_fwd, short_inv, after,
         )
         after[:] = outs[:1]
         for d, top, code in zip(part, outs, outs[len(part) :]):
             tops[d] = top
-            came[d] = rotated(code, d) if d else code
-
-    def forwards(d, early=()):
-        specs[d], spectra[d] = forward_call(came[d], fwd, turn, widen, early, after)
-        after[:] = [specs[d]]
-
-    heads(order[0])
-    heads(*order[1:3])
-    heads(*order[3:5], 0)
-    forwards(0, [inv])
-    forwards(order[0])
-    heads(order[5])
-    forwards(order[1])
-    heads(order[6])
-    for d in order[2:7]:
-        forwards(d)
-    specs = [specs[d] for d in range(count)]
-    filt = by_lag_call(me, [spectra[d] for d in range(count)])
-
-    answers, after = {}, []
-    mixed = []
-
-    def backs(e):
-        (code,) = back_call([e], me, filt, inv, turn, specs, after)
-        answers[e] = rotated(code, e) if e else code
-        after[:] = [code]
+            came[d] = came.get(d, []) + [exchanged(code, d)]
+
+    def forwards(*part):
+        for d in part:
+            specs[d], filt[:] = (lambda a, b: (a, [b]))(
+                *forward_call(
+                    d, count, me, came[d], fwd, turn, widen, [] if d else [inv], filt, after
+                )
+            )
+            after[:] = [specs[d]]
+
+    def backs(*part):
+        held = [specs[d] for d in range(count)]
+        for e in part:
+            (code,) = back_call([e], me, filt[0], inv, turn, held, after)
+            answers[e] = exchanged(code, e)
+            after[:] = [code]
 
     def finals(*part):
-        owners = [(count - e) % count for e in part]
         mixed[:] = [
             final_call(
-                owners, count, me, [answers[e] for e in part], [tops[d] for d in owners],
-                gated, output_gate, skip_gain[None], mixed, after,
+                part, count, me, [answers[e] for e in part], [tops[e] for e in part],
+                main_out[0], output_gate, skip_gain[None], mixed, after,
             )
         ]
         after[:] = mixed
 
-    for e in order[:5]:
-        backs(e)
+    mains()
+    heads(4)
+    heads(2)
+    heads(3)
+    heads(5)
+    heads(6, 0)
+    forwards(0)
+    forwards(4)
+    heads(1)
+    forwards(2)
+    heads(7)
+    forwards(3)
+    forwards(5)
+    forwards(6)
+    forwards(1)
+    forwards(7)
+    backs(4)
+    backs(5)
+    backs(6)
+    backs(7)
+    backs(3)
     backs(0)
-    finals(0, order[0])
-    backs(order[5])
-    finals(order[1])
-    backs(order[6])
-    for e in order[2:7]:
-        finals(e)
+    finals(0, 4)
+    backs(2)
+    finals(5)
+    backs(1)
+    finals(6, 7)
+    finals(3)
+    finals(2)
+    finals(1)
     return mixed[0]
 
 

time: 74.1 us -> 69.8 us (0.942)
  starting transfers between devices: 33.2 us -> 25.5 us
  waiting for transfers between devices: 5.9 us -> 9.57 us
  Pallas kernels: 31.6 us -> 30.6 us
  local copies, waits for them, and re-layouts: 2.53 us -> 3.33 us
    ppermute x14, starting transfers between devices: 30.7 us -> 23.1 us  [exchanged(): lax.ppermute(block, 'ctx', [(i, i ^ d) for i in range(count)])]
    ppermute x14, waiting for transfers between devices: 5.89 us -> 9.56 us  [exchanged(): lax.ppermute(block, 'ctx', [(i, i ^ d) for i in range(count)])]
    pallas_call x8, Pallas kernels: 12.9 us -> 11.7 us  [back_call(): pl.pallas_call(functools.partial(back_body, part, count), in_specs=[IN_SM...]
    slice x0 -> x1, local copies, waits for them, and re-layouts: none -> 0.97 us  [in_slabs(): halo = passed_along(value_input[rows - taps:], 'ctx', 1)]
    pallas_call x16 -> x17, Pallas kernels: 16.3 us -> 16.5 us  [the longest x8 8.73 us: forward_call(): pl.pallas_call(functools.partial(forward_body, d, not so_far, pieces), in...]
    unnamed x30 -> x27, local copies, waits for them, and re-layouts: 2.53 us -> 2.36 us
    pallas_call x7 -> x6, Pallas kernels: 2.41 us -> 2.41 us  [final_call(): pl.pallas_call(functools.partial(final_body, part, count), in_specs=specs...]
  transfers between devices with their start and end apart: 15 -> 15, of which waited for: 3 -> 7; matrix products, arithmetic and copies ran while one was open for 2% -> 2% of each run, Pallas kernels for 36% -> 38%
where the time goes in v2:
time: 69.8 us; the launch traced here: 69.6 us
  Pallas kernels  30.6 us (44%)
  starting transfers between devices  25.5 us (37%)
  waiting for transfers between devices  9.57 us (14%)
  local copies, waits for them, and re-layouts  3.33 us (5%)
    ppermute x14, starting transfers between devices, exchanged(): lax.ppermute(block, 'ctx', [(i, i ^ d) for i in range(count)])  23.1 us
    pallas_call x8, Pallas kernels, back_call(): pl.pallas_call(functools.partial(back_body, part, count), in_specs=[IN_SM...  11.7 us
    ppermute x14, waiting for transfers between devices, exchanged(): lax.ppermute(block, 'ctx', [(i, i ^ d) for i in range(count)])  9.56 us
    pallas_call x8, Pallas kernels, forward_call(): pl.pallas_call(functools.partial(forward_body, d, not so_far, pieces), in...  8.73 us
    pallas_call x7, Pallas kernels, head_call(): pl.pallas_call(drop_after(functools.partial(head_body, part, ahead), 9, l...  3.73 us
    pallas_call x1, Pallas kernels, main_call(): pl.pallas_call(drop_after(main_body, 6, len(after)), in_specs=[IN_SMEM] +...  3.49 us
    pallas_call x6, Pallas kernels, final_call(): pl.pallas_call(functools.partial(final_body, part, count), in_specs=specs...  2.41 us
    ppermute x1, starting transfers between devices, passed_along(): return lax.ppermute(block, axis, route)  2.37 us
  transfers between devices with their start and end apart: 15, of which 7 were waited for; matrix products, arithmetic and copies ran while one was open for 2% of the time, Pallas kernels for 38%

profile of v2, /device:TPU:0, one launch (start us, length us, event | category | flops | bytes accessed | tf_op | source)
XLA Modules:
  0.0 69.6 jit_solution(16914985232808036209)
XLA Ops:
  0.0 1.0 %slice.3 = bf16[128,1024]{1,0:T(8,128)(2,1)S(1)} slice(bf16[512,1024]{1,0:T(8,128)(2,1)} %refs_2_.15), slice={[384:512], [0:1024]} | slice | bytes 524288 | tf_op jit(solution)/shard_map/slice | solution.py:544
  1.0 2.4 %collective-permute-start = (bf16[128,1024]{1,0:T(8,128)(2,1)S(1)}, bf16[128,1024]{1,0:T(8,128)(2,1)S(1)}, u32[]{:S(2)}, u32[]{:S(2)}) collective-permute-start(bf16[128,1024]{1,0:T(8,128)(2,1)S(1)} %slice.3), channel_id=1, source_target_pairs={{0,4},{4,8},{8,12},{12,16},{16,20},{20,24},{24,28},{1,5},{5,9},{9,... | collective-permute-start | bytes 786440 | tf_op jit(solution)/shard_map/ppermute | solution.py:24
  3.4 0.0 copy-start.6
  3.4 0.0 copy-start.7
  3.4 0.5 pace.1.refs_0_
  4.0 0.6 copy-done
  4.6 0.3 copy-done.2
  4.9 0.0 copy-done.6
  4.9 0.0 copy-done.7
  5.0 0.2 copy-done.10
  5.2 3.5 %short_main.1 = (f32[384,1024]{1,0:T(8,128)S(1)}, f32[256,1024]{1,0:T(8,128)S(1)}) custom-call(s32[1]{0:T(128)} %pace.1.refs_0_, bf16[512,1024]{1,0:T(8,128)(2,1)S(1)} %copy-done, bf16[512,1024]{1,0:T(8,128)(2,1)S(1)} %copy-done.2, f32[128,1024]{1,0:T(8,128)S(1)} %copy-done.10, bf16[2,256,256]{2,1,0:T(8,128)(2,1)S(1)} %copy-done.6, ...), custom_call_target="tpu_custom_call" | custom-call | tf_op jit(solution)/shard_map/short_main/pallas_call | solution.py:237
  8.7 0.5 short_head.7
  9.2 4.1 %collective-permute-start.2 = (bf16[560,128]{1,0:T(8,128)(2,1)S(1)}, bf16[560,128]{1,0:T(8,128)(2,1)S(1)}, u32[]{:S(2)}, u32[]{:S(2)}) collective-permute-start(bf16[560,128]{1,0:T(8,128)(2,1)S(1)} %get-tuple-element.43), channel_id=1, source_target_pairs={{0,16},{4,20},{8,24},{12,28},{16,0},{20,4},{24,8},{28,12},{1,17},{... | collective-permute-start | bytes 430088 | tf_op jit(solution)/shard_map/ppermute | solution.py:539
  13.3 0.5 short_head.8
  13.8 1.6 %collective-permute-start.1 = (bf16[560,128]{1,0:T(8,128)(2,1)S(1)}, bf16[560,128]{1,0:T(8,128)(2,1)S(1)}, u32[]{:S(2)}, u32[]{:S(2)}) collective-permute-start(bf16[560,128]{1,0:T(8,128)(2,1)S(1)} %get-tuple-element.42), channel_id=1, source_target_pairs={{0,8},{4,12},{8,0},{12,4},{16,24},{20,28},{24,16},{28,20},{1,9},{5... | collective-permute-start | bytes 430088 | tf_op jit(solution)/shard_map/ppermute | solution.py:539
  15.4 0.5 short_head.9
  15.9 0.8 %collective-permute-start.7 = (bf16[560,128]{1,0:T(8,128)(2,1)S(1)}, bf16[560,128]{1,0:T(8,128)(2,1)S(1)}, u32[]{:S(2)}, u32[]{:S(2)}) collective-permute-start(bf16[560,128]{1,0:T(8,128)(2,1)S(1)} %get-tuple-element.59), channel_id=1, source_target_pairs={{0,12},{4,8},{8,4},{12,0},{16,28},{20,24},{24,20},{28,16},{1,13},{... | collective-permute-start | bytes 430088 | tf_op jit(solution)/shard_map/ppermute | solution.py:539
  16.7 0.5 short_head.10
  17.2 0.1 collective-permute-start.6
  17.3 0.8 %short_head.11 = (f32[128,128]{1,0:T(8,128)S(1)}, f32[128,128]{1,0:T(8,128)S(1)}, bf16[560,128]{1,0:T(8,128)(2,1)S(1)}, bf16[560,128]{1,0:T(8,128)(2,1)S(1)}) custom-call(s32[1]{0:T(128)} %bitcast.me.refs_0_.me_ref, bf16[128,1024]{1,0:T(8,128)(2,1)S(1)} %collective-permute-done.refs_1_, bf16[512,1024]{1,0:T(8,128)(2,1)S(1)} %copy-done, ...), custom_call_target="tpu_custom_call" | custom-call | tf_op jit(solution)/shard_map/short_head/pallas_call | solution.py:330
  18.1 3.4 %collective-permute-start.5 = (bf16[560,128]{1,0:T(8,128)(2,1)S(1)}, bf16[560,128]{1,0:T(8,128)(2,1)S(1)}, u32[]{:S(2)}, u32[]{:S(2)}) collective-permute-start(bf16[560,128]{1,0:T(8,128)(2,1)S(1)} %get-tuple-element.57), channel_id=1, source_target_pairs={{0,24},{4,28},{8,16},{12,20},{16,8},{20,12},{24,0},{28,4},{1,25},{... | collective-permute-start | bytes 430088 | tf_op jit(solution)/shard_map/ppermute | solution.py:539
  21.5 1.3 %forward.8 = (f32[1024,128]{1,0:T(8,128)S(1)}, f32[10,1024,128]{2,1,0:T(8,128)S(1)}) custom-call(s32[1]{0:T(128)} %bitcast.me.refs_0_.me_ref, bf16[2,512,256]{2,1,0:T(8,128)(2,1)S(1)} %copy-done.5, f32[512,128]{1,0:T(8,128)S(1)} %copy-done.1, bf16[16,256]{1,0:T(8,128)(2,1)S(1)} %copy-done.9, bf16[560,128]{1,0:T(8,128)(2,1)S(1)} %get-tuple-element.47.rest_0_, ...), custom_call_target="tpu_custom_call" | custom-call | tf_op jit(solution)/shard_map/forward/pallas_call | solution.py:400
  22.8 1.1 %forward.9 = (f32[1024,128]{1,0:T(8,128)S(1)}, f32[10,1024,128]{2,1,0:T(8,128)S(1)}) custom-call(s32[1]{0:T(128)} %bitcast.me.refs_0_.me_ref, bf16[2,512,256]{2,1,0:T(8,128)(2,1)S(1)} %copy-done.5, f32[512,128]{1,0:T(8,128)S(1)} %copy-done.1, bf16[16,256]{1,0:T(8,128)(2,1)S(1)} %copy-done.9, ...), custom_call_target="tpu_custom_call", output_to_operand_aliasing={{1}: (5, {})} | custom-call | tf_op jit(solution)/shard_map/forward/pallas_call | solution.py:400
  23.9 0.5 short_head.12
  24.4 0.1 collective-permute-start.4
  24.5 0.7 %collective-permute-done.1.rest_0_ = bf16[560,128]{1,0:T(8,128)(2,1)S(1)} collective-permute-done((bf16[560,128]{1,0:T(8,128)(2,1)S(1)}, bf16[560,128]{1,0:T(8,128)(2,1)S(1)}, u32[]{:S(2)}, u32[]{:S(2)}) %collective-permute-start.1) | collective-permute-done | bytes 143392 | tf_op jit(solution)/shard_map/ppermute | solution.py:539
  25.2 1.1 %forward.10 = (f32[1024,128]{1,0:T(8,128)S(1)}, f32[10,1024,128]{2,1,0:T(8,128)S(1)}) custom-call(s32[1]{0:T(128)} %bitcast.me.refs_0_.me_ref, bf16[2,512,256]{2,1,0:T(8,128)(2,1)S(1)} %copy-done.5, f32[512,128]{1,0:T(8,128)S(1)} %copy-done.1, bf16[16,256]{1,0:T(8,128)(2,1)S(1)} %copy-done.9, ...), custom_call_target="tpu_custom_call", output_to_operand_aliasing={{1}: (5, {})} | custom-call | tf_op jit(solution)/shard_map/forward/pallas_call | solution.py:400
  26.2 0.5 short_head.13
  26.7 0.6 collective-permute-start.3
  27.4 0.8 %collective-permute-done.7.rest_0_ = bf16[560,128]{1,0:T(8,128)(2,1)S(1)} collective-permute-done((bf16[560,128]{1,0:T(8,128)(2,1)S(1)}, bf16[560,128]{1,0:T(8,128)(2,1)S(1)}, u32[]{:S(2)}, u32[]{:S(2)}) %collective-permute-start.7) | collective-permute-done | bytes 143392 | tf_op jit(solution)/shard_map/ppermute | solution.py:539
  28.2 1.1 %forward.11 = (f32[1024,128]{1,0:T(8,128)S(1)}, f32[10,1024,128]{2,1,0:T(8,128)S(1)}) custom-call(s32[1]{0:T(128)} %bitcast.me.refs_0_.me_ref, bf16[2,512,256]{2,1,0:T(8,128)(2,1)S(1)} %copy-done.5, f32[512,128]{1,0:T(8,128)S(1)} %copy-done.1, bf16[16,256]{1,0:T(8,128)(2,1)S(1)} %copy-done.9, ...), custom_call_target="tpu_custom_call", output_to_operand_aliasing={{1}: (5, {})} | custom-call | tf_op jit(solution)/shard_map/forward/pallas_call | solution.py:400
  29.3 1.1 %forward.12 = (f32[1024,128]{1,0:T(8,128)S(1)}, f32[10,1024,128]{2,1,0:T(8,128)S(1)}) custom-call(s32[1]{0:T(128)} %bitcast.me.refs_0_.me_ref, bf16[2,512,256]{2,1,0:T(8,128)(2,1)S(1)} %copy-done.5, f32[512,128]{1,0:T(8,128)S(1)} %copy-done.1, bf16[16,256]{1,0:T(8,128)(2,1)S(1)} %copy-done.9, ...), custom_call_target="tpu_custom_call", output_to_operand_aliasing={{1}: (5, {})} | custom-call | tf_op jit(solution)/shard_map/forward/pallas_call | solution.py:400
  30.4 1.0 %collective-permute-done.5.rest_0_ = bf16[560,128]{1,0:T(8,128)(2,1)S(1)} collective-permute-done((bf16[560,128]{1,0:T(8,128)(2,1)S(1)}, bf16[560,128]{1,0:T(8,128)(2,1)S(1)}, u32[]{:S(2)}, u32[]{:S(2)}) %collective-permute-start.5) | collective-permute-done | bytes 143392 | tf_op jit(solution)/shard_map/ppermute | solution.py:539
  31.4 1.1 %forward.13 = (f32[1024,128]{1,0:T(8,128)S(1)}, f32[10,1024,128]{2,1,0:T(8,128)S(1)}) custom-call(s32[1]{0:T(128)} %bitcast.me.refs_0_.me_ref, bf16[2,512,256]{2,1,0:T(8,128)(2,1)S(1)} %copy-done.5, f32[512,128]{1,0:T(8,128)S(1)} %copy-done.1, bf16[16,256]{1,0:T(8,128)(2,1)S(1)} %copy-done.9, ...), custom_call_target="tpu_custom_call", output_to_operand_aliasing={{1}: (5, {})} | custom-call | tf_op jit(solution)/shard_map/forward/pallas_call | solution.py:400
  32.5 1.1 %forward.14 = (f32[1024,128]{1,0:T(8,128)S(1)}, f32[10,1024,128]{2,1,0:T(8,128)S(1)}) custom-call(s32[1]{0:T(128)} %bitcast.me.refs_0_.me_ref, bf16[2,512,256]{2,1,0:T(8,128)(2,1)S(1)} %copy-done.5, f32[512,128]{1,0:T(8,128)S(1)} %copy-done.1, bf16[16,256]{1,0:T(8,128)(2,1)S(1)} %copy-done.9, ...), custom_call_target="tpu_custom_call", output_to_operand_aliasing={{1}: (5, {})} | custom-call | tf_op jit(solution)/shard_map/forward/pallas_call | solution.py:400
  33.5 0.9 %collective-permute-done.3.rest_0_ = bf16[560,128]{1,0:T(8,128)(2,1)S(1)} collective-permute-done((bf16[560,128]{1,0:T(8,128)(2,1)S(1)}, bf16[560,128]{1,0:T(8,128)(2,1)S(1)}, u32[]{:S(2)}, u32[]{:S(2)}) %collective-permute-start.3) | collective-permute-done | bytes 143392 | tf_op jit(solution)/shard_map/ppermute | solution.py:539
  34.4 1.1 %forward.15 = (f32[1024,128]{1,0:T(8,128)S(1)}, f32[10,1024,128]{2,1,0:T(8,128)S(1)}) custom-call(s32[1]{0:T(128)} %bitcast.me.refs_0_.me_ref, bf16[2,512,256]{2,1,0:T(8,128)(2,1)S(1)} %copy-done.5, f32[512,128]{1,0:T(8,128)S(1)} %copy-done.1, bf16[16,256]{1,0:T(8,128)(2,1)S(1)} %copy-done.9, ...), custom_call_target="tpu_custom_call", output_to_operand_aliasing={{1}: (5, {})} | custom-call | tf_op jit(solution)/shard_map/forward/pallas_call | solution.py:400
  35.5 1.6 %back.8.refs_8_ = bf16[528,128]{1,0:T(8,128)(2,1)S(1)} custom-call(s32[1]{0:T(128)} %bitcast.me.refs_0_.me_ref, f32[10,1024,128]{2,1,0:T(8,128)S(1)} %get-tuple-element.70.filt, bf16[2,256,512]{2,1,0:T(8,128)(2,1)S(1)} %copy-done.3, f32[512,128]{1,0:T(8,128)S(1)} %copy-done.1, f32[1024,128]{1,0:T(8,128)S(1)} %get-tuple-element.50.rest_2_.refs_0_, ...), custom_call_target="tpu_custom_call" | custom-call | tf_op jit(solution)/shard_map/back/pallas_call | solution.py:470
  37.1 6.2 %collective-permute-start.9 = (bf16[528,128]{1,0:T(8,128)(2,1)S(1)}, bf16[528,128]{1,0:T(8,128)(2,1)S(1)}, u32[]{:S(2)}, u32[]{:S(2)}) collective-permute-start(bf16[528,128]{1,0:T(8,128)(2,1)S(1)} %back.8.refs_8_), channel_id=1, source_target_pairs={{0,16},{4,20},{8,24},{12,28},{16,0},{20,4},{24,8},{28,12},{1,17},{... | collective-permute-start | bytes 405512 | tf_op jit(solution)/shard_map/ppermute | solution.py:539
  43.4 1.4 %back.9.refs_8_ = bf16[528,128]{1,0:T(8,128)(2,1)S(1)} custom-call(s32[1]{0:T(128)} %bitcast.me.refs_0_.me_ref, f32[10,1024,128]{2,1,0:T(8,128)S(1)} %get-tuple-element.70.filt, bf16[2,256,512]{2,1,0:T(8,128)(2,1)S(1)} %copy-done.3, f32[512,128]{1,0:T(8,128)S(1)} %copy-done.1, f32[1024,128]{1,0:T(8,128)S(1)} %get-tuple-element.50.rest_2_.refs_0_, ...), custom_call_target="tpu_custom_call" | custom-call | tf_op jit(solution)/shard_map/back/pallas_call | solution.py:470
  44.8 0.1 collective-permute-start.8
  44.9 1.4 %back.10.refs_8_ = bf16[528,128]{1,0:T(8,128)(2,1)S(1)} custom-call(s32[1]{0:T(128)} %bitcast.me.refs_0_.me_ref, f32[10,1024,128]{2,1,0:T(8,128)S(1)} %get-tuple-element.70.filt, bf16[2,256,512]{2,1,0:T(8,128)(2,1)S(1)} %copy-done.3, f32[512,128]{1,0:T(8,128)S(1)} %copy-done.1, f32[1024,128]{1,0:T(8,128)S(1)} %get-tuple-element.50.rest_2_.refs_0_, ...), custom_call_target="tpu_custom_call" | custom-call | tf_op jit(solution)/shard_map/back/pallas_call | solution.py:470
  46.3 1.5 %back.11.refs_8_ = bf16[528,128]{1,0:T(8,128)(2,1)S(1)} custom-call(s32[1]{0:T(128)} %bitcast.me.refs_0_.me_ref, f32[10,1024,128]{2,1,0:T(8,128)S(1)} %get-tuple-element.70.filt, bf16[2,256,512]{2,1,0:T(8,128)(2,1)S(1)} %copy-done.3, f32[512,128]{1,0:T(8,128)S(1)} %copy-done.1, f32[1024,128]{1,0:T(8,128)S(1)} %get-tuple-element.50.rest_2_.refs_0_, ...), custom_call_target="tpu_custom_call" | custom-call | tf_op jit(solution)/shard_map/back/pallas_call | solution.py:470
  47.8 1.4 %back.12.refs_8_ = bf16[528,128]{1,0:T(8,128)(2,1)S(1)} custom-call(s32[1]{0:T(128)} %bitcast.me.refs_0_.me_ref, f32[10,1024,128]{2,1,0:T(8,128)S(1)} %get-tuple-element.70.filt, bf16[2,256,512]{2,1,0:T(8,128)(2,1)S(1)} %copy-done.3, f32[512,128]{1,0:T(8,128)S(1)} %copy-done.1, f32[1024,128]{1,0:T(8,128)S(1)} %get-tuple-element.50.rest_2_.refs_0_, ...), custom_call_target="tpu_custom_call" | custom-call | tf_op jit(solution)/shard_map/back/pallas_call | solution.py:470
  49.3 1.4 %back.13.refs_0_.refs_7_ = bf16[528,128]{1,0:T(8,128)(2,1)S(1)} custom-call(s32[1]{0:T(128)} %bitcast.me.refs_0_.me_ref, f32[10,1024,128]{2,1,0:T(8,128)S(1)} %get-tuple-element.70.filt, bf16[2,256,512]{2,1,0:T(8,128)(2,1)S(1)} %copy-done.3, f32[512,128]{1,0:T(8,128)S(1)} %copy-done.1, f32[1024,128]{1,0:T(8,128)S(1)} %get-tuple-element.50.rest_2_.refs_0_, ...), custom_call_target="tpu_custom_call" | custom-call | tf_op jit(solution)/shard_map/back/pallas_call | solution.py:470
  50.7 2.3 %collective-permute-start.12 = (bf16[528,128]{1,0:T(8,128)(2,1)S(1)}, bf16[528,128]{1,0:T(8,128)(2,1)S(1)}, u32[]{:S(2)}, u32[]{:S(2)}) collective-permute-start(bf16[528,128]{1,0:T(8,128)(2,1)S(1)} %back.12.refs_8_), channel_id=1, source_target_pairs={{0,12},{4,8},{8,4},{12,0},{16,28},{20,24},{24,20},{28,16},{1,13},{... | collective-permute-start | bytes 405512 | tf_op jit(solution)/shard_map/ppermute | solution.py:539
  53.0 1.3 %collective-permute-start.14 = (bf16[528,128]{1,0:T(8,128)(2,1)S(1)}, bf16[528,128]{1,0:T(8,128)(2,1)S(1)}, u32[]{:S(2)}, u32[]{:S(2)}) collective-permute-start(bf16[528,128]{1,0:T(8,128)(2,1)S(1)} %back.11.refs_8_), channel_id=1, source_target_pairs={{0,28},{4,24},{8,20},{12,16},{16,12},{20,8},{24,4},{28,0},{1,29},{... | collective-permute-start | bytes 405512 | tf_op jit(solution)/shard_map/ppermute | solution.py:539
  54.3 2.0 %collective-permute-start.13 = (bf16[528,128]{1,0:T(8,128)(2,1)S(1)}, bf16[528,128]{1,0:T(8,128)(2,1)S(1)}, u32[]{:S(2)}, u32[]{:S(2)}) collective-permute-start(bf16[528,128]{1,0:T(8,128)(2,1)S(1)} %back.10.refs_8_), channel_id=1, source_target_pairs={{0,24},{4,28},{8,16},{12,20},{16,8},{20,12},{24,0},{28,4},{1,25},{... | collective-permute-start | bytes 405512 | tf_op jit(solution)/shard_map/ppermute | solution.py:539
  56.2 0.5 final.6.refs_8_.refs_5_
  56.7 1.4 %back.14.refs_6_ = bf16[528,128]{1,0:T(8,128)(2,1)S(1)} custom-call(s32[1]{0:T(128)} %bitcast.me.refs_0_.me_ref, f32[10,1024,128]{2,1,0:T(8,128)S(1)} %get-tuple-element.70.filt, bf16[2,256,512]{2,1,0:T(8,128)(2,1)S(1)} %copy-done.3, f32[512,128]{1,0:T(8,128)S(1)} %copy-done.1, f32[1024,128]{1,0:T(8,128)S(1)} %get-tuple-element.50.rest_2_.refs_0_, ...), custom_call_target="tpu_custom_call" | custom-call | tf_op jit(solution)/shard_map/back/pallas_call | solution.py:470
  58.2 0.1 collective-permute-start.11
  58.3 0.2 final.7.refs_8_.refs_7_
  58.5 1.4 %back.15.refs_8_ = bf16[528,128]{1,0:T(8,128)(2,1)S(1)} custom-call(s32[1]{0:T(128)} %bitcast.me.refs_0_.me_ref, f32[10,1024,128]{2,1,0:T(8,128)S(1)} %get-tuple-element.70.filt, bf16[2,256,512]{2,1,0:T(8,128)(2,1)S(1)} %copy-done.3, f32[512,128]{1,0:T(8,128)S(1)} %copy-done.1, f32[1024,128]{1,0:T(8,128)S(1)} %get-tuple-element.50.rest_2_.refs_0_, ...), custom_call_target="tpu_custom_call" | custom-call | tf_op jit(solution)/shard_map/back/pallas_call | solution.py:470
  59.9 0.5 collective-permute-start.10
  60.4 0.4 collective-permute-done.14.refs_1_
  60.9 4.0 %collective-permute-done.13.refs_0_ = bf16[528,128]{1,0:T(8,128)(2,1)S(1)} collective-permute-done((bf16[528,128]{1,0:T(8,128)(2,1)S(1)}, bf16[528,128]{1,0:T(8,128)(2,1)S(1)}, u32[]{:S(2)}, u32[]{:S(2)}) %collective-permute-start.13) | collective-permute-done | bytes 135200 | tf_op jit(solution)/shard_map/ppermute | solution.py:539
  64.8 0.5 final.8.refs_6_
  65.3 0.1 copy.34.refs_5_
  65.4 0.2 final.9.refs_6_
  65.6 0.1 copy.35.refs_5_
  65.7 1.8 %collective-permute-done.11.refs_0_ = bf16[528,128]{1,0:T(8,128)(2,1)S(1)} collective-permute-done((bf16[528,128]{1,0:T(8,128)(2,1)S(1)}, bf16[528,128]{1,0:T(8,128)(2,1)S(1)}, u32[]{:S(2)}, u32[]{:S(2)}) %collective-permute-start.11) | collective-permute-done | bytes 135200 | tf_op jit(solution)/shard_map/ppermute | solution.py:539
  67.4 0.2 final.10.refs_6_
  67.7 1.0 %copy.36.refs_5_ = bf16[512,1024]{1,0:T(8,128)(2,1)} copy(bf16[512,1024]{1,0:T(8,128)(2,1)S(1)} %final.10.refs_6_) | data formatting | bytes 2097152
  68.7 0.8 %final.11 = bf16[512,1024]{1,0:T(8,128)(2,1)} custom-call(s32[1]{0:T(128)} %bitcast.me.refs_0_.me_ref, bf16[528,128]{1,0:T(8,128)(2,1)S(1)} %collective-permute-done.10.refs_0_, f32[128,128]{1,0:T(8,128)S(1)} %get-tuple-element.53.rest_2_.refs_1_, f32[384,1024]{1,0:T(8,128)S(1)} %get-tuple-element.39.refs_4_.refs_9_.refs_2_, ...), custom_call_target="tpu_custom_call", output_to_operand_aliasing={{}: (6, {})} | custom-call | tf_op jit(solution)/shard_map/final/pallas_call | solution.py:515
  (25 shorter events, 0.1 us)
Async XLA Ops:
  1.0 7.7 %collective-permute-start = (bf16[128,1024]{1,0:T(8,128)(2,1)S(1)}, bf16[128,1024]{1,0:T(8,128)(2,1)S(1)}, u32[]{:S(2)}, u32[]{:S(2)}) collective-permute-start(bf16[128,1024]{1,0:T(8,128)(2,1)S(1)} %slice.3), channel_id=1, source_target_pairs={{0,4},{4,8},{8,12},{12,16},{16,20},{20,24},{24,28},{1,5},{5,9},{9,... | collective-permute-start | bytes 786440 | tf_op jit(solution)/shard_map/ppermute | solution.py:24
  3.4 1.2 %copy-start = (bf16[512,1024]{1,0:T(8,128)(2,1)S(1)}, bf16[512,1024]{1,0:T(8,128)(2,1)}, u32[]{:S(2)}) copy-start(bf16[512,1024]{1,0:T(8,128)(2,1)} %refs_2_.15) | copy-start | bytes 3145732
  3.4 1.5 %copy-start.2 = (bf16[512,1024]{1,0:T(8,128)(2,1)S(1)}, bf16[512,1024]{1,0:T(8,128)(2,1)}, u32[]{:S(2)}) copy-start(bf16[512,1024]{1,0:T(8,128)(2,1)} %refs_3_.19) | copy-start | bytes 3145732
  3.4 1.6 %copy-start.6 = (bf16[2,256,256]{2,1,0:T(8,128)(2,1)S(1)}, bf16[2,256,256]{2,1,0:T(8,128)(2,1)}, u32[]{:S(2)}) copy-start(bf16[2,256,256]{2,1,0:T(8,128)(2,1)} %constant.18.clone.refs_4_.refs_7_) | copy-start | bytes 786436
  3.4 1.6 %copy-start.7 = (bf16[2,128,256]{2,1,0:T(8,128)(2,1)S(1)}, bf16[2,128,256]{2,1,0:T(8,128)(2,1)}, u32[]{:S(2)}) copy-start(bf16[2,128,256]{2,1,0:T(8,128)(2,1)} %constant.19.clone.refs_5_.refs_8_) | copy-start | bytes 393220
  3.4 1.7 %copy-start.10 = (f32[128,1024]{1,0:T(8,128)S(1)}, f32[128,1024]{1,0:T(8,128)}, u32[]{:S(2)}) copy-start(f32[128,1024]{1,0:T(8,128)} %refs_3_.12) | copy-start | bytes 1572868
  3.4 5.2 %copy-start.8 = (f32[512,64]{0,1:T(8,128)S(1)}, f32[512,64]{0,1:T(8,128)}, u32[]{:S(2)}) copy-start(f32[512,64]{0,1:T(8,128)} %param.16) | copy-start | bytes 393220
  9.2 13.6 %collective-permute-start.2 = (bf16[560,128]{1,0:T(8,128)(2,1)S(1)}, bf16[560,128]{1,0:T(8,128)(2,1)S(1)}, u32[]{:S(2)}, u32[]{:S(2)}) collective-permute-start(bf16[560,128]{1,0:T(8,128)(2,1)S(1)} %get-tuple-element.43), channel_id=1, source_target_pairs={{0,16},{4,20},{8,24},{12,28},{16,0},{20,4},{24,8},{28,12},{1,17},{... | collective-permute-start | bytes 430088 | tf_op jit(solution)/shard_map/ppermute | solution.py:539
  13.8 11.4 %collective-permute-start.1 = (bf16[560,128]{1,0:T(8,128)(2,1)S(1)}, bf16[560,128]{1,0:T(8,128)(2,1)S(1)}, u32[]{:S(2)}, u32[]{:S(2)}) collective-permute-start(bf16[560,128]{1,0:T(8,128)(2,1)S(1)} %get-tuple-element.42), channel_id=1, source_target_pairs={{0,8},{4,12},{8,0},{12,4},{16,24},{20,28},{24,16},{28,20},{1,9},{5... | collective-permute-start | bytes 430088 | tf_op jit(solution)/shard_map/ppermute | solution.py:539
  15.9 12.3 %collective-permute-start.7 = (bf16[560,128]{1,0:T(8,128)(2,1)S(1)}, bf16[560,128]{1,0:T(8,128)(2,1)S(1)}, u32[]{:S(2)}, u32[]{:S(2)}) collective-permute-start(bf16[560,128]{1,0:T(8,128)(2,1)S(1)} %get-tuple-element.59), channel_id=1, source_target_pairs={{0,12},{4,8},{8,4},{12,0},{16,28},{20,24},{24,20},{28,16},{1,13},{... | collective-permute-start | bytes 430088 | tf_op jit(solution)/shard_map/ppermute | solution.py:539
  16.7 4.8 %copy-start.1 = (f32[512,128]{1,0:T(8,128)S(1)}, f32[512,128]{1,0:T(8,128)}, u32[]{:S(2)}) copy-start(f32[512,128]{1,0:T(8,128)} %constant.22.clone.turn) | copy-start | bytes 786436
  16.7 4.8 %copy-start.3 = (bf16[2,256,512]{2,1,0:T(8,128)(2,1)S(1)}, bf16[2,256,512]{2,1,0:T(8,128)(2,1)}, u32[]{:S(2)}) copy-start(bf16[2,256,512]{2,1,0:T(8,128)(2,1)} %constant.21.clone.rest_1_.inv) | copy-start | bytes 1572868
  16.7 4.8 %copy-start.5 = (bf16[2,512,256]{2,1,0:T(8,128)(2,1)S(1)}, bf16[2,512,256]{2,1,0:T(8,128)(2,1)}, u32[]{:S(2)}) copy-start(bf16[2,512,256]{2,1,0:T(8,128)(2,1)} %constant.20.clone.fwd) | copy-start | bytes 1572868
  16.7 4.8 %copy-start.9 = (bf16[16,256]{1,0:T(8,128)(2,1)S(1)}, bf16[16,256]{1,0:T(8,128)(2,1)}, u32[]{:S(2)}) copy-start(bf16[16,256]{1,0:T(8,128)(2,1)} %constant.23.clone.widen) | copy-start | bytes 24580
  17.2 12.1 %collective-permute-start.6 = (bf16[560,128]{1,0:T(8,128)(2,1)S(1)}, bf16[560,128]{1,0:T(8,128)(2,1)S(1)}, u32[]{:S(2)}, u32[]{:S(2)}) collective-permute-start(bf16[560,128]{1,0:T(8,128)(2,1)S(1)} %get-tuple-element.58), channel_id=1, source_target_pairs={{0,20},{4,16},{8,28},{12,24},{16,4},{20,0},{24,12},{28,8},{1,21},{... | collective-permute-start | bytes 430088 | tf_op jit(solution)/shard_map/ppermute | solution.py:539
  18.1 13.3 %collective-permute-start.5 = (bf16[560,128]{1,0:T(8,128)(2,1)S(1)}, bf16[560,128]{1,0:T(8,128)(2,1)S(1)}, u32[]{:S(2)}, u32[]{:S(2)}) collective-permute-start(bf16[560,128]{1,0:T(8,128)(2,1)S(1)} %get-tuple-element.57), channel_id=1, source_target_pairs={{0,24},{4,28},{8,16},{12,20},{16,8},{20,12},{24,0},{28,4},{1,25},{... | collective-permute-start | bytes 430088 | tf_op jit(solution)/shard_map/ppermute | solution.py:539
  24.4 8.1 %collective-permute-start.4 = (bf16[560,128]{1,0:T(8,128)(2,1)S(1)}, bf16[560,128]{1,0:T(8,128)(2,1)S(1)}, u32[]{:S(2)}, u32[]{:S(2)}) collective-permute-start(bf16[560,128]{1,0:T(8,128)(2,1)S(1)} %get-tuple-element.56), channel_id=1, source_target_pairs={{0,4},{4,0},{8,12},{12,8},{16,20},{20,16},{24,28},{28,24},{1,5},{5... | collective-permute-start | bytes 430088 | tf_op jit(solution)/shard_map/ppermute | solution.py:539
  26.7 7.7 %collective-permute-start.3 = (bf16[560,128]{1,0:T(8,128)(2,1)S(1)}, bf16[560,128]{1,0:T(8,128)(2,1)S(1)}, u32[]{:S(2)}, u32[]{:S(2)}) collective-permute-start(bf16[560,128]{1,0:T(8,128)(2,1)S(1)} %get-tuple-element.55), channel_id=1, source_target_pairs={{0,28},{4,24},{8,20},{12,16},{16,12},{20,8},{24,4},{28,0},{1,29},{... | collective-permute-start | bytes 430088 | tf_op jit(solution)/shard_map/ppermute | solution.py:539
  37.1 19.1 %collective-permute-start.9 = (bf16[528,128]{1,0:T(8,128)(2,1)S(1)}, bf16[528,128]{1,0:T(8,128)(2,1)S(1)}, u32[]{:S(2)}, u32[]{:S(2)}) collective-permute-start(bf16[528,128]{1,0:T(8,128)(2,1)S(1)} %back.8.refs_8_), channel_id=1, source_target_pairs={{0,16},{4,20},{8,24},{12,28},{16,0},{20,4},{24,8},{28,12},{1,17},{... | collective-permute-start | bytes 405512 | tf_op jit(solution)/shard_map/ppermute | solution.py:539
  44.8 13.4 %collective-permute-start.8 = (bf16[528,128]{1,0:T(8,128)(2,1)S(1)}, bf16[528,128]{1,0:T(8,128)(2,1)S(1)}, u32[]{:S(2)}, u32[]{:S(2)}) collective-permute-start(bf16[528,128]{1,0:T(8,128)(2,1)S(1)} %back.9.refs_8_), channel_id=1, source_target_pairs={{0,20},{4,16},{8,28},{12,24},{16,4},{20,0},{24,12},{28,8},{1,21},{... | collective-permute-start | bytes 405512 | tf_op jit(solution)/shard_map/ppermute | solution.py:539
  49.3 7.0 %copy-start.4 = (bf16[512,1024]{1,0:T(8,128)(2,1)S(1)}, bf16[512,1024]{1,0:T(8,128)(2,1)}, u32[]{:S(2)}) copy-start(bf16[512,1024]{1,0:T(8,128)(2,1)} %refs_3_.23) | copy-start | bytes 3145732
  49.3 7.0 %copy-start.11 = (f32[1024]{0:T(1024)S(1)}, f32[1024]{0:T(1024)}, u32[]{:S(2)}) copy-start(f32[1024]{0:T(1024)} %param.17) | copy-start | bytes 12292
  50.7 14.6 %collective-permute-start.12 = (bf16[528,128]{1,0:T(8,128)(2,1)S(1)}, bf16[528,128]{1,0:T(8,128)(2,1)S(1)}, u32[]{:S(2)}, u32[]{:S(2)}) collective-permute-start(bf16[528,128]{1,0:T(8,128)(2,1)S(1)} %back.12.refs_8_), channel_id=1, source_target_pairs={{0,12},{4,8},{8,4},{12,0},{16,28},{20,24},{24,20},{28,16},{1,13},{... | collective-permute-start | bytes 405512 | tf_op jit(solution)/shard_map/ppermute | solution.py:539
  53.0 7.9 %collective-permute-start.14 = (bf16[528,128]{1,0:T(8,128)(2,1)S(1)}, bf16[528,128]{1,0:T(8,128)(2,1)S(1)}, u32[]{:S(2)}, u32[]{:S(2)}) collective-permute-start(bf16[528,128]{1,0:T(8,128)(2,1)S(1)} %back.11.refs_8_), channel_id=1, source_target_pairs={{0,28},{4,24},{8,20},{12,16},{16,12},{20,8},{24,4},{28,0},{1,29},{... | collective-permute-start | bytes 405512 | tf_op jit(solution)/shard_map/ppermute | solution.py:539
  54.3 10.6 %collective-permute-start.13 = (bf16[528,128]{1,0:T(8,128)(2,1)S(1)}, bf16[528,128]{1,0:T(8,128)(2,1)S(1)}, u32[]{:S(2)}, u32[]{:S(2)}) collective-permute-start(bf16[528,128]{1,0:T(8,128)(2,1)S(1)} %back.10.refs_8_), channel_id=1, source_target_pairs={{0,24},{4,28},{8,16},{12,20},{16,8},{20,12},{24,0},{28,4},{1,25},{... | collective-permute-start | bytes 405512 | tf_op jit(solution)/shard_map/ppermute | solution.py:539
  58.2 9.3 %collective-permute-start.11 = (bf16[528,128]{1,0:T(8,128)(2,1)S(1)}, bf16[528,128]{1,0:T(8,128)(2,1)S(1)}, u32[]{:S(2)}, u32[]{:S(2)}) collective-permute-start(bf16[528,128]{1,0:T(8,128)(2,1)S(1)} %back.14.refs_6_), channel_id=1, source_target_pairs={{0,8},{4,12},{8,0},{12,4},{16,24},{20,28},{24,16},{28,20},{1,9},{5... | collective-permute-start | bytes 405512 | tf_op jit(solution)/shard_map/ppermute | solution.py:539
  59.9 8.7 %collective-permute-start.10 = (bf16[528,128]{1,0:T(8,128)(2,1)S(1)}, bf16[528,128]{1,0:T(8,128)(2,1)S(1)}, u32[]{:S(2)}, u32[]{:S(2)}) collective-permute-start(bf16[528,128]{1,0:T(8,128)(2,1)S(1)} %back.15.refs_8_), channel_id=1, source_target_pairs={{0,4},{4,0},{8,12},{12,8},{16,20},{20,16},{24,28},{28,24},{1,5},{5... | collective-permute-start | bytes 405512 | tf_op jit(solution)/shard_map/ppermute | solution.py:539

commit v3 on v2

--- a/solution.py
+++ b/solution.py
@@ -11,7 +11,7 @@
 
 HIGHEST = lax.Precision.HIGHEST
 LANES = 128
-TILE = 16
+TILE = 8
 SPAN = 250.0
 BIAS = 125.0
 TINY = 1e-30
@@ -265,7 +265,7 @@
         start += v.shape[0]
     scale = jnp.broadcast_to(scale, (groups, LANES))
     if filter_rows is None:
-        both = jnp.concatenate([scale, scale], 0)
+        both = scale
     else:
         size = jnp.abs(filter_rows)
         many = filter_rows.shape[0] // groups
@@ -274,9 +274,13 @@
             most = jnp.maximum(most, size[c * groups : (c + 1) * groups])
         filter_scale = scale_of(jnp.max(most, axis=1, keepdims=True))
         filter_scale = jnp.broadcast_to(filter_scale, (groups, LANES))
-        both = jnp.concatenate([scale, filter_scale], 0)
-        code[rows + TILE :] = to_code(filter_rows, jnp.concatenate([filter_scale] * many, 0))
-    code[rows : rows + TILE] = both.astype(jnp.bfloat16)
+        row, lane = (lax.broadcasted_iota(jnp.int32, scale.shape, k) for k in (0, 1))
+        by_lane = jnp.sum(jnp.where(row == lane, filter_scale, 0.0), axis=0, keepdims=True)
+        both = jnp.where(row == groups - 1, by_lane, scale)
+        end = rows + filter_rows.shape[0]
+        code[rows:end] = to_code(filter_rows, jnp.concatenate([filter_scale] * many, 0))
+        rows = end
+    code[rows:] = both.astype(jnp.bfloat16)
 
 
 def ahead_body(part, me, value, gate, taps, long_taps, fwd, inv, *codes):
@@ -345,12 +349,15 @@
     groups = 8
     end = rows
     for code, length in zip(rest, pieces):
-        scales = code[length : length + TILE].astype(jnp.float32)
+        scales = code[code.shape[0] - TILE :].astype(jnp.float32)
         held_x[end - length : end] = from_code(code[:length], scales[:1])
         end -= length
     code, length = rest[0], pieces[0]
-    scale = code[length : length + TILE].astype(jnp.float32)[groups:]
-    taps = code[length + TILE :]
+    scales = code[code.shape[0] - TILE :].astype(jnp.float32)
+    row, lane = (lax.broadcasted_iota(jnp.int32, scales.shape, k) for k in (0, 1))
+    by_lane = jnp.where(row == lane, scales[groups - 1 :], 0.0)
+    scale = jnp.broadcast_to(jnp.sum(by_lane, axis=1, keepdims=True), scales.shape)
+    taps = code[length : code.shape[0] - TILE]
     many = taps.shape[0] // groups
     h_high, h_low = split(from_code(taps, jnp.concatenate([scale] * many, 0)))
     h_high, h_low = h_high.astype(jnp.float32), h_low.astype(jnp.float32)
@@ -511,11 +518,11 @@
     if so_far:
         alias = {len(args): 0}
     args += so_far + after
-    specs += [IN_ANY] * len(so_far + after)
+    specs += [IN_HBM] * len(so_far) + [IN_ANY] * len(after)
     return pl.pallas_call(
         functools.partial(final_body, part, count),
         in_specs=specs,
-        out_specs=IN_ANY,
+        out_specs=IN_HBM,
         out_shape=jax.ShapeDtypeStruct(gate.shape, jnp.bfloat16),
         scratch_shapes=[
             pltpu.VMEM((many, rows, LANES), jnp.bfloat16),
@@ -635,10 +642,8 @@
     backs(2)
     finals(5)
     backs(1)
-    finals(6, 7)
-    finals(3)
-    finals(2)
-    finals(1)
+    finals(6)
+    finals(7, 3, 2, 1)
     return mixed[0]
 
 
@@ -648,7 +653,7 @@
     taps = short_filter.shape[0]
     groups = long_filter.shape[1]
     fits = chans == LANES * count and groups == 8 * count and taps == LANES
-    fits = fits and rows % taps == 0 and rows > taps
+    fits = fits and rows % (2 * LANES) == 0 and rows > taps and count & (count - 1) == 0
     run = in_slabs if fits else plain
     return run(output_gate, input_gate, value_input, short_filter, long_filter, skip_gain)
 

time: 69.8 us -> 68.4 us (0.980)
  waiting for transfers between devices: 9.57 us -> 8.45 us
    ppermute x14, waiting for transfers between devices: 9.56 us -> 8.45 us  [exchanged(): lax.ppermute(block, 'ctx', [(i, i ^ d) for i in range(count)])]
    pallas_call x6 -> x4, Pallas kernels: 2.41 us -> 2.12 us  [final_call(): pl.pallas_call(functools.partial(final_body, part, count), in_specs=specs...]
    unnamed x27 -> x25, local copies, waits for them, and re-layouts: 2.36 us -> 2.22 us
  transfers between devices with their start and end apart: 15 -> 15, of which waited for: 7 -> 6; matrix products, arithmetic and copies ran while one was open for 2% -> 1% of each run, Pallas kernels for 38% -> 39%
where the time goes in v3:
time: 68.4 us; the launch traced here: 68.2 us
  Pallas kernels  30.7 us (45%)
  starting transfers between devices  25.3 us (37%)
  waiting for transfers between devices  8.45 us (12%)
  local copies, waits for them, and re-layouts  3.19 us (5%)
    ppermute x14, starting transfers between devices, exchanged(): lax.ppermute(block, 'ctx', [(i, i ^ d) for i in range(count)])  22.9 us
    pallas_call x8, Pallas kernels, back_call(): pl.pallas_call(functools.partial(back_body, part, count), in_specs=[IN_SM...  11.7 us
    pallas_call x8, Pallas kernels, forward_call(): pl.pallas_call(functools.partial(forward_body, d, not so_far, pieces), in...  9.21 us
    ppermute x14, waiting for transfers between devices, exchanged(): lax.ppermute(block, 'ctx', [(i, i ^ d) for i in range(count)])  8.45 us
    pallas_call x7, Pallas kernels, head_call(): pl.pallas_call(drop_after(functools.partial(head_body, part, ahead), 9, l...  3.73 us
    pallas_call x1, Pallas kernels, main_call(): pl.pallas_call(drop_after(main_body, 6, len(after)), in_specs=[IN_SMEM] +...  3.49 us
    ppermute x1, starting transfers between devices, passed_along(): return lax.ppermute(block, axis, route)  2.37 us
    unnamed x25, local copies, waits for them, and re-layouts  2.22 us
  transfers between devices with their start and end apart: 15, of which 6 were waited for; matrix products, arithmetic and copies ran while one was open for 1% of the time, Pallas kernels for 39%

profile of v3, /device:TPU:0, one launch (start us, length us, event | category | flops | bytes accessed | tf_op | source)
XLA Modules:
  0.0 68.2 jit_solution(17575518953506757442)
XLA Ops:
  0.0 1.0 %slice.3 = bf16[128,1024]{1,0:T(8,128)(2,1)S(1)} slice(bf16[512,1024]{1,0:T(8,128)(2,1)} %refs_2_.15), slice={[384:512], [0:1024]} | slice | bytes 524288 | tf_op jit(solution)/shard_map/slice | solution.py:551
  1.0 2.4 %collective-permute-start = (bf16[128,1024]{1,0:T(8,128)(2,1)S(1)}, bf16[128,1024]{1,0:T(8,128)(2,1)S(1)}, u32[]{:S(2)}, u32[]{:S(2)}) collective-permute-start(bf16[128,1024]{1,0:T(8,128)(2,1)S(1)} %slice.3), channel_id=1, source_target_pairs={{0,4},{4,8},{8,12},{12,16},{16,20},{20,24},{24,28},{1,5},{5,9},{9,... | collective-permute-start | bytes 786440 | tf_op jit(solution)/shard_map/ppermute | solution.py:24
  3.4 0.0 copy-start
  3.4 0.0 copy-start.2
  3.4 0.0 copy-start.5
  3.4 0.0 copy-start.7
  3.4 0.0 copy-start.10
  3.4 0.0 copy-start.8
  3.4 0.5 pace.1.refs_0_
  4.0 0.6 copy-done
  4.6 0.3 copy-done.2
  4.9 0.0 copy-done.5
  4.9 0.0 copy-done.7
  5.0 0.2 copy-done.10
  5.2 3.5 %short_main.1 = (f32[384,1024]{1,0:T(8,128)S(1)}, f32[256,1024]{1,0:T(8,128)S(1)}) custom-call(s32[1]{0:T(128)} %pace.1.refs_0_, bf16[512,1024]{1,0:T(8,128)(2,1)S(1)} %copy-done, bf16[512,1024]{1,0:T(8,128)(2,1)S(1)} %copy-done.2, f32[128,1024]{1,0:T(8,128)S(1)} %copy-done.10, bf16[2,256,256]{2,1,0:T(8,128)(2,1)S(1)} %copy-done.5, ...), custom_call_target="tpu_custom_call" | custom-call | tf_op jit(solution)/shard_map/short_main/pallas_call | solution.py:237
  8.7 0.5 short_head.7
  9.2 4.1 %collective-permute-start.2 = (bf16[552,128]{1,0:T(8,128)(2,1)S(1)}, bf16[552,128]{1,0:T(8,128)(2,1)S(1)}, u32[]{:S(2)}, u32[]{:S(2)}) collective-permute-start(bf16[552,128]{1,0:T(8,128)(2,1)S(1)} %get-tuple-element.43), channel_id=1, source_target_pairs={{0,16},{4,20},{8,24},{12,28},{16,0},{20,4},{24,8},{28,12},{1,17},{... | collective-permute-start | bytes 423944 | tf_op jit(solution)/shard_map/ppermute | solution.py:546
  13.3 0.5 short_head.8
  13.8 1.6 %collective-permute-start.1 = (bf16[552,128]{1,0:T(8,128)(2,1)S(1)}, bf16[552,128]{1,0:T(8,128)(2,1)S(1)}, u32[]{:S(2)}, u32[]{:S(2)}) collective-permute-start(bf16[552,128]{1,0:T(8,128)(2,1)S(1)} %get-tuple-element.42), channel_id=1, source_target_pairs={{0,8},{4,12},{8,0},{12,4},{16,24},{20,28},{24,16},{28,20},{1,9},{5... | collective-permute-start | bytes 423944 | tf_op jit(solution)/shard_map/ppermute | solution.py:546
  15.4 0.5 short_head.9
  15.9 0.8 %collective-permute-start.7 = (bf16[552,128]{1,0:T(8,128)(2,1)S(1)}, bf16[552,128]{1,0:T(8,128)(2,1)S(1)}, u32[]{:S(2)}, u32[]{:S(2)}) collective-permute-start(bf16[552,128]{1,0:T(8,128)(2,1)S(1)} %get-tuple-element.59), channel_id=1, source_target_pairs={{0,12},{4,8},{8,4},{12,0},{16,28},{20,24},{24,20},{28,16},{1,13},{... | collective-permute-start | bytes 423944 | tf_op jit(solution)/shard_map/ppermute | solution.py:546
  16.7 0.5 short_head.10
  17.2 0.1 collective-permute-start.6
  17.3 0.8 %short_head.11 = (f32[128,128]{1,0:T(8,128)S(1)}, f32[128,128]{1,0:T(8,128)S(1)}, bf16[552,128]{1,0:T(8,128)(2,1)S(1)}, bf16[552,128]{1,0:T(8,128)(2,1)S(1)}) custom-call(s32[1]{0:T(128)} %bitcast.me.refs_0_.me_ref, bf16[128,1024]{1,0:T(8,128)(2,1)S(1)} %collective-permute-done.refs_1_, bf16[512,1024]{1,0:T(8,128)(2,1)S(1)} %copy-done, ...), custom_call_target="tpu_custom_call" | custom-call | tf_op jit(solution)/shard_map/short_head/pallas_call | solution.py:334
  18.1 3.4 %collective-permute-start.5 = (bf16[552,128]{1,0:T(8,128)(2,1)S(1)}, bf16[552,128]{1,0:T(8,128)(2,1)S(1)}, u32[]{:S(2)}, u32[]{:S(2)}) collective-permute-start(bf16[552,128]{1,0:T(8,128)(2,1)S(1)} %get-tuple-element.57), channel_id=1, source_target_pairs={{0,24},{4,28},{8,16},{12,20},{16,8},{20,12},{24,0},{28,4},{1,25},{... | collective-permute-start | bytes 423944 | tf_op jit(solution)/shard_map/ppermute | solution.py:546
  21.5 1.3 %forward.8 = (f32[1024,128]{1,0:T(8,128)S(1)}, f32[10,1024,128]{2,1,0:T(8,128)S(1)}) custom-call(s32[1]{0:T(128)} %bitcast.me.refs_0_.me_ref, bf16[2,512,256]{2,1,0:T(8,128)(2,1)S(1)} %copy-done.4, f32[512,128]{1,0:T(8,128)S(1)} %copy-done.1, bf16[16,256]{1,0:T(8,128)(2,1)S(1)} %copy-done.9, bf16[552,128]{1,0:T(8,128)(2,1)S(1)} %get-tuple-element.47.rest_0_, ...), custom_call_target="tpu_custom_call" | custom-call | tf_op jit(solution)/shard_map/forward/pallas_call | solution.py:407
  22.9 1.1 %forward.9 = (f32[1024,128]{1,0:T(8,128)S(1)}, f32[10,1024,128]{2,1,0:T(8,128)S(1)}) custom-call(s32[1]{0:T(128)} %bitcast.me.refs_0_.me_ref, bf16[2,512,256]{2,1,0:T(8,128)(2,1)S(1)} %copy-done.4, f32[512,128]{1,0:T(8,128)S(1)} %copy-done.1, bf16[16,256]{1,0:T(8,128)(2,1)S(1)} %copy-done.9, ...), custom_call_target="tpu_custom_call", output_to_operand_aliasing={{1}: (5, {})} | custom-call | tf_op jit(solution)/shard_map/forward/pallas_call | solution.py:407
  24.0 0.5 short_head.12
  24.5 0.1 collective-permute-start.4
  24.6 0.5 collective-permute-done.1.rest_0_
  25.0 1.1 %forward.10 = (f32[1024,128]{1,0:T(8,128)S(1)}, f32[10,1024,128]{2,1,0:T(8,128)S(1)}) custom-call(s32[1]{0:T(128)} %bitcast.me.refs_0_.me_ref, bf16[2,512,256]{2,1,0:T(8,128)(2,1)S(1)} %copy-done.4, f32[512,128]{1,0:T(8,128)S(1)} %copy-done.1, bf16[16,256]{1,0:T(8,128)(2,1)S(1)} %copy-done.9, ...), custom_call_target="tpu_custom_call", output_to_operand_aliasing={{1}: (5, {})} | custom-call | tf_op jit(solution)/shard_map/forward/pallas_call | solution.py:407
  26.2 0.5 short_head.13
  26.7 0.7 %collective-permute-start.3 = (bf16[552,128]{1,0:T(8,128)(2,1)S(1)}, bf16[552,128]{1,0:T(8,128)(2,1)S(1)}, u32[]{:S(2)}, u32[]{:S(2)}) collective-permute-start(bf16[552,128]{1,0:T(8,128)(2,1)S(1)} %get-tuple-element.55), channel_id=1, source_target_pairs={{0,28},{4,24},{8,20},{12,16},{16,12},{20,8},{24,4},{28,0},{1,29},{... | collective-permute-start | bytes 423944 | tf_op jit(solution)/shard_map/ppermute | solution.py:546
  27.4 0.7 collective-permute-done.7.rest_0_
  28.0 1.1 %forward.11 = (f32[1024,128]{1,0:T(8,128)S(1)}, f32[10,1024,128]{2,1,0:T(8,128)S(1)}) custom-call(s32[1]{0:T(128)} %bitcast.me.refs_0_.me_ref, bf16[2,512,256]{2,1,0:T(8,128)(2,1)S(1)} %copy-done.4, f32[512,128]{1,0:T(8,128)S(1)} %copy-done.1, bf16[16,256]{1,0:T(8,128)(2,1)S(1)} %copy-done.9, ...), custom_call_target="tpu_custom_call", output_to_operand_aliasing={{1}: (5, {})} | custom-call | tf_op jit(solution)/shard_map/forward/pallas_call | solution.py:407
  29.2 1.1 %forward.12 = (f32[1024,128]{1,0:T(8,128)S(1)}, f32[10,1024,128]{2,1,0:T(8,128)S(1)}) custom-call(s32[1]{0:T(128)} %bitcast.me.refs_0_.me_ref, bf16[2,512,256]{2,1,0:T(8,128)(2,1)S(1)} %copy-done.4, f32[512,128]{1,0:T(8,128)S(1)} %copy-done.1, bf16[16,256]{1,0:T(8,128)(2,1)S(1)} %copy-done.9, ...), custom_call_target="tpu_custom_call", output_to_operand_aliasing={{1}: (5, {})} | custom-call | tf_op jit(solution)/shard_map/forward/pallas_call | solution.py:407
  30.3 0.8 %collective-permute-done.5.rest_0_ = bf16[552,128]{1,0:T(8,128)(2,1)S(1)} collective-permute-done((bf16[552,128]{1,0:T(8,128)(2,1)S(1)}, bf16[552,128]{1,0:T(8,128)(2,1)S(1)}, u32[]{:S(2)}, u32[]{:S(2)}) %collective-permute-start.5) | collective-permute-done | bytes 141344 | tf_op jit(solution)/shard_map/ppermute | solution.py:546
  31.2 1.1 %forward.13 = (f32[1024,128]{1,0:T(8,128)S(1)}, f32[10,1024,128]{2,1,0:T(8,128)S(1)}) custom-call(s32[1]{0:T(128)} %bitcast.me.refs_0_.me_ref, bf16[2,512,256]{2,1,0:T(8,128)(2,1)S(1)} %copy-done.4, f32[512,128]{1,0:T(8,128)S(1)} %copy-done.1, bf16[16,256]{1,0:T(8,128)(2,1)S(1)} %copy-done.9, ...), custom_call_target="tpu_custom_call", output_to_operand_aliasing={{1}: (5, {})} | custom-call | tf_op jit(solution)/shard_map/forward/pallas_call | solution.py:407
  32.3 1.1 %forward.14 = (f32[1024,128]{1,0:T(8,128)S(1)}, f32[10,1024,128]{2,1,0:T(8,128)S(1)}) custom-call(s32[1]{0:T(128)} %bitcast.me.refs_0_.me_ref, bf16[2,512,256]{2,1,0:T(8,128)(2,1)S(1)} %copy-done.4, f32[512,128]{1,0:T(8,128)S(1)} %copy-done.1, bf16[16,256]{1,0:T(8,128)(2,1)S(1)} %copy-done.9, ...), custom_call_target="tpu_custom_call", output_to_operand_aliasing={{1}: (5, {})} | custom-call | tf_op jit(solution)/shard_map/forward/pallas_call | solution.py:407
  33.4 0.9 %collective-permute-done.3.rest_0_ = bf16[552,128]{1,0:T(8,128)(2,1)S(1)} collective-permute-done((bf16[552,128]{1,0:T(8,128)(2,1)S(1)}, bf16[552,128]{1,0:T(8,128)(2,1)S(1)}, u32[]{:S(2)}, u32[]{:S(2)}) %collective-permute-start.3) | collective-permute-done | bytes 141344 | tf_op jit(solution)/shard_map/ppermute | solution.py:546
  34.3 1.1 %forward.15 = (f32[1024,128]{1,0:T(8,128)S(1)}, f32[10,1024,128]{2,1,0:T(8,128)S(1)}) custom-call(s32[1]{0:T(128)} %bitcast.me.refs_0_.me_ref, bf16[2,512,256]{2,1,0:T(8,128)(2,1)S(1)} %copy-done.4, f32[512,128]{1,0:T(8,128)S(1)} %copy-done.1, bf16[16,256]{1,0:T(8,128)(2,1)S(1)} %copy-done.9, ...), custom_call_target="tpu_custom_call", output_to_operand_aliasing={{1}: (5, {})} | custom-call | tf_op jit(solution)/shard_map/forward/pallas_call | solution.py:407
  35.4 1.6 %back.8.refs_8_ = bf16[520,128]{1,0:T(8,128)(2,1)S(1)} custom-call(s32[1]{0:T(128)} %bitcast.me.refs_0_.me_ref, f32[10,1024,128]{2,1,0:T(8,128)S(1)} %get-tuple-element.70.filt, bf16[2,256,512]{2,1,0:T(8,128)(2,1)S(1)} %copy-done.3, f32[512,128]{1,0:T(8,128)S(1)} %copy-done.1, f32[1024,128]{1,0:T(8,128)S(1)} %get-tuple-element.50.rest_2_.refs_0_, ...), custom_call_target="tpu_custom_call" | custom-call | tf_op jit(solution)/shard_map/back/pallas_call | solution.py:477
  37.1 6.1 %collective-permute-start.10 = (bf16[520,128]{1,0:T(8,128)(2,1)S(1)}, bf16[520,128]{1,0:T(8,128)(2,1)S(1)}, u32[]{:S(2)}, u32[]{:S(2)}) collective-permute-start(bf16[520,128]{1,0:T(8,128)(2,1)S(1)} %back.8.refs_8_), channel_id=1, source_target_pairs={{0,16},{4,20},{8,24},{12,28},{16,0},{20,4},{24,8},{28,12},{1,17},{... | collective-permute-start | bytes 399368 | tf_op jit(solution)/shard_map/ppermute | solution.py:546
  43.2 1.4 %back.9.refs_8_ = bf16[520,128]{1,0:T(8,128)(2,1)S(1)} custom-call(s32[1]{0:T(128)} %bitcast.me.refs_0_.me_ref, f32[10,1024,128]{2,1,0:T(8,128)S(1)} %get-tuple-element.70.filt, bf16[2,256,512]{2,1,0:T(8,128)(2,1)S(1)} %copy-done.3, f32[512,128]{1,0:T(8,128)S(1)} %copy-done.1, f32[1024,128]{1,0:T(8,128)S(1)} %get-tuple-element.50.rest_2_.refs_0_, ...), custom_call_target="tpu_custom_call" | custom-call | tf_op jit(solution)/shard_map/back/pallas_call | solution.py:477
  44.6 0.1 collective-permute-start.12
  44.7 1.4 %back.10.refs_8_ = bf16[520,128]{1,0:T(8,128)(2,1)S(1)} custom-call(s32[1]{0:T(128)} %bitcast.me.refs_0_.me_ref, f32[10,1024,128]{2,1,0:T(8,128)S(1)} %get-tuple-element.70.filt, bf16[2,256,512]{2,1,0:T(8,128)(2,1)S(1)} %copy-done.3, f32[512,128]{1,0:T(8,128)S(1)} %copy-done.1, f32[1024,128]{1,0:T(8,128)S(1)} %get-tuple-element.50.rest_2_.refs_0_, ...), custom_call_target="tpu_custom_call" | custom-call | tf_op jit(solution)/shard_map/back/pallas_call | solution.py:477
  46.1 1.5 %back.11.refs_8_ = bf16[520,128]{1,0:T(8,128)(2,1)S(1)} custom-call(s32[1]{0:T(128)} %bitcast.me.refs_0_.me_ref, f32[10,1024,128]{2,1,0:T(8,128)S(1)} %get-tuple-element.70.filt, bf16[2,256,512]{2,1,0:T(8,128)(2,1)S(1)} %copy-done.3, f32[512,128]{1,0:T(8,128)S(1)} %copy-done.1, f32[1024,128]{1,0:T(8,128)S(1)} %get-tuple-element.50.rest_2_.refs_0_, ...), custom_call_target="tpu_custom_call" | custom-call | tf_op jit(solution)/shard_map/back/pallas_call | solution.py:477
  47.6 1.4 %back.12.refs_8_ = bf16[520,128]{1,0:T(8,128)(2,1)S(1)} custom-call(s32[1]{0:T(128)} %bitcast.me.refs_0_.me_ref, f32[10,1024,128]{2,1,0:T(8,128)S(1)} %get-tuple-element.70.filt, bf16[2,256,512]{2,1,0:T(8,128)(2,1)S(1)} %copy-done.3, f32[512,128]{1,0:T(8,128)S(1)} %copy-done.1, f32[1024,128]{1,0:T(8,128)S(1)} %get-tuple-element.50.rest_2_.refs_0_, ...), custom_call_target="tpu_custom_call" | custom-call | tf_op jit(solution)/shard_map/back/pallas_call | solution.py:477
  49.0 0.0 copy-start.6
  49.1 0.0 copy-start.11
  49.1 1.4 %back.13.refs_0_.refs_7_ = bf16[520,128]{1,0:T(8,128)(2,1)S(1)} custom-call(s32[1]{0:T(128)} %bitcast.me.refs_0_.me_ref, f32[10,1024,128]{2,1,0:T(8,128)S(1)} %get-tuple-element.70.filt, bf16[2,256,512]{2,1,0:T(8,128)(2,1)S(1)} %copy-done.3, f32[512,128]{1,0:T(8,128)S(1)} %copy-done.1, f32[1024,128]{1,0:T(8,128)S(1)} %get-tuple-element.50.rest_2_.refs_0_, ...), custom_call_target="tpu_custom_call" | custom-call | tf_op jit(solution)/shard_map/back/pallas_call | solution.py:477
  50.5 2.2 %collective-permute-start.9 = (bf16[520,128]{1,0:T(8,128)(2,1)S(1)}, bf16[520,128]{1,0:T(8,128)(2,1)S(1)}, u32[]{:S(2)}, u32[]{:S(2)}) collective-permute-start(bf16[520,128]{1,0:T(8,128)(2,1)S(1)} %back.12.refs_8_), channel_id=1, source_target_pairs={{0,12},{4,8},{8,4},{12,0},{16,28},{20,24},{24,20},{28,16},{1,13},{... | collective-permute-start | bytes 399368 | tf_op jit(solution)/shard_map/ppermute | solution.py:546
  52.7 1.2 %collective-permute-start.8 = (bf16[520,128]{1,0:T(8,128)(2,1)S(1)}, bf16[520,128]{1,0:T(8,128)(2,1)S(1)}, u32[]{:S(2)}, u32[]{:S(2)}) collective-permute-start(bf16[520,128]{1,0:T(8,128)(2,1)S(1)} %back.11.refs_8_), channel_id=1, source_target_pairs={{0,28},{4,24},{8,20},{12,16},{16,12},{20,8},{24,4},{28,0},{1,29},{... | collective-permute-start | bytes 399368 | tf_op jit(solution)/shard_map/ppermute | solution.py:546
  53.9 2.0 %collective-permute-start.14 = (bf16[520,128]{1,0:T(8,128)(2,1)S(1)}, bf16[520,128]{1,0:T(8,128)(2,1)S(1)}, u32[]{:S(2)}, u32[]{:S(2)}) collective-permute-start(bf16[520,128]{1,0:T(8,128)(2,1)S(1)} %back.10.refs_8_), channel_id=1, source_target_pairs={{0,24},{4,28},{8,16},{12,20},{16,8},{20,12},{24,0},{28,4},{1,25},{... | collective-permute-start | bytes 399368 | tf_op jit(solution)/shard_map/ppermute | solution.py:546
  56.0 0.5 final.4.refs_8_.refs_5_
  56.5 1.4 %back.14.refs_6_ = bf16[520,128]{1,0:T(8,128)(2,1)S(1)} custom-call(s32[1]{0:T(128)} %bitcast.me.refs_0_.me_ref, f32[10,1024,128]{2,1,0:T(8,128)S(1)} %get-tuple-element.70.filt, bf16[2,256,512]{2,1,0:T(8,128)(2,1)S(1)} %copy-done.3, f32[512,128]{1,0:T(8,128)S(1)} %copy-done.1, f32[1024,128]{1,0:T(8,128)S(1)} %get-tuple-element.50.rest_2_.refs_0_, ...), custom_call_target="tpu_custom_call" | custom-call | tf_op jit(solution)/shard_map/back/pallas_call | solution.py:477
  57.9 0.2 final.5.refs_8_.refs_5_
  58.1 1.4 %back.15.refs_6_ = bf16[520,128]{1,0:T(8,128)(2,1)S(1)} custom-call(s32[1]{0:T(128)} %bitcast.me.refs_0_.me_ref, f32[10,1024,128]{2,1,0:T(8,128)S(1)} %get-tuple-element.70.filt, bf16[2,256,512]{2,1,0:T(8,128)(2,1)S(1)} %copy-done.3, f32[512,128]{1,0:T(8,128)S(1)} %copy-done.1, f32[1024,128]{1,0:T(8,128)S(1)} %get-tuple-element.50.rest_2_.refs_0_, ...), custom_call_target="tpu_custom_call" | custom-call | tf_op jit(solution)/shard_map/back/pallas_call | solution.py:477
  59.6 0.5 collective-permute-start.13
  60.0 4.2 %collective-permute-done.14.refs_0_ = bf16[520,128]{1,0:T(8,128)(2,1)S(1)} collective-permute-done((bf16[520,128]{1,0:T(8,128)(2,1)S(1)}, bf16[520,128]{1,0:T(8,128)(2,1)S(1)}, u32[]{:S(2)}, u32[]{:S(2)}) %collective-permute-start.14) | collective-permute-done | bytes 133152 | tf_op jit(solution)/shard_map/ppermute | solution.py:546
  64.3 0.2 final.6.refs_12_
  64.5 1.0 %copy.32.refs_11_ = bf16[512,1024]{1,0:T(8,128)(2,1)} copy(bf16[512,1024]{1,0:T(8,128)(2,1)S(1)} %final.6.refs_12_) | data formatting | bytes 2097152
  65.5 1.3 %collective-permute-done.11.refs_2_ = bf16[520,128]{1,0:T(8,128)(2,1)S(1)} collective-permute-done((bf16[520,128]{1,0:T(8,128)(2,1)S(1)}, bf16[520,128]{1,0:T(8,128)(2,1)S(1)}, u32[]{:S(2)}, u32[]{:S(2)}) %collective-permute-start.11) | collective-permute-done | bytes 133152 | tf_op jit(solution)/shard_map/ppermute | solution.py:546
  66.8 1.2 %final.7 = bf16[512,1024]{1,0:T(8,128)(2,1)} custom-call(s32[1]{0:T(128)} %bitcast.me.refs_0_.me_ref, bf16[520,128]{1,0:T(8,128)(2,1)S(1)} %collective-permute-done.8.refs_0_, bf16[520,128]{1,0:T(8,128)(2,1)S(1)} %collective-permute-done.9.refs_1_, bf16[520,128]{1,0:T(8,128)(2,1)S(1)} %collective-permute-done.11.refs_2_, ...), custom_call_target="tpu_custom_call", output_to_operand_aliasing={{}: (12, {})} | custom-call | tf_op jit(solution)/shard_map/final/pallas_call | solution.py:522
  (21 shorter events, 0.0 us)
Async XLA Ops:
  1.0 7.7 %collective-permute-start = (bf16[128,1024]{1,0:T(8,128)(2,1)S(1)}, bf16[128,1024]{1,0:T(8,128)(2,1)S(1)}, u32[]{:S(2)}, u32[]{:S(2)}) collective-permute-start(bf16[128,1024]{1,0:T(8,128)(2,1)S(1)} %slice.3), channel_id=1, source_target_pairs={{0,4},{4,8},{8,12},{12,16},{16,20},{20,24},{24,28},{1,5},{5,9},{9,... | collective-permute-start | bytes 786440 | tf_op jit(solution)/shard_map/ppermute | solution.py:24
  3.4 1.2 %copy-start = (bf16[512,1024]{1,0:T(8,128)(2,1)S(1)}, bf16[512,1024]{1,0:T(8,128)(2,1)}, u32[]{:S(2)}) copy-start(bf16[512,1024]{1,0:T(8,128)(2,1)} %refs_2_.15) | copy-start | bytes 3145732
  3.4 1.5 %copy-start.2 = (bf16[512,1024]{1,0:T(8,128)(2,1)S(1)}, bf16[512,1024]{1,0:T(8,128)(2,1)}, u32[]{:S(2)}) copy-start(bf16[512,1024]{1,0:T(8,128)(2,1)} %refs_3_.17) | copy-start | bytes 3145732
  3.4 1.6 %copy-start.5 = (bf16[2,256,256]{2,1,0:T(8,128)(2,1)S(1)}, bf16[2,256,256]{2,1,0:T(8,128)(2,1)}, u32[]{:S(2)}) copy-start(bf16[2,256,256]{2,1,0:T(8,128)(2,1)} %constant.18.clone.refs_4_.refs_7_) | copy-start | bytes 786436
  3.4 1.6 %copy-start.7 = (bf16[2,128,256]{2,1,0:T(8,128)(2,1)S(1)}, bf16[2,128,256]{2,1,0:T(8,128)(2,1)}, u32[]{:S(2)}) copy-start(bf16[2,128,256]{2,1,0:T(8,128)(2,1)} %constant.19.clone.refs_5_.refs_8_) | copy-start | bytes 393220
  3.4 1.7 %copy-start.10 = (f32[128,1024]{1,0:T(8,128)S(1)}, f32[128,1024]{1,0:T(8,128)}, u32[]{:S(2)}) copy-start(f32[128,1024]{1,0:T(8,128)} %refs_3_.10) | copy-start | bytes 1572868
  3.4 5.2 %copy-start.8 = (f32[512,64]{0,1:T(8,128)S(1)}, f32[512,64]{0,1:T(8,128)}, u32[]{:S(2)}) copy-start(f32[512,64]{0,1:T(8,128)} %param.16) | copy-start | bytes 393220
  9.2 13.7 %collective-permute-start.2 = (bf16[552,128]{1,0:T(8,128)(2,1)S(1)}, bf16[552,128]{1,0:T(8,128)(2,1)S(1)}, u32[]{:S(2)}, u32[]{:S(2)}) collective-permute-start(bf16[552,128]{1,0:T(8,128)(2,1)S(1)} %get-tuple-element.43), channel_id=1, source_target_pairs={{0,16},{4,20},{8,24},{12,28},{16,0},{20,4},{24,8},{28,12},{1,17},{... | collective-permute-start | bytes 423944 | tf_op jit(solution)/shard_map/ppermute | solution.py:546
  13.8 11.3 %collective-permute-start.1 = (bf16[552,128]{1,0:T(8,128)(2,1)S(1)}, bf16[552,128]{1,0:T(8,128)(2,1)S(1)}, u32[]{:S(2)}, u32[]{:S(2)}) collective-permute-start(bf16[552,128]{1,0:T(8,128)(2,1)S(1)} %get-tuple-element.42), channel_id=1, source_target_pairs={{0,8},{4,12},{8,0},{12,4},{16,24},{20,28},{24,16},{28,20},{1,9},{5... | collective-permute-start | bytes 423944 | tf_op jit(solution)/shard_map/ppermute | solution.py:546
  15.9 12.1 %collective-permute-start.7 = (bf16[552,128]{1,0:T(8,128)(2,1)S(1)}, bf16[552,128]{1,0:T(8,128)(2,1)S(1)}, u32[]{:S(2)}, u32[]{:S(2)}) collective-permute-start(bf16[552,128]{1,0:T(8,128)(2,1)S(1)} %get-tuple-element.59), channel_id=1, source_target_pairs={{0,12},{4,8},{8,4},{12,0},{16,28},{20,24},{24,20},{28,16},{1,13},{... | collective-permute-start | bytes 423944 | tf_op jit(solution)/shard_map/ppermute | solution.py:546
  16.7 4.8 %copy-start.1 = (f32[512,128]{1,0:T(8,128)S(1)}, f32[512,128]{1,0:T(8,128)}, u32[]{:S(2)}) copy-start(f32[512,128]{1,0:T(8,128)} %constant.22.clone.turn) | copy-start | bytes 786436
  16.7 4.8 %copy-start.3 = (bf16[2,256,512]{2,1,0:T(8,128)(2,1)S(1)}, bf16[2,256,512]{2,1,0:T(8,128)(2,1)}, u32[]{:S(2)}) copy-start(bf16[2,256,512]{2,1,0:T(8,128)(2,1)} %constant.21.clone.rest_1_.inv) | copy-start | bytes 1572868
  16.7 4.8 %copy-start.4 = (bf16[2,512,256]{2,1,0:T(8,128)(2,1)S(1)}, bf16[2,512,256]{2,1,0:T(8,128)(2,1)}, u32[]{:S(2)}) copy-start(bf16[2,512,256]{2,1,0:T(8,128)(2,1)} %constant.20.clone.fwd) | copy-start | bytes 1572868
  16.7 4.8 %copy-start.9 = (bf16[16,256]{1,0:T(8,128)(2,1)S(1)}, bf16[16,256]{1,0:T(8,128)(2,1)}, u32[]{:S(2)}) copy-start(bf16[16,256]{1,0:T(8,128)(2,1)} %constant.23.clone.widen) | copy-start | bytes 24580
  17.2 12.0 %collective-permute-start.6 = (bf16[552,128]{1,0:T(8,128)(2,1)S(1)}, bf16[552,128]{1,0:T(8,128)(2,1)S(1)}, u32[]{:S(2)}, u32[]{:S(2)}) collective-permute-start(bf16[552,128]{1,0:T(8,128)(2,1)S(1)} %get-tuple-element.58), channel_id=1, source_target_pairs={{0,20},{4,16},{8,28},{12,24},{16,4},{20,0},{24,12},{28,8},{1,21},{... | collective-permute-start | bytes 423944 | tf_op jit(solution)/shard_map/ppermute | solution.py:546
  18.1 13.1 %collective-permute-start.5 = (bf16[552,128]{1,0:T(8,128)(2,1)S(1)}, bf16[552,128]{1,0:T(8,128)(2,1)S(1)}, u32[]{:S(2)}, u32[]{:S(2)}) collective-permute-start(bf16[552,128]{1,0:T(8,128)(2,1)S(1)} %get-tuple-element.57), channel_id=1, source_target_pairs={{0,24},{4,28},{8,16},{12,20},{16,8},{20,12},{24,0},{28,4},{1,25},{... | collective-permute-start | bytes 423944 | tf_op jit(solution)/shard_map/ppermute | solution.py:546
  24.5 7.8 %collective-permute-start.4 = (bf16[552,128]{1,0:T(8,128)(2,1)S(1)}, bf16[552,128]{1,0:T(8,128)(2,1)S(1)}, u32[]{:S(2)}, u32[]{:S(2)}) collective-permute-start(bf16[552,128]{1,0:T(8,128)(2,1)S(1)} %get-tuple-element.56), channel_id=1, source_target_pairs={{0,4},{4,0},{8,12},{12,8},{16,20},{20,16},{24,28},{28,24},{1,5},{5... | collective-permute-start | bytes 423944 | tf_op jit(solution)/shard_map/ppermute | solution.py:546
  26.7 7.7 %collective-permute-start.3 = (bf16[552,128]{1,0:T(8,128)(2,1)S(1)}, bf16[552,128]{1,0:T(8,128)(2,1)S(1)}, u32[]{:S(2)}, u32[]{:S(2)}) collective-permute-start(bf16[552,128]{1,0:T(8,128)(2,1)S(1)} %get-tuple-element.55), channel_id=1, source_target_pairs={{0,28},{4,24},{8,20},{12,16},{16,12},{20,8},{24,4},{28,0},{1,29},{... | collective-permute-start | bytes 423944 | tf_op jit(solution)/shard_map/ppermute | solution.py:546
  37.1 18.9 %collective-permute-start.10 = (bf16[520,128]{1,0:T(8,128)(2,1)S(1)}, bf16[520,128]{1,0:T(8,128)(2,1)S(1)}, u32[]{:S(2)}, u32[]{:S(2)}) collective-permute-start(bf16[520,128]{1,0:T(8,128)(2,1)S(1)} %back.8.refs_8_), channel_id=1, source_target_pairs={{0,16},{4,20},{8,24},{12,28},{16,0},{20,4},{24,8},{28,12},{1,17},{... | collective-permute-start | bytes 399368 | tf_op jit(solution)/shard_map/ppermute | solution.py:546
  44.6 13.3 %collective-permute-start.12 = (bf16[520,128]{1,0:T(8,128)(2,1)S(1)}, bf16[520,128]{1,0:T(8,128)(2,1)S(1)}, u32[]{:S(2)}, u32[]{:S(2)}) collective-permute-start(bf16[520,128]{1,0:T(8,128)(2,1)S(1)} %back.9.refs_8_), channel_id=1, source_target_pairs={{0,20},{4,16},{8,28},{12,24},{16,4},{20,0},{24,12},{28,8},{1,21},{... | collective-permute-start | bytes 399368 | tf_op jit(solution)/shard_map/ppermute | solution.py:546
  49.0 6.9 %copy-start.6 = (bf16[512,1024]{1,0:T(8,128)(2,1)S(1)}, bf16[512,1024]{1,0:T(8,128)(2,1)}, u32[]{:S(2)}) copy-start(bf16[512,1024]{1,0:T(8,128)(2,1)} %refs_9_.1) | copy-start | bytes 3145732
  49.1 6.9 %copy-start.11 = (f32[1024]{0:T(1024)S(1)}, f32[1024]{0:T(1024)}, u32[]{:S(2)}) copy-start(f32[1024]{0:T(1024)} %param.17) | copy-start | bytes 12292
  50.5 15.0 %collective-permute-start.9 = (bf16[520,128]{1,0:T(8,128)(2,1)S(1)}, bf16[520,128]{1,0:T(8,128)(2,1)S(1)}, u32[]{:S(2)}, u32[]{:S(2)}) collective-permute-start(bf16[520,128]{1,0:T(8,128)(2,1)S(1)} %back.12.refs_8_), channel_id=1, source_target_pairs={{0,12},{4,8},{8,4},{12,0},{16,28},{20,24},{24,20},{28,16},{1,13},{... | collective-permute-start | bytes 399368 | tf_op jit(solution)/shard_map/ppermute | solution.py:546
  52.7 12.8 %collective-permute-start.8 = (bf16[520,128]{1,0:T(8,128)(2,1)S(1)}, bf16[520,128]{1,0:T(8,128)(2,1)S(1)}, u32[]{:S(2)}, u32[]{:S(2)}) collective-permute-start(bf16[520,128]{1,0:T(8,128)(2,1)S(1)} %back.11.refs_8_), channel_id=1, source_target_pairs={{0,28},{4,24},{8,20},{12,16},{16,12},{20,8},{24,4},{28,0},{1,29},{... | collective-permute-start | bytes 399368 | tf_op jit(solution)/shard_map/ppermute | solution.py:546
  53.9 10.3 %collective-permute-start.14 = (bf16[520,128]{1,0:T(8,128)(2,1)S(1)}, bf16[520,128]{1,0:T(8,128)(2,1)S(1)}, u32[]{:S(2)}, u32[]{:S(2)}) collective-permute-start(bf16[520,128]{1,0:T(8,128)(2,1)S(1)} %back.10.refs_8_), channel_id=1, source_target_pairs={{0,24},{4,28},{8,16},{12,20},{16,8},{20,12},{24,0},{28,4},{1,25},{... | collective-permute-start | bytes 399368 | tf_op jit(solution)/shard_map/ppermute | solution.py:546
  59.6 5.9 %collective-permute-start.13 = (bf16[520,128]{1,0:T(8,128)(2,1)S(1)}, bf16[520,128]{1,0:T(8,128)(2,1)S(1)}, u32[]{:S(2)}, u32[]{:S(2)}) collective-permute-start(bf16[520,128]{1,0:T(8,128)(2,1)S(1)} %back.15.refs_6_), channel_id=1, source_target_pairs={{0,4},{4,0},{8,12},{12,8},{16,20},{20,16},{24,28},{28,24},{1,5},{5... | collective-permute-start | bytes 399368 | tf_op jit(solution)/shard_map/ppermute | solution.py:546
  60.0 6.8 %collective-permute-start.11 = (bf16[520,128]{1,0:T(8,128)(2,1)S(1)}, bf16[520,128]{1,0:T(8,128)(2,1)S(1)}, u32[]{:S(2)}, u32[]{:S(2)}) collective-permute-start(bf16[520,128]{1,0:T(8,128)(2,1)S(1)} %back.14.refs_6_), channel_id=1, source_target_pairs={{0,8},{4,12},{8,0},{12,4},{16,24},{20,28},{24,16},{28,20},{1,9},{5... | collective-permute-start | bytes 399368 | tf_op jit(solution)/shard_map/ppermute | solution.py:546

commit v4 on v3

--- a/solution.py
+++ b/solution.py
@@ -264,50 +264,23 @@
         code[start : start + v.shape[0]] = to_code(v, scale)
         start += v.shape[0]
     scale = jnp.broadcast_to(scale, (groups, LANES))
-    if filter_rows is None:
-        both = scale
-    else:
-        size = jnp.abs(filter_rows)
-        many = filter_rows.shape[0] // groups
-        most = size[:groups]
-        for c in range(1, many):
-            most = jnp.maximum(most, size[c * groups : (c + 1) * groups])
-        filter_scale = scale_of(jnp.max(most, axis=1, keepdims=True))
-        filter_scale = jnp.broadcast_to(filter_scale, (groups, LANES))
-        row, lane = (lax.broadcasted_iota(jnp.int32, scale.shape, k) for k in (0, 1))
-        by_lane = jnp.sum(jnp.where(row == lane, filter_scale, 0.0), axis=0, keepdims=True)
-        both = jnp.where(row == groups - 1, by_lane, scale)
-        end = rows + filter_rows.shape[0]
-        code[rows:end] = to_code(filter_rows, jnp.concatenate([filter_scale] * many, 0))
-        rows = end
+    size = jnp.abs(filter_rows)
+    many = filter_rows.shape[0] // groups
+    most = size[:groups]
+    for c in range(1, many):
+        most = jnp.maximum(most, size[c * groups : (c + 1) * groups])
+    filter_scale = scale_of(jnp.max(most, axis=1, keepdims=True))
+    filter_scale = jnp.broadcast_to(filter_scale, (groups, LANES))
+    row, lane = (lax.broadcasted_iota(jnp.int32, scale.shape, k) for k in (0, 1))
+    by_lane = jnp.sum(jnp.where(row == lane, filter_scale, 0.0), axis=0, keepdims=True)
+    both = jnp.where(row == groups - 1, by_lane, scale)
+    end = rows + filter_rows.shape[0]
+    code[rows:end] = to_code(filter_rows, jnp.concatenate([filter_scale] * many, 0))
+    rows = end
     code[rows:] = both.astype(jnp.bfloat16)
 
 
-def ahead_body(part, me, value, gate, taps, long_taps, fwd, inv, *codes):
-    count = taps.shape[0]
-    for d, code in zip(part, codes):
-        slab = me[0] ^ d
-        cols = lanes_of(slab)
-        taps_spec = dot3(fwd[:, :, :count], taps[:, cols])
-        short = short_rows(value[:, cols], taps_spec, fwd, inv)
-        write_code(code, [gate[count:, cols].astype(jnp.float32) * short], long_taps[slab])
-
-
-def ahead_call(part, me, value, gate, taps, long_taps, fwd, inv, after):
-    rows = value.shape[0] - taps.shape[0] + TILE + long_taps.shape[1]
-    code = jax.ShapeDtypeStruct((rows, LANES), jnp.bfloat16)
-    return pl.pallas_call(
-        drop_after(functools.partial(ahead_body, part), 7, len(after)),
-        in_specs=[IN_SMEM] + [IN_VMEM] * 6 + [IN_ANY] * len(after),
-        out_specs=[IN_VMEM] * len(part),
-        out_shape=[code] * len(part),
-        compiler_params=kernel_params(12),
-        cost_estimate=cost(1),
-        name="short_ahead",
-    )(me, value, gate, taps, long_taps, fwd, inv, *after)
-
-
-def head_body(part, ahead, me, halo, value, gate, gated, taps_spec, long_taps, fwd, inv, *outs):
+def head_body(part, me, halo, value, gate, gated, taps_spec, long_taps, fwd, inv, *outs):
     taps = halo.shape[0]
     tops, codes = outs[: len(part)], outs[len(part) :]
     for d, top, code in zip(part, tops, codes):
@@ -317,22 +290,16 @@
         short = short_rows(ext, taps_spec[:, cols], fwd, inv)
         first = gate[:taps, cols].astype(jnp.float32) * short
         top[...] = first
-        if d in ahead:
-            write_code(code, [first], None)
-        else:
-            write_code(code, [first, gated[:, cols]], long_taps[slab])
-
-
-def head_call(part, ahead, me, halo, value, gate, gated, taps_spec, long_taps, fwd, inv, after):
+        write_code(code, [first, gated[:, cols]], long_taps[slab])
+
+
+def head_call(part, me, halo, value, gate, gated, taps_spec, long_taps, fwd, inv, after):
     taps = halo.shape[0]
     whole = taps + gated.shape[0] + TILE + long_taps.shape[1]
-    codes = [
-        jax.ShapeDtypeStruct((taps + TILE if d in ahead else whole, LANES), jnp.bfloat16)
-        for d in part
-    ]
+    codes = [jax.ShapeDtypeStruct((whole, LANES), jnp.bfloat16)] * len(part)
     top = jax.ShapeDtypeStruct((taps, LANES), jnp.float32)
     return pl.pallas_call(
-        drop_after(functools.partial(head_body, part, ahead), 9, len(after)),
+        drop_after(functools.partial(head_body, part), 9, len(after)),
         in_specs=[IN_SMEM] + [IN_VMEM] * 8 + [IN_ANY] * len(after),
         out_specs=[IN_VMEM] * (2 * len(part)),
         out_shape=[top] * len(part) + codes,
@@ -342,22 +309,17 @@
     )(me, halo, value, gate, gated, taps_spec, long_taps, fwd, inv, *after)
 
 
-def forward_body(d, clear, pieces, me, fwd, turn, widen, *rest):
+def forward_body(d, clear, me, code, fwd, turn, widen, *rest):
     spec_out, filter_out, held_x, held_h = rest[-4:]
     rows = held_x.shape[0]
     half = rows // 2
     groups = 8
-    end = rows
-    for code, length in zip(rest, pieces):
-        scales = code[code.shape[0] - TILE :].astype(jnp.float32)
-        held_x[end - length : end] = from_code(code[:length], scales[:1])
-        end -= length
-    code, length = rest[0], pieces[0]
     scales = code[code.shape[0] - TILE :].astype(jnp.float32)
+    held_x[...] = from_code(code[:rows], scales[:1])
     row, lane = (lax.broadcasted_iota(jnp.int32, scales.shape, k) for k in (0, 1))
     by_lane = jnp.where(row == lane, scales[groups - 1 :], 0.0)
     scale = jnp.broadcast_to(jnp.sum(by_lane, axis=1, keepdims=True), scales.shape)
-    taps = code[length : code.shape[0] - TILE]
+    taps = code[rows : code.shape[0] - TILE]
     many = taps.shape[0] // groups
     h_high, h_low = split(from_code(taps, jnp.concatenate([scale] * many, 0)))
     h_high, h_low = h_high.astype(jnp.float32), h_low.astype(jnp.float32)
@@ -399,14 +361,12 @@
         filter_out[later, at] += moved
 
 
-def forward_call(d, count, me, codes, fwd, turn, widen, early, so_far, after):
+def forward_call(d, count, me, code, fwd, turn, widen, early, so_far, after):
     rows = 2 * fwd.shape[2]
     held = so_far + early
-    last = codes[-1].shape[0] - TILE
-    pieces = [rows - last, last] if len(codes) > 1 else [rows]
     return pl.pallas_call(
-        functools.partial(forward_body, d, not so_far, pieces),
-        in_specs=[IN_SMEM] + [IN_VMEM] * (3 + len(codes) + len(held)) + [IN_ANY] * len(after),
+        functools.partial(forward_body, d, not so_far),
+        in_specs=[IN_SMEM] + [IN_VMEM] * (4 + len(held)) + [IN_ANY] * len(after),
         out_specs=[IN_VMEM] * 2,
         out_shape=[
             jax.ShapeDtypeStruct((2 * rows, LANES), jnp.float32),
@@ -416,11 +376,11 @@
             pltpu.VMEM((rows, LANES), jnp.float32),
             pltpu.VMEM((2, rows, LANES), jnp.float32),
         ],
-        input_output_aliases={4 + len(codes): 1} if so_far else {},
+        input_output_aliases={5: 1} if so_far else {},
         compiler_params=kernel_params(12),
         cost_estimate=cost(1),
         name="forward",
-    )(me, fwd, turn, widen, *codes, *held, *after)
+    )(me, code, fwd, turn, widen, *held, *after)
 
 
 def back_body(part, count, me_ref, filt, inv, turn, *refs):
@@ -489,50 +449,72 @@
     )(me, filt, inv, turn, *specs, *after)
 
 
-def final_body(part, count, me, *refs):
+def finish(code, top, gated, gate, skip, cols, out):
+    taps = top.shape[0]
+    rows = gate.shape[0]
+    scale = code[rows : rows + 1].astype(jnp.float32)
+    for r, part_gated in ((slice(0, taps), top[...]), (slice(taps, rows), gated[:, cols])):
+        total = from_code(code[r], scale) + skip[:, cols] * part_gated
+        out[r] = (gate[r, cols].astype(jnp.float32) * total).astype(jnp.bfloat16)
+
+
+def final_body(part, me, gated, gate, skip, *refs):
     many = len(part)
-    codes, tops, (gated, gate, skip) = refs[:many], refs[many : 2 * many], refs[2 * many : 2 * many + 3]
-    out, held, sems = refs[-3:]
-    taps = tops[0].shape[0]
-    rows = gate.shape[0]
-    copies = []
-    for at, d in enumerate(part):
-        cols = lanes_of(me[0] ^ d)
-        code, top = codes[at], tops[at]
-        scale = code[rows : rows + 1].astype(jnp.float32)
-        for r, part_gated in ((slice(0, taps), top[...]), (slice(taps, rows), gated[:, cols])):
-            total = from_code(code[r], scale) + skip[:, cols] * part_gated
-            held[at, r] = (gate[r, cols].astype(jnp.float32) * total).astype(jnp.bfloat16)
-        copies.append(pltpu.make_async_copy(held.at[at], out.at[:, cols], sems.at[at]))
-        copies[-1].start()
-    for copy in copies:
-        copy.wait()
-
-
-def final_call(part, count, me, codes, tops, gated, gate, skip, so_far, after):
-    rows = gate.shape[0]
+    codes, tops, outs = refs[:many], refs[many : 2 * many], refs[2 * many :]
+    for d, code, top, out in zip(part, codes, tops, outs):
+        finish(code, top, gated, gate, skip, lanes_of(me[0] ^ d), out)
+
+
+def final_call(part, me, codes, tops, gated, gate, skip, after):
     many = len(part)
-    args = [me, *codes, *tops, gated, gate, skip]
-    specs = [IN_SMEM] + [IN_VMEM] * (2 * many + 3)
-    alias = {}
-    if so_far:
-        alias = {len(args): 0}
-    args += so_far + after
-    specs += [IN_HBM] * len(so_far) + [IN_ANY] * len(after)
+    slab = jax.ShapeDtypeStruct((gate.shape[0], LANES), jnp.bfloat16)
     return pl.pallas_call(
-        functools.partial(final_body, part, count),
-        in_specs=specs,
-        out_specs=IN_HBM,
-        out_shape=jax.ShapeDtypeStruct(gate.shape, jnp.bfloat16),
-        scratch_shapes=[
-            pltpu.VMEM((many, rows, LANES), jnp.bfloat16),
-            pltpu.SemaphoreType.DMA((many,)),
-        ],
-        input_output_aliases=alias,
+        drop_after(functools.partial(final_body, part), 4 + 2 * many, len(after)),
+        in_specs=[IN_SMEM] + [IN_VMEM] * (3 + 2 * many) + [IN_ANY] * len(after),
+        out_specs=[IN_VMEM] * many,
+        out_shape=[slab] * many,
         compiler_params=kernel_params(12),
         cost_estimate=cost(many),
         name="final",
-    )(*args)
+    )(me, gated, gate, skip, *codes, *tops, *after)
+
+
+def last_body(part, ready, me, gated, gate, skip, *refs):
+    many = len(part)
+    codes, tops = refs[:many], refs[many : 2 * many]
+    slabs, (out, held, sems) = refs[2 * many : -3], refs[-3:]
+    copies = []
+
+    def send(d, slab):
+        at = len(copies)
+        copies.append(pltpu.make_async_copy(slab, out.at[:, lanes_of(me[0] ^ d)], sems.at[at]))
+        copies[-1].start()
+
+    for d, slab in zip(ready, slabs):
+        send(d, slab)
+    for at, d in enumerate(part):
+        finish(codes[at], tops[at], gated, gate, skip, lanes_of(me[0] ^ d), held.at[at])
+        send(d, held.at[at])
+    for copy in copies:
+        copy.wait()
+
+
+def last_call(part, me, codes, tops, gated, gate, skip, slabs):
+    many = len(part)
+    ready = tuple(slabs)
+    return pl.pallas_call(
+        functools.partial(last_body, part, ready),
+        in_specs=[IN_SMEM] + [IN_VMEM] * (3 + 2 * many + len(ready)),
+        out_specs=IN_ANY,
+        out_shape=jax.ShapeDtypeStruct(gate.shape, jnp.bfloat16),
+        scratch_shapes=[
+            pltpu.VMEM((many, gate.shape[0], LANES), jnp.bfloat16),
+            pltpu.SemaphoreType.DMA((many + len(ready),)),
+        ],
+        compiler_params=kernel_params(12),
+        cost_estimate=cost(many),
+        name="last",
+    )(me, gated, gate, skip, *codes, *tops, *slabs.values())
 
 
 def in_slabs(output_gate, input_gate, value_input, short_filter, long_filter, skip_gain):
@@ -548,7 +530,9 @@
     def table(values):
         return jnp.asarray(split_table(values))
 
-    halo = passed_along(value_input[rows - taps :], "ctx", 1)
+    paced = pace_call(me)
+    start = rows - taps + jnp.minimum(paced[0], 0)
+    halo = passed_along(lax.dynamic_slice_in_dim(value_input, start, taps, 0), "ctx", 1)
     long_taps = long_filter.T.reshape(count, groups, rows // LANES, LANES)
     long_taps = jnp.swapaxes(long_taps, 1, 2).reshape(count, -1, LANES)
 
@@ -561,9 +545,8 @@
     widen = jnp.asarray(widening(groups, LANES))
 
     came, tops, specs, answers = {}, {}, {}, {}
-    after, filt, mixed = [], [], []
-
-    paced = pace_call(me)
+    after, filt, mixed = [], [], {}
+
     main_out = []
 
     def mains():
@@ -572,24 +555,15 @@
         )
         after[:] = main_out[:1]
 
-    def aheads(*part):
-        codes = ahead_call(
-            part, paced, value_input, input_gate, short_filter, long_taps, short_fwd, short_inv,
-            after,
-        )
-        after[:] = codes[:1]
-        for d, code in zip(part, codes):
-            came[d] = [exchanged(code, d)]
-
     def heads(*part):
         outs = head_call(
-            part, tuple(came), me, halo, value_input, input_gate, *main_out, long_taps,
+            part, me, halo, value_input, input_gate, *main_out, long_taps,
             short_fwd, short_inv, after,
         )
         after[:] = outs[:1]
         for d, top, code in zip(part, outs, outs[len(part) :]):
             tops[d] = top
-            came[d] = came.get(d, []) + [exchanged(code, d)]
+            came[d] = exchanged(code, d)
 
     def forwards(*part):
         for d in part:
@@ -608,27 +582,27 @@
             after[:] = [code]
 
     def finals(*part):
-        mixed[:] = [
-            final_call(
-                part, count, me, [answers[e] for e in part], [tops[e] for e in part],
-                main_out[0], output_gate, skip_gain[None], mixed, after,
-            )
-        ]
-        after[:] = mixed
+        args = [me, [answers[e] for e in part], [tops[e] for e in part]]
+        args += [main_out[0], output_gate, skip_gain[None]]
+        if len(mixed) + len(part) == count:
+            return last_call(part, *args, mixed)
+        outs = final_call(part, *args, after)
+        mixed.update(zip(part, outs))
+        after[:] = outs[:1]
 
     mains()
     heads(4)
     heads(2)
+    heads(5)
     heads(3)
-    heads(5)
     heads(6, 0)
     forwards(0)
     forwards(4)
     heads(1)
     forwards(2)
     heads(7)
+    forwards(5)
     forwards(3)
-    forwards(5)
     forwards(6)
     forwards(1)
     forwards(7)
@@ -642,9 +616,8 @@
     backs(2)
     finals(5)
     backs(1)
-    finals(6)
-    finals(7, 3, 2, 1)
-    return mixed[0]
+    finals(6, 7)
+    return finals(3, 2, 1)
 
 
 def local(output_gate, input_gate, value_input, short_filter, long_filter, skip_gain):

time: 68.4 us -> 67.4 us (0.985)
  local copies, waits for them, and re-layouts: 3.19 us -> 0.13 us
  starting transfers between devices: 25.3 us -> 27 us
  between operations: 0.54 us -> 1.49 us
    unnamed x25 -> x24, local copies, waits for them, and re-layouts: 2.22 us -> 0.06 us
    ppermute x14, starting transfers between devices: 22.9 us -> 24.6 us  [exchanged(): lax.ppermute(block, 'ctx', [(i, i ^ d) for i in range(count)])]
    slice x1 -> x0, local copies, waits for them, and re-layouts: 0.97 us -> none  [in_slabs(): halo = passed_along(value_input[rows - taps:], 'ctx', 1)]
  transfers between devices with their start and end apart: 15 -> 15, of which waited for: 6 -> 5; matrix products, arithmetic and copies ran while one was open for 1% -> 0% of each run, Pallas kernels for 39% -> 38%
where the time goes in v4:
time: 67.4 us; the launch traced here: 67.2 us
  Pallas kernels  30.4 us (45%)
  starting transfers between devices  27 us (40%)
  waiting for transfers between devices  8.25 us (12%)
  between operations  1.49 us (2%)
    ppermute x14, starting transfers between devices, exchanged(): lax.ppermute(block, 'ctx', [(i, i ^ d) for i in range(count)])  24.6 us
    pallas_call x8, Pallas kernels, back_call(): pl.pallas_call(functools.partial(back_body, part, count), in_specs=[IN_SM...  11.8 us
    pallas_call x8, Pallas kernels, forward_call(): pl.pallas_call(functools.partial(forward_body, d, not so_far), in_specs=[...  9.09 us
    ppermute x14, waiting for transfers between devices, exchanged(): lax.ppermute(block, 'ctx', [(i, i ^ d) for i in range(count)])  8.25 us
    pallas_call x7, Pallas kernels, head_call(): pl.pallas_call(drop_after(functools.partial(head_body, part), 9, len(afte...  3.74 us
    pallas_call x1, Pallas kernels, main_call(): pl.pallas_call(drop_after(main_body, 6, len(after)), in_specs=[IN_SMEM] +...  3.43 us
    ppermute x1, starting transfers between devices, passed_along(): return lax.ppermute(block, axis, route)  2.4 us
  transfers between devices with their start and end apart: 15, of which 5 were waited for; matrix products, arithmetic and copies ran while one was open for 0% of the time, Pallas kernels for 38%

profile of v4, /device:TPU:0, one launch (start us, length us, event | category | flops | bytes accessed | tf_op | source)
XLA Modules:
  0.0 67.2 jit_solution(10684090609761930815)
XLA Ops:
  0.0 0.5 pace.1.refs_0_
  1.5 0.1 constant_dynamic-slice_fusion
  1.6 2.4 %collective-permute-start = (bf16[128,1024]{1,0:T(8,128)(2,1)S(1)}, bf16[128,1024]{1,0:T(8,128)(2,1)S(1)}, u32[]{:S(2)}, u32[]{:S(2)}) collective-permute-start(bf16[128,1024]{1,0:T(8,128)(2,1)S(1)} %constant_dynamic-slice_fusion), channel_id=1, source_target_pairs={{0,4},{4,8},{8,12},{12,16},{16,20},{20,24},{24,28},{1,5},{5,9},{9,... | collective-permute-start | bytes 786440 | tf_op jit(solution)/shard_map/ppermute | solution.py:24
  4.0 3.4 %short_main.1 = (f32[384,1024]{1,0:T(8,128)S(1)}, f32[256,1024]{1,0:T(8,128)S(1)}) custom-call(s32[1]{0:T(128)} %pace.1.refs_0_, bf16[512,1024]{1,0:T(8,128)(2,1)S(1)} %copy-done, bf16[512,1024]{1,0:T(8,128)(2,1)S(1)} %copy-done.2, f32[128,1024]{1,0:T(8,128)S(1)} %copy-done.10, bf16[2,256,256]{2,1,0:T(8,128)(2,1)S(1)} %copy-done.5, ...), custom_call_target="tpu_custom_call" | custom-call | tf_op jit(solution)/shard_map/short_main/pallas_call | solution.py:237
  7.4 0.0 collective-permute-done.refs_1_
  7.5 0.5 short_head.7
  8.0 5.9 %collective-permute-start.2 = (bf16[552,128]{1,0:T(8,128)(2,1)S(1)}, bf16[552,128]{1,0:T(8,128)(2,1)S(1)}, u32[]{:S(2)}, u32[]{:S(2)}) collective-permute-start(bf16[552,128]{1,0:T(8,128)(2,1)S(1)} %get-tuple-element.47), channel_id=1, source_target_pairs={{0,16},{4,20},{8,24},{12,28},{16,0},{20,4},{24,8},{28,12},{1,17},{... | collective-permute-start | bytes 423944 | tf_op jit(solution)/shard_map/ppermute | solution.py:528
  13.9 0.5 short_head.8
  14.4 1.6 %collective-permute-start.1 = (bf16[552,128]{1,0:T(8,128)(2,1)S(1)}, bf16[552,128]{1,0:T(8,128)(2,1)S(1)}, u32[]{:S(2)}, u32[]{:S(2)}) collective-permute-start(bf16[552,128]{1,0:T(8,128)(2,1)S(1)} %get-tuple-element.46), channel_id=1, source_target_pairs={{0,8},{4,12},{8,0},{12,4},{16,24},{20,28},{24,16},{28,20},{1,9},{5... | collective-permute-start | bytes 423944 | tf_op jit(solution)/shard_map/ppermute | solution.py:528
  16.0 0.5 short_head.9
  16.5 0.1 collective-permute-start.7
  16.6 0.0 copy-start.1
  16.6 0.0 copy-start.3
  16.6 0.0 copy-start.4
  16.6 0.0 copy-start.9
  16.6 0.5 short_head.10
  17.1 0.2 collective-permute-start.6
  17.3 0.8 %short_head.11 = (f32[128,128]{1,0:T(8,128)S(1)}, f32[128,128]{1,0:T(8,128)S(1)}, bf16[552,128]{1,0:T(8,128)(2,1)S(1)}, bf16[552,128]{1,0:T(8,128)(2,1)S(1)}) custom-call(s32[1]{0:T(128)} %bitcast.me.refs_0_.me_ref, bf16[128,1024]{1,0:T(8,128)(2,1)S(1)} %collective-permute-done.refs_1_, bf16[512,1024]{1,0:T(8,128)(2,1)S(1)} %copy-done, ...), custom_call_target="tpu_custom_call" | custom-call | tf_op jit(solution)/shard_map/short_head/pallas_call | solution.py:301
  18.1 4.0 %collective-permute-start.5 = (bf16[552,128]{1,0:T(8,128)(2,1)S(1)}, bf16[552,128]{1,0:T(8,128)(2,1)S(1)}, u32[]{:S(2)}, u32[]{:S(2)}) collective-permute-start(bf16[552,128]{1,0:T(8,128)(2,1)S(1)} %get-tuple-element.61), channel_id=1, source_target_pairs={{0,24},{4,28},{8,16},{12,20},{16,8},{20,12},{24,0},{28,4},{1,25},{... | collective-permute-start | bytes 423944 | tf_op jit(solution)/shard_map/ppermute | solution.py:528
  22.1 1.3 %forward.8 = (f32[1024,128]{1,0:T(8,128)S(1)}, f32[10,1024,128]{2,1,0:T(8,128)S(1)}) custom-call(s32[1]{0:T(128)} %bitcast.me.refs_0_.me_ref, bf16[552,128]{1,0:T(8,128)(2,1)S(1)} %get-tuple-element.51.code, bf16[2,512,256]{2,1,0:T(8,128)(2,1)S(1)} %copy-done.4, f32[512,128]{1,0:T(8,128)S(1)} %copy-done.1, bf16[16,256]{1,0:T(8,128)(2,1)S(1)} %copy-done.9, ...), custom_call_target="tpu_custom_call" | custom-call | tf_op jit(solution)/shard_map/forward/pallas_call | solution.py:367
  23.4 0.0 collective-permute-done.2.code
  23.4 1.1 %forward.9 = (f32[1024,128]{1,0:T(8,128)S(1)}, f32[10,1024,128]{2,1,0:T(8,128)S(1)}) custom-call(s32[1]{0:T(128)} %bitcast.me.refs_0_.me_ref, bf16[552,128]{1,0:T(8,128)(2,1)S(1)} %collective-permute-done.2.code, bf16[2,512,256]{2,1,0:T(8,128)(2,1)S(1)} %copy-done.4, f32[512,128]{1,0:T(8,128)S(1)} %copy-done.1, ...), custom_call_target="tpu_custom_call", output_to_operand_aliasing={{1}: (5, {})} | custom-call | tf_op jit(solution)/shard_map/forward/pallas_call | solution.py:367
  24.5 0.5 short_head.12
  25.0 0.1 collective-permute-start.4
  25.1 0.0 collective-permute-done.1.code
  25.1 1.1 %forward.10 = (f32[1024,128]{1,0:T(8,128)S(1)}, f32[10,1024,128]{2,1,0:T(8,128)S(1)}) custom-call(s32[1]{0:T(128)} %bitcast.me.refs_0_.me_ref, bf16[552,128]{1,0:T(8,128)(2,1)S(1)} %collective-permute-done.1.code, bf16[2,512,256]{2,1,0:T(8,128)(2,1)S(1)} %copy-done.4, f32[512,128]{1,0:T(8,128)S(1)} %copy-done.1, ...), custom_call_target="tpu_custom_call", output_to_operand_aliasing={{1}: (5, {})} | custom-call | tf_op jit(solution)/shard_map/forward/pallas_call | solution.py:367
  26.3 0.5 short_head.13
  26.8 1.3 %collective-permute-start.3 = (bf16[552,128]{1,0:T(8,128)(2,1)S(1)}, bf16[552,128]{1,0:T(8,128)(2,1)S(1)}, u32[]{:S(2)}, u32[]{:S(2)}) collective-permute-start(bf16[552,128]{1,0:T(8,128)(2,1)S(1)} %get-tuple-element.59), channel_id=1, source_target_pairs={{0,28},{4,24},{8,20},{12,16},{16,12},{20,8},{24,4},{28,0},{1,29},{... | collective-permute-start | bytes 423944 | tf_op jit(solution)/shard_map/ppermute | solution.py:528
  28.1 0.0 collective-permute-done.7.code
  28.1 1.1 %forward.11 = (f32[1024,128]{1,0:T(8,128)S(1)}, f32[10,1024,128]{2,1,0:T(8,128)S(1)}) custom-call(s32[1]{0:T(128)} %bitcast.me.refs_0_.me_ref, bf16[552,128]{1,0:T(8,128)(2,1)S(1)} %collective-permute-done.7.code, bf16[2,512,256]{2,1,0:T(8,128)(2,1)S(1)} %copy-done.4, f32[512,128]{1,0:T(8,128)S(1)} %copy-done.1, ...), custom_call_target="tpu_custom_call", output_to_operand_aliasing={{1}: (5, {})} | custom-call | tf_op jit(solution)/shard_map/forward/pallas_call | solution.py:367
  29.2 0.0 collective-permute-done.6.code
  29.2 1.1 %forward.12 = (f32[1024,128]{1,0:T(8,128)S(1)}, f32[10,1024,128]{2,1,0:T(8,128)S(1)}) custom-call(s32[1]{0:T(128)} %bitcast.me.refs_0_.me_ref, bf16[552,128]{1,0:T(8,128)(2,1)S(1)} %collective-permute-done.6.code, bf16[2,512,256]{2,1,0:T(8,128)(2,1)S(1)} %copy-done.4, f32[512,128]{1,0:T(8,128)S(1)} %copy-done.1, ...), custom_call_target="tpu_custom_call", output_to_operand_aliasing={{1}: (5, {})} | custom-call | tf_op jit(solution)/shard_map/forward/pallas_call | solution.py:367
  30.3 0.2 collective-permute-done.5.code
  30.5 1.1 %forward.13 = (f32[1024,128]{1,0:T(8,128)S(1)}, f32[10,1024,128]{2,1,0:T(8,128)S(1)}) custom-call(s32[1]{0:T(128)} %bitcast.me.refs_0_.me_ref, bf16[552,128]{1,0:T(8,128)(2,1)S(1)} %collective-permute-done.5.code, bf16[2,512,256]{2,1,0:T(8,128)(2,1)S(1)} %copy-done.4, f32[512,128]{1,0:T(8,128)S(1)} %copy-done.1, ...), custom_call_target="tpu_custom_call", output_to_operand_aliasing={{1}: (5, {})} | custom-call | tf_op jit(solution)/shard_map/forward/pallas_call | solution.py:367
  31.7 0.0 collective-permute-done.4.code
  31.7 1.1 %forward.14 = (f32[1024,128]{1,0:T(8,128)S(1)}, f32[10,1024,128]{2,1,0:T(8,128)S(1)}) custom-call(s32[1]{0:T(128)} %bitcast.me.refs_0_.me_ref, bf16[552,128]{1,0:T(8,128)(2,1)S(1)} %collective-permute-done.4.code, bf16[2,512,256]{2,1,0:T(8,128)(2,1)S(1)} %copy-done.4, f32[512,128]{1,0:T(8,128)S(1)} %copy-done.1, ...), custom_call_target="tpu_custom_call", output_to_operand_aliasing={{1}: (5, {})} | custom-call | tf_op jit(solution)/shard_map/forward/pallas_call | solution.py:367
  32.8 1.3 %collective-permute-done.3.code = bf16[552,128]{1,0:T(8,128)(2,1)S(1)} collective-permute-done((bf16[552,128]{1,0:T(8,128)(2,1)S(1)}, bf16[552,128]{1,0:T(8,128)(2,1)S(1)}, u32[]{:S(2)}, u32[]{:S(2)}) %collective-permute-start.3) | collective-permute-done | bytes 141344 | tf_op jit(solution)/shard_map/ppermute | solution.py:528
  34.1 1.1 %forward.15 = (f32[1024,128]{1,0:T(8,128)S(1)}, f32[10,1024,128]{2,1,0:T(8,128)S(1)}) custom-call(s32[1]{0:T(128)} %bitcast.me.refs_0_.me_ref, bf16[552,128]{1,0:T(8,128)(2,1)S(1)} %collective-permute-done.3.code, bf16[2,512,256]{2,1,0:T(8,128)(2,1)S(1)} %copy-done.4, f32[512,128]{1,0:T(8,128)S(1)} %copy-done.1, ...), custom_call_target="tpu_custom_call", output_to_operand_aliasing={{1}: (5, {})} | custom-call | tf_op jit(solution)/shard_map/forward/pallas_call | solution.py:367
  35.2 1.6 %back.8.refs_8_ = bf16[520,128]{1,0:T(8,128)(2,1)S(1)} custom-call(s32[1]{0:T(128)} %bitcast.me.refs_0_.me_ref, f32[10,1024,128]{2,1,0:T(8,128)S(1)} %get-tuple-element.74.filt, bf16[2,256,512]{2,1,0:T(8,128)(2,1)S(1)} %copy-done.3, f32[512,128]{1,0:T(8,128)S(1)} %copy-done.1, f32[1024,128]{1,0:T(8,128)S(1)} %get-tuple-element.54.rest_1_.refs_0_, ...), custom_call_target="tpu_custom_call" | custom-call | tf_op jit(solution)/shard_map/back/pallas_call | solution.py:437
  36.9 5.8 %collective-permute-start.9 = (bf16[520,128]{1,0:T(8,128)(2,1)S(1)}, bf16[520,128]{1,0:T(8,128)(2,1)S(1)}, u32[]{:S(2)}, u32[]{:S(2)}) collective-permute-start(bf16[520,128]{1,0:T(8,128)(2,1)S(1)} %back.8.refs_8_), channel_id=1, source_target_pairs={{0,16},{4,20},{8,24},{12,28},{16,0},{20,4},{24,8},{28,12},{1,17},{... | collective-permute-start | bytes 399368 | tf_op jit(solution)/shard_map/ppermute | solution.py:528
  42.7 1.4 %back.9.refs_8_ = bf16[520,128]{1,0:T(8,128)(2,1)S(1)} custom-call(s32[1]{0:T(128)} %bitcast.me.refs_0_.me_ref, f32[10,1024,128]{2,1,0:T(8,128)S(1)} %get-tuple-element.74.filt, bf16[2,256,512]{2,1,0:T(8,128)(2,1)S(1)} %copy-done.3, f32[512,128]{1,0:T(8,128)S(1)} %copy-done.1, f32[1024,128]{1,0:T(8,128)S(1)} %get-tuple-element.54.rest_1_.refs_0_, ...), custom_call_target="tpu_custom_call" | custom-call | tf_op jit(solution)/shard_map/back/pallas_call | solution.py:437
  44.2 0.1 collective-permute-start.11
  44.2 1.5 %back.10.refs_8_ = bf16[520,128]{1,0:T(8,128)(2,1)S(1)} custom-call(s32[1]{0:T(128)} %bitcast.me.refs_0_.me_ref, f32[10,1024,128]{2,1,0:T(8,128)S(1)} %get-tuple-element.74.filt, bf16[2,256,512]{2,1,0:T(8,128)(2,1)S(1)} %copy-done.3, f32[512,128]{1,0:T(8,128)S(1)} %copy-done.1, f32[1024,128]{1,0:T(8,128)S(1)} %get-tuple-element.54.rest_1_.refs_0_, ...), custom_call_target="tpu_custom_call" | custom-call | tf_op jit(solution)/shard_map/back/pallas_call | solution.py:437
  45.7 1.5 %back.11.refs_8_ = bf16[520,128]{1,0:T(8,128)(2,1)S(1)} custom-call(s32[1]{0:T(128)} %bitcast.me.refs_0_.me_ref, f32[10,1024,128]{2,1,0:T(8,128)S(1)} %get-tuple-element.74.filt, bf16[2,256,512]{2,1,0:T(8,128)(2,1)S(1)} %copy-done.3, f32[512,128]{1,0:T(8,128)S(1)} %copy-done.1, f32[1024,128]{1,0:T(8,128)S(1)} %get-tuple-element.54.rest_1_.refs_0_, ...), custom_call_target="tpu_custom_call" | custom-call | tf_op jit(solution)/shard_map/back/pallas_call | solution.py:437
  47.2 1.4 %back.12.refs_8_ = bf16[520,128]{1,0:T(8,128)(2,1)S(1)} custom-call(s32[1]{0:T(128)} %bitcast.me.refs_0_.me_ref, f32[10,1024,128]{2,1,0:T(8,128)S(1)} %get-tuple-element.74.filt, bf16[2,256,512]{2,1,0:T(8,128)(2,1)S(1)} %copy-done.3, f32[512,128]{1,0:T(8,128)S(1)} %copy-done.1, f32[1024,128]{1,0:T(8,128)S(1)} %get-tuple-element.54.rest_1_.refs_0_, ...), custom_call_target="tpu_custom_call" | custom-call | tf_op jit(solution)/shard_map/back/pallas_call | solution.py:437
  48.6 0.0 copy-start.6
  48.6 0.0 copy-start.11
  48.6 1.5 %back.13.refs_4_.refs_8_ = bf16[520,128]{1,0:T(8,128)(2,1)S(1)} custom-call(s32[1]{0:T(128)} %bitcast.me.refs_0_.me_ref, f32[10,1024,128]{2,1,0:T(8,128)S(1)} %get-tuple-element.74.filt, bf16[2,256,512]{2,1,0:T(8,128)(2,1)S(1)} %copy-done.3, f32[512,128]{1,0:T(8,128)S(1)} %copy-done.1, f32[1024,128]{1,0:T(8,128)S(1)} %get-tuple-element.54.rest_1_.refs_0_, ...), custom_call_target="tpu_custom_call" | custom-call | tf_op jit(solution)/shard_map/back/pallas_call | solution.py:437
  50.1 1.8 %collective-permute-start.8 = (bf16[520,128]{1,0:T(8,128)(2,1)S(1)}, bf16[520,128]{1,0:T(8,128)(2,1)S(1)}, u32[]{:S(2)}, u32[]{:S(2)}) collective-permute-start(bf16[520,128]{1,0:T(8,128)(2,1)S(1)} %back.12.refs_8_), channel_id=1, source_target_pairs={{0,12},{4,8},{8,4},{12,0},{16,28},{20,24},{24,20},{28,16},{1,13},{... | collective-permute-start | bytes 399368 | tf_op jit(solution)/shard_map/ppermute | solution.py:528
  51.9 1.2 %collective-permute-start.14 = (bf16[520,128]{1,0:T(8,128)(2,1)S(1)}, bf16[520,128]{1,0:T(8,128)(2,1)S(1)}, u32[]{:S(2)}, u32[]{:S(2)}) collective-permute-start(bf16[520,128]{1,0:T(8,128)(2,1)S(1)} %back.11.refs_8_), channel_id=1, source_target_pairs={{0,28},{4,24},{8,20},{12,16},{16,12},{20,8},{24,4},{28,0},{1,29},{... | collective-permute-start | bytes 399368 | tf_op jit(solution)/shard_map/ppermute | solution.py:528
  53.1 1.8 %collective-permute-start.13 = (bf16[520,128]{1,0:T(8,128)(2,1)S(1)}, bf16[520,128]{1,0:T(8,128)(2,1)S(1)}, u32[]{:S(2)}, u32[]{:S(2)}) collective-permute-start(bf16[520,128]{1,0:T(8,128)(2,1)S(1)} %back.10.refs_8_), channel_id=1, source_target_pairs={{0,24},{4,28},{8,16},{12,20},{16,8},{20,12},{24,0},{28,4},{1,25},{... | collective-permute-start | bytes 399368 | tf_op jit(solution)/shard_map/ppermute | solution.py:528
  54.9 0.0 collective-permute-done.9.refs_5_
  54.9 0.3 final.3
  55.2 1.4 %back.14.refs_6_ = bf16[520,128]{1,0:T(8,128)(2,1)S(1)} custom-call(s32[1]{0:T(128)} %bitcast.me.refs_0_.me_ref, f32[10,1024,128]{2,1,0:T(8,128)S(1)} %get-tuple-element.74.filt, bf16[2,256,512]{2,1,0:T(8,128)(2,1)S(1)} %copy-done.3, f32[512,128]{1,0:T(8,128)S(1)} %copy-done.1, f32[1024,128]{1,0:T(8,128)S(1)} %get-tuple-element.54.rest_1_.refs_0_, ...), custom_call_target="tpu_custom_call" | custom-call | tf_op jit(solution)/shard_map/back/pallas_call | solution.py:437
  56.7 0.1 final.4.refs_8_
  56.8 1.5 %back.15.refs_8_ = bf16[520,128]{1,0:T(8,128)(2,1)S(1)} custom-call(s32[1]{0:T(128)} %bitcast.me.refs_0_.me_ref, f32[10,1024,128]{2,1,0:T(8,128)S(1)} %get-tuple-element.74.filt, bf16[2,256,512]{2,1,0:T(8,128)(2,1)S(1)} %copy-done.3, f32[512,128]{1,0:T(8,128)S(1)} %copy-done.1, f32[1024,128]{1,0:T(8,128)S(1)} %get-tuple-element.54.rest_1_.refs_0_, ...), custom_call_target="tpu_custom_call" | custom-call | tf_op jit(solution)/shard_map/back/pallas_call | solution.py:437
  58.3 0.7 %collective-permute-start.12 = (bf16[520,128]{1,0:T(8,128)(2,1)S(1)}, bf16[520,128]{1,0:T(8,128)(2,1)S(1)}, u32[]{:S(2)}, u32[]{:S(2)}) collective-permute-start(bf16[520,128]{1,0:T(8,128)(2,1)S(1)} %back.15.refs_8_), channel_id=1, source_target_pairs={{0,4},{4,0},{8,12},{12,8},{16,20},{20,16},{24,28},{28,24},{1,5},{5... | collective-permute-start | bytes 399368 | tf_op jit(solution)/shard_map/ppermute | solution.py:528
  59.0 0.0 collective-permute-start.10
  59.0 0.6 collective-permute-done.14.refs_5_
  59.6 3.9 %collective-permute-done.13.refs_4_ = bf16[520,128]{1,0:T(8,128)(2,1)S(1)} collective-permute-done((bf16[520,128]{1,0:T(8,128)(2,1)S(1)}, bf16[520,128]{1,0:T(8,128)(2,1)S(1)}, u32[]{:S(2)}, u32[]{:S(2)}) %collective-permute-start.13) | collective-permute-done | bytes 133152 | tf_op jit(solution)/shard_map/ppermute | solution.py:528
  63.5 0.3 final.5
  63.8 0.0 collective-permute-done.12.refs_2_
  63.8 2.1 %collective-permute-done.10.refs_1_ = bf16[520,128]{1,0:T(8,128)(2,1)S(1)} collective-permute-done((bf16[520,128]{1,0:T(8,128)(2,1)S(1)}, bf16[520,128]{1,0:T(8,128)(2,1)S(1)}, u32[]{:S(2)}, u32[]{:S(2)}) %collective-permute-start.10) | collective-permute-done | bytes 133152 | tf_op jit(solution)/shard_map/ppermute | solution.py:528
  66.0 1.1 %last.1 = bf16[512,1024]{1,0:T(8,128)(2,1)} custom-call(s32[1]{0:T(128)} %bitcast.me.refs_0_.me_ref, f32[384,1024]{1,0:T(8,128)S(1)} %get-tuple-element.43.refs_4_.refs_9_.refs_1_.gated, bf16[512,1024]{1,0:T(8,128)(2,1)S(1)} %copy-done.6, f32[1,1024]{1,0:T(1,128)S(1)} %bitcast.21, bf16[520,128]{1,0:T(8,128)(2,1)S(1)} %collective-permute-done.8.refs_0_, ...), custom_call_target="tpu_custom_call" | custom-call | tf_op jit(solution)/shard_map/last/pallas_call | solution.py:505
  (20 shorter events, 0.0 us)
Async XLA Ops:
  0.0 1.5 %copy-start = (bf16[512,1024]{1,0:T(8,128)(2,1)S(1)}, bf16[512,1024]{1,0:T(8,128)(2,1)}, u32[]{:S(2)}) copy-start(bf16[512,1024]{1,0:T(8,128)(2,1)} %refs_2_.18) | copy-start | bytes 3145732
  0.0 4.0 %copy-start.2 = (bf16[512,1024]{1,0:T(8,128)(2,1)S(1)}, bf16[512,1024]{1,0:T(8,128)(2,1)}, u32[]{:S(2)}) copy-start(bf16[512,1024]{1,0:T(8,128)(2,1)} %refs_3_.15) | copy-start | bytes 3145732
  0.0 4.0 %copy-start.5 = (bf16[2,256,256]{2,1,0:T(8,128)(2,1)S(1)}, bf16[2,256,256]{2,1,0:T(8,128)(2,1)}, u32[]{:S(2)}) copy-start(bf16[2,256,256]{2,1,0:T(8,128)(2,1)} %constant.29.clone.refs_4_.refs_7_) | copy-start | bytes 786436
  0.0 4.0 %copy-start.7 = (bf16[2,128,256]{2,1,0:T(8,128)(2,1)S(1)}, bf16[2,128,256]{2,1,0:T(8,128)(2,1)}, u32[]{:S(2)}) copy-start(bf16[2,128,256]{2,1,0:T(8,128)(2,1)} %constant.30.clone.refs_5_.refs_8_) | copy-start | bytes 393220
  0.0 4.0 %copy-start.10 = (f32[128,1024]{1,0:T(8,128)S(1)}, f32[128,1024]{1,0:T(8,128)}, u32[]{:S(2)}) copy-start(f32[128,1024]{1,0:T(8,128)} %refs_3_.8) | copy-start | bytes 1572868
  0.0 7.4 %copy-start.8 = (f32[512,64]{0,1:T(8,128)S(1)}, f32[512,64]{0,1:T(8,128)}, u32[]{:S(2)}) copy-start(f32[512,64]{0,1:T(8,128)} %param.16) | copy-start | bytes 393220
  1.6 5.9 %collective-permute-start = (bf16[128,1024]{1,0:T(8,128)(2,1)S(1)}, bf16[128,1024]{1,0:T(8,128)(2,1)S(1)}, u32[]{:S(2)}, u32[]{:S(2)}) collective-permute-start(bf16[128,1024]{1,0:T(8,128)(2,1)S(1)} %constant_dynamic-slice_fusion), channel_id=1, source_target_pairs={{0,4},{4,8},{8,12},{12,16},{16,20},{20,24},{24,28},{1,5},{5,9},{9,... | collective-permute-start | bytes 786440 | tf_op jit(solution)/shard_map/ppermute | solution.py:24
  8.0 15.5 %collective-permute-start.2 = (bf16[552,128]{1,0:T(8,128)(2,1)S(1)}, bf16[552,128]{1,0:T(8,128)(2,1)S(1)}, u32[]{:S(2)}, u32[]{:S(2)}) collective-permute-start(bf16[552,128]{1,0:T(8,128)(2,1)S(1)} %get-tuple-element.47), channel_id=1, source_target_pairs={{0,16},{4,20},{8,24},{12,28},{16,0},{20,4},{24,8},{28,12},{1,17},{... | collective-permute-start | bytes 423944 | tf_op jit(solution)/shard_map/ppermute | solution.py:528
  14.4 10.8 %collective-permute-start.1 = (bf16[552,128]{1,0:T(8,128)(2,1)S(1)}, bf16[552,128]{1,0:T(8,128)(2,1)S(1)}, u32[]{:S(2)}, u32[]{:S(2)}) collective-permute-start(bf16[552,128]{1,0:T(8,128)(2,1)S(1)} %get-tuple-element.46), channel_id=1, source_target_pairs={{0,8},{4,12},{8,0},{12,4},{16,24},{20,28},{24,16},{28,20},{1,9},{5... | collective-permute-start | bytes 423944 | tf_op jit(solution)/shard_map/ppermute | solution.py:528
  16.5 11.6 %collective-permute-start.7 = (bf16[552,128]{1,0:T(8,128)(2,1)S(1)}, bf16[552,128]{1,0:T(8,128)(2,1)S(1)}, u32[]{:S(2)}, u32[]{:S(2)}) collective-permute-start(bf16[552,128]{1,0:T(8,128)(2,1)S(1)} %get-tuple-element.63), channel_id=1, source_target_pairs={{0,20},{4,16},{8,28},{12,24},{16,4},{20,0},{24,12},{28,8},{1,21},{... | collective-permute-start | bytes 423944 | tf_op jit(solution)/shard_map/ppermute | solution.py:528
  16.6 5.5 %copy-start.1 = (f32[512,128]{1,0:T(8,128)S(1)}, f32[512,128]{1,0:T(8,128)}, u32[]{:S(2)}) copy-start(f32[512,128]{1,0:T(8,128)} %constant.33.clone.turn) | copy-start | bytes 786436
  16.6 5.5 %copy-start.3 = (bf16[2,256,512]{2,1,0:T(8,128)(2,1)S(1)}, bf16[2,256,512]{2,1,0:T(8,128)(2,1)}, u32[]{:S(2)}) copy-start(bf16[2,256,512]{2,1,0:T(8,128)(2,1)} %constant.32.clone.rest_0_.inv) | copy-start | bytes 1572868
  16.6 5.5 %copy-start.4 = (bf16[2,512,256]{2,1,0:T(8,128)(2,1)S(1)}, bf16[2,512,256]{2,1,0:T(8,128)(2,1)}, u32[]{:S(2)}) copy-start(bf16[2,512,256]{2,1,0:T(8,128)(2,1)} %constant.31.clone.fwd) | copy-start | bytes 1572868
  16.6 5.5 %copy-start.9 = (bf16[16,256]{1,0:T(8,128)(2,1)S(1)}, bf16[16,256]{1,0:T(8,128)(2,1)}, u32[]{:S(2)}) copy-start(bf16[16,256]{1,0:T(8,128)(2,1)} %constant.34.clone.widen) | copy-start | bytes 24580
  17.1 12.1 %collective-permute-start.6 = (bf16[552,128]{1,0:T(8,128)(2,1)S(1)}, bf16[552,128]{1,0:T(8,128)(2,1)S(1)}, u32[]{:S(2)}, u32[]{:S(2)}) collective-permute-start(bf16[552,128]{1,0:T(8,128)(2,1)S(1)} %get-tuple-element.62), channel_id=1, source_target_pairs={{0,12},{4,8},{8,4},{12,0},{16,28},{20,24},{24,20},{28,16},{1,13},{... | collective-permute-start | bytes 423944 | tf_op jit(solution)/shard_map/ppermute | solution.py:528
  18.1 12.4 %collective-permute-start.5 = (bf16[552,128]{1,0:T(8,128)(2,1)S(1)}, bf16[552,128]{1,0:T(8,128)(2,1)S(1)}, u32[]{:S(2)}, u32[]{:S(2)}) collective-permute-start(bf16[552,128]{1,0:T(8,128)(2,1)S(1)} %get-tuple-element.61), channel_id=1, source_target_pairs={{0,24},{4,28},{8,16},{12,20},{16,8},{20,12},{24,0},{28,4},{1,25},{... | collective-permute-start | bytes 423944 | tf_op jit(solution)/shard_map/ppermute | solution.py:528
  25.0 6.6 %collective-permute-start.4 = (bf16[552,128]{1,0:T(8,128)(2,1)S(1)}, bf16[552,128]{1,0:T(8,128)(2,1)S(1)}, u32[]{:S(2)}, u32[]{:S(2)}) collective-permute-start(bf16[552,128]{1,0:T(8,128)(2,1)S(1)} %get-tuple-element.60), channel_id=1, source_target_pairs={{0,4},{4,0},{8,12},{12,8},{16,20},{20,16},{24,28},{28,24},{1,5},{5... | collective-permute-start | bytes 423944 | tf_op jit(solution)/shard_map/ppermute | solution.py:528
  26.8 7.4 %collective-permute-start.3 = (bf16[552,128]{1,0:T(8,128)(2,1)S(1)}, bf16[552,128]{1,0:T(8,128)(2,1)S(1)}, u32[]{:S(2)}, u32[]{:S(2)}) collective-permute-start(bf16[552,128]{1,0:T(8,128)(2,1)S(1)} %get-tuple-element.59), channel_id=1, source_target_pairs={{0,28},{4,24},{8,20},{12,16},{16,12},{20,8},{24,4},{28,0},{1,29},{... | collective-permute-start | bytes 423944 | tf_op jit(solution)/shard_map/ppermute | solution.py:528
  36.9 18.0 %collective-permute-start.9 = (bf16[520,128]{1,0:T(8,128)(2,1)S(1)}, bf16[520,128]{1,0:T(8,128)(2,1)S(1)}, u32[]{:S(2)}, u32[]{:S(2)}) collective-permute-start(bf16[520,128]{1,0:T(8,128)(2,1)S(1)} %back.8.refs_8_), channel_id=1, source_target_pairs={{0,16},{4,20},{8,24},{12,28},{16,0},{20,4},{24,8},{28,12},{1,17},{... | collective-permute-start | bytes 399368 | tf_op jit(solution)/shard_map/ppermute | solution.py:528
  44.2 12.5 %collective-permute-start.11 = (bf16[520,128]{1,0:T(8,128)(2,1)S(1)}, bf16[520,128]{1,0:T(8,128)(2,1)S(1)}, u32[]{:S(2)}, u32[]{:S(2)}) collective-permute-start(bf16[520,128]{1,0:T(8,128)(2,1)S(1)} %back.9.refs_8_), channel_id=1, source_target_pairs={{0,20},{4,16},{8,28},{12,24},{16,4},{20,0},{24,12},{28,8},{1,21},{... | collective-permute-start | bytes 399368 | tf_op jit(solution)/shard_map/ppermute | solution.py:528
  48.6 6.3 %copy-start.6 = (bf16[512,1024]{1,0:T(8,128)(2,1)S(1)}, bf16[512,1024]{1,0:T(8,128)(2,1)}, u32[]{:S(2)}) copy-start(bf16[512,1024]{1,0:T(8,128)(2,1)} %gate.1) | copy-start | bytes 3145732
  48.6 6.3 %copy-start.11 = (f32[1024]{0:T(1024)S(1)}, f32[1024]{0:T(1024)}, u32[]{:S(2)}) copy-start(f32[1024]{0:T(1024)} %param.17) | copy-start | bytes 12292
  50.1 13.7 %collective-permute-start.8 = (bf16[520,128]{1,0:T(8,128)(2,1)S(1)}, bf16[520,128]{1,0:T(8,128)(2,1)S(1)}, u32[]{:S(2)}, u32[]{:S(2)}) collective-permute-start(bf16[520,128]{1,0:T(8,128)(2,1)S(1)} %back.12.refs_8_), channel_id=1, source_target_pairs={{0,12},{4,8},{8,4},{12,0},{16,28},{20,24},{24,20},{28,16},{1,13},{... | collective-permute-start | bytes 399368 | tf_op jit(solution)/shard_map/ppermute | solution.py:528
  51.9 7.7 %collective-permute-start.14 = (bf16[520,128]{1,0:T(8,128)(2,1)S(1)}, bf16[520,128]{1,0:T(8,128)(2,1)S(1)}, u32[]{:S(2)}, u32[]{:S(2)}) collective-permute-start(bf16[520,128]{1,0:T(8,128)(2,1)S(1)} %back.11.refs_8_), channel_id=1, source_target_pairs={{0,28},{4,24},{8,20},{12,16},{16,12},{20,8},{24,4},{28,0},{1,29},{... | collective-permute-start | bytes 399368 | tf_op jit(solution)/shard_map/ppermute | solution.py:528
  53.1 10.4 %collective-permute-start.13 = (bf16[520,128]{1,0:T(8,128)(2,1)S(1)}, bf16[520,128]{1,0:T(8,128)(2,1)S(1)}, u32[]{:S(2)}, u32[]{:S(2)}) collective-permute-start(bf16[520,128]{1,0:T(8,128)(2,1)S(1)} %back.10.refs_8_), channel_id=1, source_target_pairs={{0,24},{4,28},{8,16},{12,20},{16,8},{20,12},{24,0},{28,4},{1,25},{... | collective-permute-start | bytes 399368 | tf_op jit(solution)/shard_map/ppermute | solution.py:528
  58.3 5.5 %collective-permute-start.12 = (bf16[520,128]{1,0:T(8,128)(2,1)S(1)}, bf16[520,128]{1,0:T(8,128)(2,1)S(1)}, u32[]{:S(2)}, u32[]{:S(2)}) collective-permute-start(bf16[520,128]{1,0:T(8,128)(2,1)S(1)} %back.15.refs_8_), channel_id=1, source_target_pairs={{0,4},{4,0},{8,12},{12,8},{16,20},{20,16},{24,28},{28,24},{1,5},{5... | collective-permute-start | bytes 399368 | tf_op jit(solution)/shard_map/ppermute | solution.py:528
  59.0 7.0 %collective-permute-start.10 = (bf16[520,128]{1,0:T(8,128)(2,1)S(1)}, bf16[520,128]{1,0:T(8,128)(2,1)S(1)}, u32[]{:S(2)}, u32[]{:S(2)}) collective-permute-start(bf16[520,128]{1,0:T(8,128)(2,1)S(1)} %back.14.refs_6_), channel_id=1, source_target_pairs={{0,8},{4,12},{8,0},{12,4},{16,24},{20,28},{24,16},{28,20},{1,9},{5... | collective-permute-start | bytes 399368 | tf_op jit(solution)/shard_map/ppermute | solution.py:528

commit v5 on v4

--- a/solution.py
+++ b/solution.py
@@ -141,9 +141,9 @@
     return np.repeat(both[:, None], lanes, 1)
 
 
-def widening(groups, lanes):
+def widening(groups, lanes, pieces):
     one = np.kron(np.eye(groups), np.ones((1, lanes // groups)))
-    return np.kron(np.eye(2), one).astype(jnp.bfloat16)
+    return np.kron(np.eye(pieces), one).astype(jnp.bfloat16)
 
 
 def dot(a, b):
@@ -323,12 +323,15 @@
     many = taps.shape[0] // groups
     h_high, h_low = split(from_code(taps, jnp.concatenate([scale] * many, 0)))
     h_high, h_low = h_high.astype(jnp.float32), h_low.astype(jnp.float32)
+    pieces = []
     for c in range(many):
         at = slice(c * groups, (c + 1) * groups)
-        pair = jnp.concatenate([h_high[at], h_low[at]], 0).T.astype(jnp.bfloat16)
-        wide = dot(pair, widen[...])
+        pieces += [h_high[at], h_low[at]]
+    wide = dot(jnp.concatenate(pieces, 0).T.astype(jnp.bfloat16), widen[...])
+    for c in range(many):
         for k in range(2):
-            held_h[k, c * LANES : (c + 1) * LANES] = wide[:, k * LANES : (k + 1) * LANES]
+            at = (2 * c + k) * LANES
+            held_h[k, c * LANES : (c + 1) * LANES] = wide[:, at : at + LANES]
     highs, lows = [], []
     for odd in range(2):
         step = pl.ds(odd, half, stride=2)
@@ -420,7 +423,7 @@
             total[im, LANES:] = d_im * w_re - d_re * w_im
             return 0
 
-        lax.fori_loop(0, half // 8, chunk, 0, unroll=4)
+        lax.fori_loop(0, half // 8, chunk, 0, unroll=8)
         values = dot3(inv, total[...])
         held[pl.ds(0, half, stride=2)] = values[:, :LANES]
         held[pl.ds(1, half, stride=2)] = values[:, LANES:]
@@ -542,7 +545,7 @@
     forward, inverse = tables(half)
     fwd, inv = table(forward[:, :half]), table(inverse[:half] / 2)
     turn = jnp.asarray(turning(rows, LANES))
-    widen = jnp.asarray(widening(groups, LANES))
+    widen = jnp.asarray(widening(groups, LANES, 2 * rows // LANES))
 
     came, tops, specs, answers = {}, {}, {}, {}
     after, filt, mixed = [], [], {}

time: 67.4 us -> 67.4 us (level)
  no operation moved by 1% of the time
where the time goes in v5:
time: 67.4 us; the launch traced here: 67.3 us
  Pallas kernels  30.5 us (45%)
  starting transfers between devices  27 us (40%)
  waiting for transfers between devices  8.11 us (12%)
  between operations  1.49 us (2%)
    ppermute x14, starting transfers between devices, exchanged(): lax.ppermute(block, 'ctx', [(i, i ^ d) for i in range(count)])  24.6 us
    pallas_call x8, Pallas kernels, back_call(): pl.pallas_call(functools.partial(back_body, part, count), in_specs=[IN_SM...  11.9 us
    pallas_call x8, Pallas kernels, forward_call(): pl.pallas_call(functools.partial(forward_body, d, not so_far), in_specs=[...  9.16 us
    ppermute x14, waiting for transfers between devices, exchanged(): lax.ppermute(block, 'ctx', [(i, i ^ d) for i in range(count)])  8.11 us
    pallas_call x7, Pallas kernels, head_call(): pl.pallas_call(drop_after(functools.partial(head_body, part), 9, len(afte...  3.74 us
    pallas_call x1, Pallas kernels, main_call(): pl.pallas_call(drop_after(main_body, 6, len(after)), in_specs=[IN_SMEM] +...  3.39 us
    ppermute x1, starting transfers between devices, passed_along(): return lax.ppermute(block, axis, route)  2.4 us
  transfers between devices with their start and end apart: 15, of which 5 were waited for; matrix products, arithmetic and copies ran while one was open for 0% of the time, Pallas kernels for 38%

profile of v5, /device:TPU:0, one launch (start us, length us, event | category | flops | bytes accessed | tf_op | source)
XLA Modules:
  0.0 67.3 jit_solution(10428538230184294131)
XLA Ops:
  0.0 0.5 pace.1.refs_0_
  1.5 0.1 constant_dynamic-slice_fusion
  1.6 2.4 %collective-permute-start = (bf16[128,1024]{1,0:T(8,128)(2,1)S(1)}, bf16[128,1024]{1,0:T(8,128)(2,1)S(1)}, u32[]{:S(2)}, u32[]{:S(2)}) collective-permute-start(bf16[128,1024]{1,0:T(8,128)(2,1)S(1)} %constant_dynamic-slice_fusion), channel_id=1, source_target_pairs={{0,4},{4,8},{8,12},{12,16},{16,20},{20,24},{24,28},{1,5},{5,9},{9,... | collective-permute-start | bytes 786440 | tf_op jit(solution)/shard_map/ppermute | solution.py:24
  4.0 3.4 %short_main.1 = (f32[384,1024]{1,0:T(8,128)S(1)}, f32[256,1024]{1,0:T(8,128)S(1)}) custom-call(s32[1]{0:T(128)} %pace.1.refs_0_, bf16[512,1024]{1,0:T(8,128)(2,1)S(1)} %copy-done, bf16[512,1024]{1,0:T(8,128)(2,1)S(1)} %copy-done.2, f32[128,1024]{1,0:T(8,128)S(1)} %copy-done.10, bf16[2,256,256]{2,1,0:T(8,128)(2,1)S(1)} %copy-done.5, ...), custom_call_target="tpu_custom_call" | custom-call | tf_op jit(solution)/shard_map/short_main/pallas_call | solution.py:237
  7.4 0.0 collective-permute-done.refs_1_
  7.4 0.5 short_head.7
  7.9 5.9 %collective-permute-start.2 = (bf16[552,128]{1,0:T(8,128)(2,1)S(1)}, bf16[552,128]{1,0:T(8,128)(2,1)S(1)}, u32[]{:S(2)}, u32[]{:S(2)}) collective-permute-start(bf16[552,128]{1,0:T(8,128)(2,1)S(1)} %get-tuple-element.47), channel_id=1, source_target_pairs={{0,16},{4,20},{8,24},{12,28},{16,0},{20,4},{24,8},{28,12},{1,17},{... | collective-permute-start | bytes 423944 | tf_op jit(solution)/shard_map/ppermute | solution.py:531
  13.9 0.5 short_head.8
  14.4 1.6 %collective-permute-start.1 = (bf16[552,128]{1,0:T(8,128)(2,1)S(1)}, bf16[552,128]{1,0:T(8,128)(2,1)S(1)}, u32[]{:S(2)}, u32[]{:S(2)}) collective-permute-start(bf16[552,128]{1,0:T(8,128)(2,1)S(1)} %get-tuple-element.46), channel_id=1, source_target_pairs={{0,8},{4,12},{8,0},{12,4},{16,24},{20,28},{24,16},{28,20},{1,9},{5... | collective-permute-start | bytes 423944 | tf_op jit(solution)/shard_map/ppermute | solution.py:531
  16.0 0.5 short_head.9
  16.5 0.1 collective-permute-start.7
  16.6 0.0 copy-start.1
  16.6 0.0 copy-start.3
  16.6 0.0 copy-start.4
  16.6 0.0 copy-start.8
  16.6 0.5 short_head.10
  17.1 0.2 collective-permute-start.6
  17.3 0.8 %short_head.11 = (f32[128,128]{1,0:T(8,128)S(1)}, f32[128,128]{1,0:T(8,128)S(1)}, bf16[552,128]{1,0:T(8,128)(2,1)S(1)}, bf16[552,128]{1,0:T(8,128)(2,1)S(1)}) custom-call(s32[1]{0:T(128)} %bitcast.me.refs_0_.me_ref, bf16[128,1024]{1,0:T(8,128)(2,1)S(1)} %collective-permute-done.refs_1_, bf16[512,1024]{1,0:T(8,128)(2,1)S(1)} %copy-done, ...), custom_call_target="tpu_custom_call" | custom-call | tf_op jit(solution)/shard_map/short_head/pallas_call | solution.py:301
  18.1 4.0 %collective-permute-start.5 = (bf16[552,128]{1,0:T(8,128)(2,1)S(1)}, bf16[552,128]{1,0:T(8,128)(2,1)S(1)}, u32[]{:S(2)}, u32[]{:S(2)}) collective-permute-start(bf16[552,128]{1,0:T(8,128)(2,1)S(1)} %get-tuple-element.61), channel_id=1, source_target_pairs={{0,24},{4,28},{8,16},{12,20},{16,8},{20,12},{24,0},{28,4},{1,25},{... | collective-permute-start | bytes 423944 | tf_op jit(solution)/shard_map/ppermute | solution.py:531
  22.1 1.3 %forward.8 = (f32[1024,128]{1,0:T(8,128)S(1)}, f32[10,1024,128]{2,1,0:T(8,128)S(1)}) custom-call(s32[1]{0:T(128)} %bitcast.me.refs_0_.me_ref, bf16[552,128]{1,0:T(8,128)(2,1)S(1)} %get-tuple-element.51.code, bf16[2,512,256]{2,1,0:T(8,128)(2,1)S(1)} %copy-done.4, f32[512,128]{1,0:T(8,128)S(1)} %copy-done.1, bf16[64,1024]{1,0:T(8,128)(2,1)S(1)} %copy-done.8, ...), custom_call_target="tpu_custom_call" | custom-call | tf_op jit(solution)/shard_map/forward/pallas_call | solution.py:370
  23.4 0.0 collective-permute-done.2.code
  23.4 1.1 %forward.9 = (f32[1024,128]{1,0:T(8,128)S(1)}, f32[10,1024,128]{2,1,0:T(8,128)S(1)}) custom-call(s32[1]{0:T(128)} %bitcast.me.refs_0_.me_ref, bf16[552,128]{1,0:T(8,128)(2,1)S(1)} %collective-permute-done.2.code, bf16[2,512,256]{2,1,0:T(8,128)(2,1)S(1)} %copy-done.4, f32[512,128]{1,0:T(8,128)S(1)} %copy-done.1, ...), custom_call_target="tpu_custom_call", output_to_operand_aliasing={{1}: (5, {})} | custom-call | tf_op jit(solution)/shard_map/forward/pallas_call | solution.py:370
  24.6 0.5 short_head.12
  25.1 0.1 collective-permute-start.4
  25.2 0.0 collective-permute-done.1.code
  25.2 1.1 %forward.10 = (f32[1024,128]{1,0:T(8,128)S(1)}, f32[10,1024,128]{2,1,0:T(8,128)S(1)}) custom-call(s32[1]{0:T(128)} %bitcast.me.refs_0_.me_ref, bf16[552,128]{1,0:T(8,128)(2,1)S(1)} %collective-permute-done.1.code, bf16[2,512,256]{2,1,0:T(8,128)(2,1)S(1)} %copy-done.4, f32[512,128]{1,0:T(8,128)S(1)} %copy-done.1, ...), custom_call_target="tpu_custom_call", output_to_operand_aliasing={{1}: (5, {})} | custom-call | tf_op jit(solution)/shard_map/forward/pallas_call | solution.py:370
  26.3 0.5 short_head.13
  26.8 1.4 %collective-permute-start.3 = (bf16[552,128]{1,0:T(8,128)(2,1)S(1)}, bf16[552,128]{1,0:T(8,128)(2,1)S(1)}, u32[]{:S(2)}, u32[]{:S(2)}) collective-permute-start(bf16[552,128]{1,0:T(8,128)(2,1)S(1)} %get-tuple-element.59), channel_id=1, source_target_pairs={{0,28},{4,24},{8,20},{12,16},{16,12},{20,8},{24,4},{28,0},{1,29},{... | collective-permute-start | bytes 423944 | tf_op jit(solution)/shard_map/ppermute | solution.py:531
  28.2 0.0 collective-permute-done.7.code
  28.2 1.1 %forward.11 = (f32[1024,128]{1,0:T(8,128)S(1)}, f32[10,1024,128]{2,1,0:T(8,128)S(1)}) custom-call(s32[1]{0:T(128)} %bitcast.me.refs_0_.me_ref, bf16[552,128]{1,0:T(8,128)(2,1)S(1)} %collective-permute-done.7.code, bf16[2,512,256]{2,1,0:T(8,128)(2,1)S(1)} %copy-done.4, f32[512,128]{1,0:T(8,128)S(1)} %copy-done.1, ...), custom_call_target="tpu_custom_call", output_to_operand_aliasing={{1}: (5, {})} | custom-call | tf_op jit(solution)/shard_map/forward/pallas_call | solution.py:370
  29.3 0.0 collective-permute-done.6.code
  29.3 1.1 %forward.12 = (f32[1024,128]{1,0:T(8,128)S(1)}, f32[10,1024,128]{2,1,0:T(8,128)S(1)}) custom-call(s32[1]{0:T(128)} %bitcast.me.refs_0_.me_ref, bf16[552,128]{1,0:T(8,128)(2,1)S(1)} %collective-permute-done.6.code, bf16[2,512,256]{2,1,0:T(8,128)(2,1)S(1)} %copy-done.4, f32[512,128]{1,0:T(8,128)S(1)} %copy-done.1, ...), custom_call_target="tpu_custom_call", output_to_operand_aliasing={{1}: (5, {})} | custom-call | tf_op jit(solution)/shard_map/forward/pallas_call | solution.py:370
  30.4 0.1 collective-permute-done.5.code
  30.5 1.1 %forward.13 = (f32[1024,128]{1,0:T(8,128)S(1)}, f32[10,1024,128]{2,1,0:T(8,128)S(1)}) custom-call(s32[1]{0:T(128)} %bitcast.me.refs_0_.me_ref, bf16[552,128]{1,0:T(8,128)(2,1)S(1)} %collective-permute-done.5.code, bf16[2,512,256]{2,1,0:T(8,128)(2,1)S(1)} %copy-done.4, f32[512,128]{1,0:T(8,128)S(1)} %copy-done.1, ...), custom_call_target="tpu_custom_call", output_to_operand_aliasing={{1}: (5, {})} | custom-call | tf_op jit(solution)/shard_map/forward/pallas_call | solution.py:370
  31.6 0.0 collective-permute-done.4.code
  31.6 1.1 %forward.14 = (f32[1024,128]{1,0:T(8,128)S(1)}, f32[10,1024,128]{2,1,0:T(8,128)S(1)}) custom-call(s32[1]{0:T(128)} %bitcast.me.refs_0_.me_ref, bf16[552,128]{1,0:T(8,128)(2,1)S(1)} %collective-permute-done.4.code, bf16[2,512,256]{2,1,0:T(8,128)(2,1)S(1)} %copy-done.4, f32[512,128]{1,0:T(8,128)S(1)} %copy-done.1, ...), custom_call_target="tpu_custom_call", output_to_operand_aliasing={{1}: (5, {})} | custom-call | tf_op jit(solution)/shard_map/forward/pallas_call | solution.py:370
  32.8 1.4 %collective-permute-done.3.code = bf16[552,128]{1,0:T(8,128)(2,1)S(1)} collective-permute-done((bf16[552,128]{1,0:T(8,128)(2,1)S(1)}, bf16[552,128]{1,0:T(8,128)(2,1)S(1)}, u32[]{:S(2)}, u32[]{:S(2)}) %collective-permute-start.3) | collective-permute-done | bytes 141344 | tf_op jit(solution)/shard_map/ppermute | solution.py:531
  34.2 1.1 %forward.15 = (f32[1024,128]{1,0:T(8,128)S(1)}, f32[10,1024,128]{2,1,0:T(8,128)S(1)}) custom-call(s32[1]{0:T(128)} %bitcast.me.refs_0_.me_ref, bf16[552,128]{1,0:T(8,128)(2,1)S(1)} %collective-permute-done.3.code, bf16[2,512,256]{2,1,0:T(8,128)(2,1)S(1)} %copy-done.4, f32[512,128]{1,0:T(8,128)S(1)} %copy-done.1, ...), custom_call_target="tpu_custom_call", output_to_operand_aliasing={{1}: (5, {})} | custom-call | tf_op jit(solution)/shard_map/forward/pallas_call | solution.py:370
  35.3 1.7 %back.8.refs_8_ = bf16[520,128]{1,0:T(8,128)(2,1)S(1)} custom-call(s32[1]{0:T(128)} %bitcast.me.refs_0_.me_ref, f32[10,1024,128]{2,1,0:T(8,128)S(1)} %get-tuple-element.74.filt, bf16[2,256,512]{2,1,0:T(8,128)(2,1)S(1)} %copy-done.3, f32[512,128]{1,0:T(8,128)S(1)} %copy-done.1, f32[1024,128]{1,0:T(8,128)S(1)} %get-tuple-element.54.rest_1_.refs_0_, ...), custom_call_target="tpu_custom_call" | custom-call | tf_op jit(solution)/shard_map/back/pallas_call | solution.py:440
  37.0 5.8 %collective-permute-start.9 = (bf16[520,128]{1,0:T(8,128)(2,1)S(1)}, bf16[520,128]{1,0:T(8,128)(2,1)S(1)}, u32[]{:S(2)}, u32[]{:S(2)}) collective-permute-start(bf16[520,128]{1,0:T(8,128)(2,1)S(1)} %back.8.refs_8_), channel_id=1, source_target_pairs={{0,16},{4,20},{8,24},{12,28},{16,0},{20,4},{24,8},{28,12},{1,17},{... | collective-permute-start | bytes 399368 | tf_op jit(solution)/shard_map/ppermute | solution.py:531
  42.8 1.5 %back.9.refs_8_ = bf16[520,128]{1,0:T(8,128)(2,1)S(1)} custom-call(s32[1]{0:T(128)} %bitcast.me.refs_0_.me_ref, f32[10,1024,128]{2,1,0:T(8,128)S(1)} %get-tuple-element.74.filt, bf16[2,256,512]{2,1,0:T(8,128)(2,1)S(1)} %copy-done.3, f32[512,128]{1,0:T(8,128)S(1)} %copy-done.1, f32[1024,128]{1,0:T(8,128)S(1)} %get-tuple-element.54.rest_1_.refs_0_, ...), custom_call_target="tpu_custom_call" | custom-call | tf_op jit(solution)/shard_map/back/pallas_call | solution.py:440
  44.2 0.1 collective-permute-start.11
  44.3 1.5 %back.10.refs_8_ = bf16[520,128]{1,0:T(8,128)(2,1)S(1)} custom-call(s32[1]{0:T(128)} %bitcast.me.refs_0_.me_ref, f32[10,1024,128]{2,1,0:T(8,128)S(1)} %get-tuple-element.74.filt, bf16[2,256,512]{2,1,0:T(8,128)(2,1)S(1)} %copy-done.3, f32[512,128]{1,0:T(8,128)S(1)} %copy-done.1, f32[1024,128]{1,0:T(8,128)S(1)} %get-tuple-element.54.rest_1_.refs_0_, ...), custom_call_target="tpu_custom_call" | custom-call | tf_op jit(solution)/shard_map/back/pallas_call | solution.py:440
  45.8 1.5 %back.11.refs_8_ = bf16[520,128]{1,0:T(8,128)(2,1)S(1)} custom-call(s32[1]{0:T(128)} %bitcast.me.refs_0_.me_ref, f32[10,1024,128]{2,1,0:T(8,128)S(1)} %get-tuple-element.74.filt, bf16[2,256,512]{2,1,0:T(8,128)(2,1)S(1)} %copy-done.3, f32[512,128]{1,0:T(8,128)S(1)} %copy-done.1, f32[1024,128]{1,0:T(8,128)S(1)} %get-tuple-element.54.rest_1_.refs_0_, ...), custom_call_target="tpu_custom_call" | custom-call | tf_op jit(solution)/shard_map/back/pallas_call | solution.py:440
  47.3 1.5 %back.12.refs_8_ = bf16[520,128]{1,0:T(8,128)(2,1)S(1)} custom-call(s32[1]{0:T(128)} %bitcast.me.refs_0_.me_ref, f32[10,1024,128]{2,1,0:T(8,128)S(1)} %get-tuple-element.74.filt, bf16[2,256,512]{2,1,0:T(8,128)(2,1)S(1)} %copy-done.3, f32[512,128]{1,0:T(8,128)S(1)} %copy-done.1, f32[1024,128]{1,0:T(8,128)S(1)} %get-tuple-element.54.rest_1_.refs_0_, ...), custom_call_target="tpu_custom_call" | custom-call | tf_op jit(solution)/shard_map/back/pallas_call | solution.py:440
  48.8 0.0 copy-start.6
  48.8 0.0 copy-start.11
  48.8 1.5 %back.13.refs_4_.refs_8_ = bf16[520,128]{1,0:T(8,128)(2,1)S(1)} custom-call(s32[1]{0:T(128)} %bitcast.me.refs_0_.me_ref, f32[10,1024,128]{2,1,0:T(8,128)S(1)} %get-tuple-element.74.filt, bf16[2,256,512]{2,1,0:T(8,128)(2,1)S(1)} %copy-done.3, f32[512,128]{1,0:T(8,128)S(1)} %copy-done.1, f32[1024,128]{1,0:T(8,128)S(1)} %get-tuple-element.54.rest_1_.refs_0_, ...), custom_call_target="tpu_custom_call" | custom-call | tf_op jit(solution)/shard_map/back/pallas_call | solution.py:440
  50.2 1.7 %collective-permute-start.8 = (bf16[520,128]{1,0:T(8,128)(2,1)S(1)}, bf16[520,128]{1,0:T(8,128)(2,1)S(1)}, u32[]{:S(2)}, u32[]{:S(2)}) collective-permute-start(bf16[520,128]{1,0:T(8,128)(2,1)S(1)} %back.12.refs_8_), channel_id=1, source_target_pairs={{0,12},{4,8},{8,4},{12,0},{16,28},{20,24},{24,20},{28,16},{1,13},{... | collective-permute-start | bytes 399368 | tf_op jit(solution)/shard_map/ppermute | solution.py:531
  52.0 1.3 %collective-permute-start.14 = (bf16[520,128]{1,0:T(8,128)(2,1)S(1)}, bf16[520,128]{1,0:T(8,128)(2,1)S(1)}, u32[]{:S(2)}, u32[]{:S(2)}) collective-permute-start(bf16[520,128]{1,0:T(8,128)(2,1)S(1)} %back.11.refs_8_), channel_id=1, source_target_pairs={{0,28},{4,24},{8,20},{12,16},{16,12},{20,8},{24,4},{28,0},{1,29},{... | collective-permute-start | bytes 399368 | tf_op jit(solution)/shard_map/ppermute | solution.py:531
  53.3 1.7 %collective-permute-start.13 = (bf16[520,128]{1,0:T(8,128)(2,1)S(1)}, bf16[520,128]{1,0:T(8,128)(2,1)S(1)}, u32[]{:S(2)}, u32[]{:S(2)}) collective-permute-start(bf16[520,128]{1,0:T(8,128)(2,1)S(1)} %back.10.refs_8_), channel_id=1, source_target_pairs={{0,24},{4,28},{8,16},{12,20},{16,8},{20,12},{24,0},{28,4},{1,25},{... | collective-permute-start | bytes 399368 | tf_op jit(solution)/shard_map/ppermute | solution.py:531
  55.0 0.0 collective-permute-done.9.refs_5_
  55.0 0.3 final.3
  55.3 1.5 %back.14.refs_6_ = bf16[520,128]{1,0:T(8,128)(2,1)S(1)} custom-call(s32[1]{0:T(128)} %bitcast.me.refs_0_.me_ref, f32[10,1024,128]{2,1,0:T(8,128)S(1)} %get-tuple-element.74.filt, bf16[2,256,512]{2,1,0:T(8,128)(2,1)S(1)} %copy-done.3, f32[512,128]{1,0:T(8,128)S(1)} %copy-done.1, f32[1024,128]{1,0:T(8,128)S(1)} %get-tuple-element.54.rest_1_.refs_0_, ...), custom_call_target="tpu_custom_call" | custom-call | tf_op jit(solution)/shard_map/back/pallas_call | solution.py:440
  56.8 0.1 final.4.refs_8_
  56.9 1.5 %back.15.refs_8_ = bf16[520,128]{1,0:T(8,128)(2,1)S(1)} custom-call(s32[1]{0:T(128)} %bitcast.me.refs_0_.me_ref, f32[10,1024,128]{2,1,0:T(8,128)S(1)} %get-tuple-element.74.filt, bf16[2,256,512]{2,1,0:T(8,128)(2,1)S(1)} %copy-done.3, f32[512,128]{1,0:T(8,128)S(1)} %copy-done.1, f32[1024,128]{1,0:T(8,128)S(1)} %get-tuple-element.54.rest_1_.refs_0_, ...), custom_call_target="tpu_custom_call" | custom-call | tf_op jit(solution)/shard_map/back/pallas_call | solution.py:440
  58.4 0.7 %collective-permute-start.12 = (bf16[520,128]{1,0:T(8,128)(2,1)S(1)}, bf16[520,128]{1,0:T(8,128)(2,1)S(1)}, u32[]{:S(2)}, u32[]{:S(2)}) collective-permute-start(bf16[520,128]{1,0:T(8,128)(2,1)S(1)} %back.15.refs_8_), channel_id=1, source_target_pairs={{0,4},{4,0},{8,12},{12,8},{16,20},{20,16},{24,28},{28,24},{1,5},{5... | collective-permute-start | bytes 399368 | tf_op jit(solution)/shard_map/ppermute | solution.py:531
  59.1 0.6 collective-permute-done.14.refs_5_
  59.7 4.0 %collective-permute-done.13.refs_4_ = bf16[520,128]{1,0:T(8,128)(2,1)S(1)} collective-permute-done((bf16[520,128]{1,0:T(8,128)(2,1)S(1)}, bf16[520,128]{1,0:T(8,128)(2,1)S(1)}, u32[]{:S(2)}, u32[]{:S(2)}) %collective-permute-start.13) | collective-permute-done | bytes 133152 | tf_op jit(solution)/shard_map/ppermute | solution.py:531
  63.7 0.3 final.5
  63.9 0.0 collective-permute-done.8.refs_0_
  63.9 0.0 collective-permute-done.12.refs_2_
  63.9 2.0 %collective-permute-done.10.refs_1_ = bf16[520,128]{1,0:T(8,128)(2,1)S(1)} collective-permute-done((bf16[520,128]{1,0:T(8,128)(2,1)S(1)}, bf16[520,128]{1,0:T(8,128)(2,1)S(1)}, u32[]{:S(2)}, u32[]{:S(2)}) %collective-permute-start.10) | collective-permute-done | bytes 133152 | tf_op jit(solution)/shard_map/ppermute | solution.py:531
  66.0 1.1 %last.1 = bf16[512,1024]{1,0:T(8,128)(2,1)} custom-call(s32[1]{0:T(128)} %bitcast.me.refs_0_.me_ref, f32[384,1024]{1,0:T(8,128)S(1)} %get-tuple-element.43.refs_4_.refs_9_.refs_1_.gated, bf16[512,1024]{1,0:T(8,128)(2,1)S(1)} %copy-done.6, f32[1,1024]{1,0:T(1,128)S(1)} %bitcast.21, bf16[520,128]{1,0:T(8,128)(2,1)S(1)} %collective-permute-done.8.refs_0_, ...), custom_call_target="tpu_custom_call" | custom-call | tf_op jit(solution)/shard_map/last/pallas_call | solution.py:508
  (20 shorter events, 0.0 us)
Async XLA Ops:
  0.0 1.5 %copy-start = (bf16[512,1024]{1,0:T(8,128)(2,1)S(1)}, bf16[512,1024]{1,0:T(8,128)(2,1)}, u32[]{:S(2)}) copy-start(bf16[512,1024]{1,0:T(8,128)(2,1)} %refs_2_.18) | copy-start | bytes 3145732
  0.0 4.0 %copy-start.2 = (bf16[512,1024]{1,0:T(8,128)(2,1)S(1)}, bf16[512,1024]{1,0:T(8,128)(2,1)}, u32[]{:S(2)}) copy-start(bf16[512,1024]{1,0:T(8,128)(2,1)} %refs_3_.15) | copy-start | bytes 3145732
  0.0 4.0 %copy-start.5 = (bf16[2,256,256]{2,1,0:T(8,128)(2,1)S(1)}, bf16[2,256,256]{2,1,0:T(8,128)(2,1)}, u32[]{:S(2)}) copy-start(bf16[2,256,256]{2,1,0:T(8,128)(2,1)} %constant.29.clone.refs_4_.refs_7_) | copy-start | bytes 786436
  0.0 4.0 %copy-start.7 = (bf16[2,128,256]{2,1,0:T(8,128)(2,1)S(1)}, bf16[2,128,256]{2,1,0:T(8,128)(2,1)}, u32[]{:S(2)}) copy-start(bf16[2,128,256]{2,1,0:T(8,128)(2,1)} %constant.30.clone.refs_5_.refs_8_) | copy-start | bytes 393220
  0.0 4.0 %copy-start.10 = (f32[128,1024]{1,0:T(8,128)S(1)}, f32[128,1024]{1,0:T(8,128)}, u32[]{:S(2)}) copy-start(f32[128,1024]{1,0:T(8,128)} %refs_3_.8) | copy-start | bytes 1572868
  0.0 7.4 %copy-start.9 = (f32[512,64]{0,1:T(8,128)S(1)}, f32[512,64]{0,1:T(8,128)}, u32[]{:S(2)}) copy-start(f32[512,64]{0,1:T(8,128)} %param.16) | copy-start | bytes 393220
  1.6 5.9 %collective-permute-start = (bf16[128,1024]{1,0:T(8,128)(2,1)S(1)}, bf16[128,1024]{1,0:T(8,128)(2,1)S(1)}, u32[]{:S(2)}, u32[]{:S(2)}) collective-permute-start(bf16[128,1024]{1,0:T(8,128)(2,1)S(1)} %constant_dynamic-slice_fusion), channel_id=1, source_target_pairs={{0,4},{4,8},{8,12},{12,16},{16,20},{20,24},{24,28},{1,5},{5,9},{9,... | collective-permute-start | bytes 786440 | tf_op jit(solution)/shard_map/ppermute | solution.py:24
  7.9 15.5 %collective-permute-start.2 = (bf16[552,128]{1,0:T(8,128)(2,1)S(1)}, bf16[552,128]{1,0:T(8,128)(2,1)S(1)}, u32[]{:S(2)}, u32[]{:S(2)}) collective-permute-start(bf16[552,128]{1,0:T(8,128)(2,1)S(1)} %get-tuple-element.47), channel_id=1, source_target_pairs={{0,16},{4,20},{8,24},{12,28},{16,0},{20,4},{24,8},{28,12},{1,17},{... | collective-permute-start | bytes 423944 | tf_op jit(solution)/shard_map/ppermute | solution.py:531
  14.4 10.8 %collective-permute-start.1 = (bf16[552,128]{1,0:T(8,128)(2,1)S(1)}, bf16[552,128]{1,0:T(8,128)(2,1)S(1)}, u32[]{:S(2)}, u32[]{:S(2)}) collective-permute-start(bf16[552,128]{1,0:T(8,128)(2,1)S(1)} %get-tuple-element.46), channel_id=1, source_target_pairs={{0,8},{4,12},{8,0},{12,4},{16,24},{20,28},{24,16},{28,20},{1,9},{5... | collective-permute-start | bytes 423944 | tf_op jit(solution)/shard_map/ppermute | solution.py:531
  16.5 11.7 %collective-permute-start.7 = (bf16[552,128]{1,0:T(8,128)(2,1)S(1)}, bf16[552,128]{1,0:T(8,128)(2,1)S(1)}, u32[]{:S(2)}, u32[]{:S(2)}) collective-permute-start(bf16[552,128]{1,0:T(8,128)(2,1)S(1)} %get-tuple-element.63), channel_id=1, source_target_pairs={{0,20},{4,16},{8,28},{12,24},{16,4},{20,0},{24,12},{28,8},{1,21},{... | collective-permute-start | bytes 423944 | tf_op jit(solution)/shard_map/ppermute | solution.py:531
  16.6 5.5 %copy-start.1 = (f32[512,128]{1,0:T(8,128)S(1)}, f32[512,128]{1,0:T(8,128)}, u32[]{:S(2)}) copy-start(f32[512,128]{1,0:T(8,128)} %constant.33.clone.turn) | copy-start | bytes 786436
  16.6 5.5 %copy-start.3 = (bf16[2,256,512]{2,1,0:T(8,128)(2,1)S(1)}, bf16[2,256,512]{2,1,0:T(8,128)(2,1)}, u32[]{:S(2)}) copy-start(bf16[2,256,512]{2,1,0:T(8,128)(2,1)} %constant.32.clone.rest_0_.inv) | copy-start | bytes 1572868
  16.6 5.5 %copy-start.4 = (bf16[2,512,256]{2,1,0:T(8,128)(2,1)S(1)}, bf16[2,512,256]{2,1,0:T(8,128)(2,1)}, u32[]{:S(2)}) copy-start(bf16[2,512,256]{2,1,0:T(8,128)(2,1)} %constant.31.clone.fwd) | copy-start | bytes 1572868
  16.6 5.5 %copy-start.8 = (bf16[64,1024]{1,0:T(8,128)(2,1)S(1)}, bf16[64,1024]{1,0:T(8,128)(2,1)}, u32[]{:S(2)}) copy-start(bf16[64,1024]{1,0:T(8,128)(2,1)} %constant.34.clone.widen) | copy-start | bytes 393220
  17.1 12.2 %collective-permute-start.6 = (bf16[552,128]{1,0:T(8,128)(2,1)S(1)}, bf16[552,128]{1,0:T(8,128)(2,1)S(1)}, u32[]{:S(2)}, u32[]{:S(2)}) collective-permute-start(bf16[552,128]{1,0:T(8,128)(2,1)S(1)} %get-tuple-element.62), channel_id=1, source_target_pairs={{0,12},{4,8},{8,4},{12,0},{16,28},{20,24},{24,20},{28,16},{1,13},{... | collective-permute-start | bytes 423944 | tf_op jit(solution)/shard_map/ppermute | solution.py:531
  18.1 12.4 %collective-permute-start.5 = (bf16[552,128]{1,0:T(8,128)(2,1)S(1)}, bf16[552,128]{1,0:T(8,128)(2,1)S(1)}, u32[]{:S(2)}, u32[]{:S(2)}) collective-permute-start(bf16[552,128]{1,0:T(8,128)(2,1)S(1)} %get-tuple-element.61), channel_id=1, source_target_pairs={{0,24},{4,28},{8,16},{12,20},{16,8},{20,12},{24,0},{28,4},{1,25},{... | collective-permute-start | bytes 423944 | tf_op jit(solution)/shard_map/ppermute | solution.py:531
  25.1 6.6 %collective-permute-start.4 = (bf16[552,128]{1,0:T(8,128)(2,1)S(1)}, bf16[552,128]{1,0:T(8,128)(2,1)S(1)}, u32[]{:S(2)}, u32[]{:S(2)}) collective-permute-start(bf16[552,128]{1,0:T(8,128)(2,1)S(1)} %get-tuple-element.60), channel_id=1, source_target_pairs={{0,4},{4,0},{8,12},{12,8},{16,20},{20,16},{24,28},{28,24},{1,5},{5... | collective-permute-start | bytes 423944 | tf_op jit(solution)/shard_map/ppermute | solution.py:531
  26.8 7.4 %collective-permute-start.3 = (bf16[552,128]{1,0:T(8,128)(2,1)S(1)}, bf16[552,128]{1,0:T(8,128)(2,1)S(1)}, u32[]{:S(2)}, u32[]{:S(2)}) collective-permute-start(bf16[552,128]{1,0:T(8,128)(2,1)S(1)} %get-tuple-element.59), channel_id=1, source_target_pairs={{0,28},{4,24},{8,20},{12,16},{16,12},{20,8},{24,4},{28,0},{1,29},{... | collective-permute-start | bytes 423944 | tf_op jit(solution)/shard_map/ppermute | solution.py:531
  37.0 18.0 %collective-permute-start.9 = (bf16[520,128]{1,0:T(8,128)(2,1)S(1)}, bf16[520,128]{1,0:T(8,128)(2,1)S(1)}, u32[]{:S(2)}, u32[]{:S(2)}) collective-permute-start(bf16[520,128]{1,0:T(8,128)(2,1)S(1)} %back.8.refs_8_), channel_id=1, source_target_pairs={{0,16},{4,20},{8,24},{12,28},{16,0},{20,4},{24,8},{28,12},{1,17},{... | collective-permute-start | bytes 399368 | tf_op jit(solution)/shard_map/ppermute | solution.py:531
  44.2 12.5 %collective-permute-start.11 = (bf16[520,128]{1,0:T(8,128)(2,1)S(1)}, bf16[520,128]{1,0:T(8,128)(2,1)S(1)}, u32[]{:S(2)}, u32[]{:S(2)}) collective-permute-start(bf16[520,128]{1,0:T(8,128)(2,1)S(1)} %back.9.refs_8_), channel_id=1, source_target_pairs={{0,20},{4,16},{8,28},{12,24},{16,4},{20,0},{24,12},{28,8},{1,21},{... | collective-permute-start | bytes 399368 | tf_op jit(solution)/shard_map/ppermute | solution.py:531
  48.8 6.2 %copy-start.6 = (bf16[512,1024]{1,0:T(8,128)(2,1)S(1)}, bf16[512,1024]{1,0:T(8,128)(2,1)}, u32[]{:S(2)}) copy-start(bf16[512,1024]{1,0:T(8,128)(2,1)} %gate.1) | copy-start | bytes 3145732
  48.8 6.2 %copy-start.11 = (f32[1024]{0:T(1024)S(1)}, f32[1024]{0:T(1024)}, u32[]{:S(2)}) copy-start(f32[1024]{0:T(1024)} %param.17) | copy-start | bytes 12292
  50.2 13.7 %collective-permute-start.8 = (bf16[520,128]{1,0:T(8,128)(2,1)S(1)}, bf16[520,128]{1,0:T(8,128)(2,1)S(1)}, u32[]{:S(2)}, u32[]{:S(2)}) collective-permute-start(bf16[520,128]{1,0:T(8,128)(2,1)S(1)} %back.12.refs_8_), channel_id=1, source_target_pairs={{0,12},{4,8},{8,4},{12,0},{16,28},{20,24},{24,20},{28,16},{1,13},{... | collective-permute-start | bytes 399368 | tf_op jit(solution)/shard_map/ppermute | solution.py:531
  52.0 7.7 %collective-permute-start.14 = (bf16[520,128]{1,0:T(8,128)(2,1)S(1)}, bf16[520,128]{1,0:T(8,128)(2,1)S(1)}, u32[]{:S(2)}, u32[]{:S(2)}) collective-permute-start(bf16[520,128]{1,0:T(8,128)(2,1)S(1)} %back.11.refs_8_), channel_id=1, source_target_pairs={{0,28},{4,24},{8,20},{12,16},{16,12},{20,8},{24,4},{28,0},{1,29},{... | collective-permute-start | bytes 399368 | tf_op jit(solution)/shard_map/ppermute | solution.py:531
  53.3 10.4 %collective-permute-start.13 = (bf16[520,128]{1,0:T(8,128)(2,1)S(1)}, bf16[520,128]{1,0:T(8,128)(2,1)S(1)}, u32[]{:S(2)}, u32[]{:S(2)}) collective-permute-start(bf16[520,128]{1,0:T(8,128)(2,1)S(1)} %back.10.refs_8_), channel_id=1, source_target_pairs={{0,24},{4,28},{8,16},{12,20},{16,8},{20,12},{24,0},{28,4},{1,25},{... | collective-permute-start | bytes 399368 | tf_op jit(solution)/shard_map/ppermute | solution.py:531
  58.4 5.6 %collective-permute-start.12 = (bf16[520,128]{1,0:T(8,128)(2,1)S(1)}, bf16[520,128]{1,0:T(8,128)(2,1)S(1)}, u32[]{:S(2)}, u32[]{:S(2)}) collective-permute-start(bf16[520,128]{1,0:T(8,128)(2,1)S(1)} %back.15.refs_8_), channel_id=1, source_target_pairs={{0,4},{4,0},{8,12},{12,8},{16,20},{20,16},{24,28},{28,24},{1,5},{5... | collective-permute-start | bytes 399368 | tf_op jit(solution)/shard_map/ppermute | solution.py:531
  59.1 6.9 %collective-permute-start.10 = (bf16[520,128]{1,0:T(8,128)(2,1)S(1)}, bf16[520,128]{1,0:T(8,128)(2,1)S(1)}, u32[]{:S(2)}, u32[]{:S(2)}) collective-permute-start(bf16[520,128]{1,0:T(8,128)(2,1)S(1)} %back.14.refs_6_), channel_id=1, source_target_pairs={{0,8},{4,12},{8,0},{12,4},{16,24},{20,28},{24,16},{28,20},{1,9},{5... | collective-permute-start | bytes 399368 | tf_op jit(solution)/shard_map/ppermute | solution.py:531
